TPU v7x, 256 devices: a whole 4x4x8 slice. The times are simulated.
256 devices in a mesh: wide: 32 (over y, z), narrow: 8 (over x, core).
Axes of the slice: x: 4, y: 4, z: 8, core: 2. Of those that a mesh axis runs over, the one named last changes fastest.
Arguments:
- cross_input: bfloat16 [32768, 3456], P(('wide', 'narrow')), may hold values from -6 to 6
- upstream: bfloat16 [32768, 3456], P(('wide', 'narrow')), may hold values from -6 to 6
- cross_down: bfloat16 [512, 3456], replicated, may hold values from -0.109375 to 0.109375
- cross_up: bfloat16 [512, 3456], replicated, may hold values from -0.25 to 0.25
- cross_bias: bfloat16 [3456], replicated, may hold values from -3 to 3
- bag_rows: int32 [32768, 26, 16], P(('wide', 'narrow')), may hold values from 0 to 511
- bag_lengths: int32 [32768, 26], P(('wide', 'narrow')), may hold values from 0 to 16
- table_owner: int32 [26], replicated, may hold values from 0 to 31, as said below
- table_rows: float32 [16384, 128], P('wide'), may hold values from -4 to 4
- row_accum: float32 [16384], P('wide'), may hold values from 20 to 600
- admitted: int32 [16384], P('wide'), may hold values 0 or 1
Outputs:
- new_rows: float32 [16384, 128], P('wide')
- new_accum: float32 [16384], P('wide')
- grad_up: float32 [512, 3456], P(('wide', 'narrow'))
- grad_down: float32 [512, 3456], P(('wide', 'narrow'))
Inputs may be any that keep to these rules, and one draw needn't show every extreme that they name: `table_owner`: each wide index owns at most 2 tables, and some wide index owns exactly 2. `bag_rows`: ids at positions at or past a bag's length are arbitrary and unused.
All inputs are finite; a program needn't handle non-finite values. No bound on the sum of `admitted` on one device may be relied on, other than what follows from the above.
Results may differ from a plain program's by a relative error of at most 0.0041.
Values may be sent and summed in bfloat16 or wider, within the bound.
No kernel may reach another device: no remote copies, remote signals or barrier semaphores. Data moves between devices by JAX's collectives and lax.ppermute only.
A program may use at most 128 MiB of HBM per device.

v0:
```python
import math

import jax
import jax.numpy as jnp
from jax import lax
from jax.sharding import PartitionSpec as P


def adagrad_rows(rows, accum, admitted, grad):
    begin_acc = jnp.where(admitted == 1, jnp.float32(0.1), accum)
    new_acc = begin_acc + jnp.mean(grad * grad, axis=1)
    new_values = rows - 0.5 * grad / (jnp.sqrt(new_acc)[:, None] + 1e-08)
    return (new_values, new_acc)


def local(
    cross_input,
    upstream,
    cross_down,
    cross_up,
    cross_bias,
    bag_rows,
    bag_lengths,
    table_owner,
    table_rows,
    row_accum,
    admitted,
):
    emb = table_rows.shape[1]
    samples, tables = bag_lengths.shape
    bag_len = bag_rows.shape[2]
    unique = table_rows.shape[0]
    wide_count = lax.axis_size("wide")
    narrow_count = lax.axis_size("narrow")
    low_rank = lax.dot_general(
        cross_input, cross_down, (((1,), (1,)), ((), ())), preferred_element_type=jnp.float32
    ).astype(jnp.bfloat16)
    scale_tail = jnp.dot(
        low_rank, cross_up[:, emb:], preferred_element_type=jnp.float32
    ) + cross_bias[emb:].astype(jnp.float32)
    d_scale = (upstream.astype(jnp.float32) * cross_input.astype(jnp.float32)).astype(jnp.bfloat16)
    d_low = lax.dot_general(
        d_scale, cross_up, (((1,), (1,)), ((), ())), preferred_element_type=jnp.float32
    ).astype(jnp.bfloat16)
    tail_grad = upstream[:, emb:].astype(jnp.float32) * (scale_tail + 1.0) + jnp.dot(
        d_low, cross_down[:, emb:], preferred_element_type=jnp.float32
    )
    pooled = tail_grad.astype(jnp.bfloat16).reshape(samples, tables, emb)
    tslot = (2 * tables + wide_count - 1) // wide_count
    slot_total = wide_count * tslot
    table_ids = jnp.arange(tables, dtype=jnp.int32)
    same_owner = table_owner[:, None] == table_owner[None, :]
    earlier = table_ids[None, :] < table_ids[:, None]
    rank_in = jnp.sum(jnp.where(same_owner & earlier, 1, 0), axis=1).astype(jnp.int32)
    slot_of = table_owner * tslot + rank_in
    matches = slot_of[None, :] == jnp.arange(slot_total, dtype=jnp.int32)[:, None]
    table_of_slot = jnp.sum(jnp.where(matches, table_ids[None, :], 0), axis=1)
    filled = jnp.any(matches, axis=1)
    send_grad = jnp.take(pooled, table_of_slot, axis=1)
    send_rows = jnp.take(bag_rows, table_of_slot, axis=1)
    send_lengths = jnp.where(filled[None, :], jnp.take(bag_lengths, table_of_slot, axis=1), 0)
    got_grad, got_rows, got_lengths = (
        lax.all_to_all(send_grad, "wide", split_axis=1, concat_axis=0, tiled=True),
        lax.all_to_all(send_rows, "wide", split_axis=1, concat_axis=0, tiled=True),
        lax.all_to_all(send_lengths, "wide", split_axis=1, concat_axis=0, tiled=True),
    )
    norm_scale = 1.0 / math.sqrt(samples * wide_count * narrow_count)
    up_full = (
        lax.dot_general(
            low_rank, d_scale, (((0,), (0,)), ((), ())), preferred_element_type=jnp.float32
        )
        * norm_scale
    )
    down_full = (
        lax.dot_general(
            d_low, cross_input, (((0,), (0,)), ((), ())), preferred_element_type=jnp.float32
        )
        * norm_scale
    )
    grad_up, grad_down = (
        lax.psum_scatter(up_full, ("wide", "narrow"), scatter_dimension=0, tiled=True),
        lax.psum_scatter(down_full, ("wide", "narrow"), scatter_dimension=0, tiled=True),
    )
    flat_grad = got_grad.reshape(-1, emb)
    flat_rows = got_rows.reshape(-1, bag_len)
    flat_lengths = got_lengths.reshape(-1)
    bag_total = flat_grad.shape[0]
    block_bags = math.gcd(bag_total, 1024)
    block_count = bag_total // block_bags
    row_ids = jnp.arange(unique, dtype=jnp.int32)

    def add_block(running, pieces):
        grad_block, rows_block, length_block = pieces
        counts = jnp.zeros((block_bags, unique), jnp.float32)
        for position in range(bag_len):
            hit = (rows_block[:, position][:, None] == row_ids[None, :]) & (
                position < length_block
            )[:, None]
            counts = counts + jnp.where(hit, 1.0, 0.0).astype(jnp.float32)
        counts = counts.astype(jnp.bfloat16)
        return (
            running
            + lax.dot_general(
                counts, grad_block, (((0,), (0,)), ((), ())), preferred_element_type=jnp.float32
            ),
            None,
        )

    blocks = (
        flat_grad.reshape(block_count, block_bags, emb),
        flat_rows.reshape(block_count, block_bags, bag_len),
        flat_lengths.reshape(block_count, block_bags),
    )
    local_grad, unused = lax.scan(add_block, jnp.zeros((unique, emb), jnp.float32), blocks)
    total_grad = lax.psum(local_grad, "narrow")
    new_rows, new_accum = adagrad_rows(table_rows, row_accum, admitted, total_grad)
    return (new_rows, new_accum, grad_up, grad_down)


def solution(mesh):
    return jax.shard_map(
        local,
        mesh=mesh,
        in_specs=(
            P(("wide", "narrow"), None),
            P(("wide", "narrow"), None),
            P(),
            P(),
            P(),
            P(("wide", "narrow"), None, None),
            P(("wide", "narrow"), None),
            P(),
            P("wide", None),
            P("wide"),
            P("wide"),
        ),
        out_specs=(
            P("wide", None),
            P("wide"),
            P(("wide", "narrow"), None),
            P(("wide", "narrow"), None),
        ),
        check_vma=False,
    )
```

profile of v0, /device:TPU:1, one launch (start us, length us, event | category | flops | bytes accessed | tf_op | source)
XLA Modules:
  0.0 575.9 jit_solution(15703449645657906530)
XLA Ops:
  7.2 0.9 select_reduce_fusion.1
  8.1 0.7 multiply_add_fusion.1
  8.9 0.1 reduce_sum.34
  9.1 0.1 broadcast_in_dim.158
  9.2 1.3 gather_fusion.1
  10.5 0.8 select_select_fusion
  11.3 12.0 %all-to-all-start.1 = ((s32[128,32,2]{0,2,1:T(2,128)}), s32[128,32,2]{0,2,1:T(2,128)S(1)}, u32[]{:S(2)}, u32[]{:S(2)}) async-start(s32[128,32,2]{0,2,1:T(2,128)} %select_select_fusion), calls=%async_computation.1 | async-start | bytes 65536 | tf_op jit(solution)/shard_map/all_to_all | solution.py:65
  23.3 0.7 slice_convert_fusion
  24.0 0.6 gather_fusion
  24.7 0.5 copy-done.1
  25.2 3.4 convolution_convert_fusion.1
  28.6 1.8 fusion.57
  30.5 0.9 select_bitcast_fusion.1
  31.4 0.7 all-to-all-done.1
  32.1 8.6 %all-to-all-start = ((s32[128,64,16]{0,2,1:T(8,128)}), s32[128,64,16]{0,2,1:T(8,128)S(1)}, u32[]{:S(2)}, u32[]{:S(2)}) async-start(s32[128,64,16]{0,2,1:T(8,128)} %select_bitcast_fusion.1), calls=%async_computation | async-start | bytes 1048576 | tf_op jit(solution)/shard_map/all_to_all | solution.py:64
  40.7 3.4 convolution_convert_fusion
  44.1 0.1 copy-done.6
  44.2 0.7 fusion.58
  44.9 0.6 copy.31
  45.5 0.6 copy.32
  46.2 2.2 gather_fusion.2
  48.4 3.2 select_bitcast_fusion
  51.6 2.7 all-to-all-done
  54.4 0.8 copy-done.5
  55.2 7.9 %all-to-all-start.2 = ((bf16[128,64,128]{2,0,1:T(8,128)(2,1)}), bf16[128,64,128]{2,0,1:T(8,128)(2,1)S(1)}, u32[]{:S(2)}, u32[]{:S(2)}) async-start(bf16[128,64,128]{2,0,1:T(8,128)(2,1)} %select_bitcast_fusion), calls=%async_computation.2 | async-start | bytes 4194304 | tf_op jit(solution)/shard_map/all_to_all | solution.py:63
  63.2 5.3 convolution_multiply_fusion.1
  68.4 2.1 copy.30
  70.5 2.8 reshape_reshape.10
  73.2 5.9 %copy.29 = s32[128,32,2,16]{3,2,0,1:T(2,128)} copy(s32[128,32,2,16]{0,3,2,1:T(8,128)} %bitcast.89) | data formatting | bytes 1048576 | tf_op jit(solution)/shard_map/all_to_all | solution.py:64
  79.1 3.5 copy.34
  82.6 30.0 %all-to-all-done.2 = bf16[128,64,128]{2,0,1:T(8,128)(2,1)S(1)} async-done(((bf16[128,64,128]{2,0,1:T(8,128)(2,1)}), bf16[128,64,128]{2,0,1:T(8,128)(2,1)S(1)}, u32[]{:S(2)}, u32[]{:S(2)}) %all-to-all-start.2) | async-done | bytes 2097184 | tf_op jit(solution)/shard_map/all_to_all | solution.py:63
  112.6 3.6 copy.33
  116.2 91.4 %while.12 = (s32[]{:T(128)}, f32[512,128]{1,0:T(8,128)}, s32[8,1024,16]{1,2,0:T(8,128)}, s32[8,1024]{1,0:T(8,128)S(1)}, bf16[8,1024,128]{2,1,0:T(8,128)(2,1)}, /*index=5*/s32[]{:T(128)}, s32[]{:T(128)}) while((s32[]{:T(128)}, f32[512,128]{1,0:T(8,128)}, s32[8,1024,16]{1,2,0:T(8,128)}, s32[8,1024]{1,0:T(8,128)S(1)}, ...), condition=%wide.region_4.5_spmd.clone.clone, body=%wide.region_3.4_spmd.clone.clone.sunk | while | flops 167919616 | bytes 1151583 | solution.py:114
  116.2 0.8 dynamic-slice_bitcast_fusion.2
  117.1 0.2 compare_reduce_fusion.17
  117.3 10.3 %convolution_add_fusion.4 = f32[512,128]{1,0:T(8,128)} fusion(s32[1024]{0:T(1024)S(1)} %bitcast.94, s32[1024]{0:T(1024)S(1)} %bitcast.95, s32[1024]{0:T(1024)S(1)} %bitcast.96, s32[1024]{0:T(1024)S(1)} %bitcast.97, s32[1024]{0:T(1024)S(1)} %bitcast.98, s32[1024]{0:T(1024)S(1)} %bitcast.99, s32[1024]{0:T(1024)S(1)} %bitcast.100, ...), kind=kOutput, calls=%fused_computation.37.clone.1 | convolution fusion | flops 167903232 | bytes 868865 | tf_op jit(solution)/shard_map/while/body/eval_jaxpr/dot_general | solution.py:103
  127.6 0.8 dynamic-slice_bitcast_fusion.2
  128.5 0.2 compare_reduce_fusion.17
  128.7 10.3 %convolution_add_fusion.4 = f32[512,128]{1,0:T(8,128)} fusion(s32[1024]{0:T(1024)S(1)} %bitcast.94, s32[1024]{0:T(1024)S(1)} %bitcast.95, s32[1024]{0:T(1024)S(1)} %bitcast.96, s32[1024]{0:T(1024)S(1)} %bitcast.97, s32[1024]{0:T(1024)S(1)} %bitcast.98, s32[1024]{0:T(1024)S(1)} %bitcast.99, s32[1024]{0:T(1024)S(1)} %bitcast.100, ...), kind=kOutput, calls=%fused_computation.37.clone.1 | convolution fusion | flops 167903232 | bytes 868865 | tf_op jit(solution)/shard_map/while/body/eval_jaxpr/dot_general | solution.py:103
  139.0 0.8 dynamic-slice_bitcast_fusion.2
  139.9 0.2 compare_reduce_fusion.17
  140.1 10.3 %convolution_add_fusion.4 = f32[512,128]{1,0:T(8,128)} fusion(s32[1024]{0:T(1024)S(1)} %bitcast.94, s32[1024]{0:T(1024)S(1)} %bitcast.95, s32[1024]{0:T(1024)S(1)} %bitcast.96, s32[1024]{0:T(1024)S(1)} %bitcast.97, s32[1024]{0:T(1024)S(1)} %bitcast.98, s32[1024]{0:T(1024)S(1)} %bitcast.99, s32[1024]{0:T(1024)S(1)} %bitcast.100, ...), kind=kOutput, calls=%fused_computation.37.clone.1 | convolution fusion | flops 167903232 | bytes 868865 | tf_op jit(solution)/shard_map/while/body/eval_jaxpr/dot_general | solution.py:103
  150.5 0.8 dynamic-slice_bitcast_fusion.2
  151.4 0.2 compare_reduce_fusion.17
  151.6 10.3 %convolution_add_fusion.4 = f32[512,128]{1,0:T(8,128)} fusion(s32[1024]{0:T(1024)S(1)} %bitcast.94, s32[1024]{0:T(1024)S(1)} %bitcast.95, s32[1024]{0:T(1024)S(1)} %bitcast.96, s32[1024]{0:T(1024)S(1)} %bitcast.97, s32[1024]{0:T(1024)S(1)} %bitcast.98, s32[1024]{0:T(1024)S(1)} %bitcast.99, s32[1024]{0:T(1024)S(1)} %bitcast.100, ...), kind=kOutput, calls=%fused_computation.37.clone.1 | convolution fusion | flops 167903232 | bytes 868865 | tf_op jit(solution)/shard_map/while/body/eval_jaxpr/dot_general | solution.py:103
  161.9 0.8 dynamic-slice_bitcast_fusion.2
  162.8 0.2 compare_reduce_fusion.17
  163.0 10.3 %convolution_add_fusion.4 = f32[512,128]{1,0:T(8,128)} fusion(s32[1024]{0:T(1024)S(1)} %bitcast.94, s32[1024]{0:T(1024)S(1)} %bitcast.95, s32[1024]{0:T(1024)S(1)} %bitcast.96, s32[1024]{0:T(1024)S(1)} %bitcast.97, s32[1024]{0:T(1024)S(1)} %bitcast.98, s32[1024]{0:T(1024)S(1)} %bitcast.99, s32[1024]{0:T(1024)S(1)} %bitcast.100, ...), kind=kOutput, calls=%fused_computation.37.clone.1 | convolution fusion | flops 167903232 | bytes 868865 | tf_op jit(solution)/shard_map/while/body/eval_jaxpr/dot_general | solution.py:103
  173.3 0.8 dynamic-slice_bitcast_fusion.2
  174.2 0.2 compare_reduce_fusion.17
  174.4 10.3 %convolution_add_fusion.4 = f32[512,128]{1,0:T(8,128)} fusion(s32[1024]{0:T(1024)S(1)} %bitcast.94, s32[1024]{0:T(1024)S(1)} %bitcast.95, s32[1024]{0:T(1024)S(1)} %bitcast.96, s32[1024]{0:T(1024)S(1)} %bitcast.97, s32[1024]{0:T(1024)S(1)} %bitcast.98, s32[1024]{0:T(1024)S(1)} %bitcast.99, s32[1024]{0:T(1024)S(1)} %bitcast.100, ...), kind=kOutput, calls=%fused_computation.37.clone.1 | convolution fusion | flops 167903232 | bytes 868865 | tf_op jit(solution)/shard_map/while/body/eval_jaxpr/dot_general | solution.py:103
  184.8 0.8 dynamic-slice_bitcast_fusion.2
  185.7 0.2 compare_reduce_fusion.17
  185.9 10.3 %convolution_add_fusion.4 = f32[512,128]{1,0:T(8,128)} fusion(s32[1024]{0:T(1024)S(1)} %bitcast.94, s32[1024]{0:T(1024)S(1)} %bitcast.95, s32[1024]{0:T(1024)S(1)} %bitcast.96, s32[1024]{0:T(1024)S(1)} %bitcast.97, s32[1024]{0:T(1024)S(1)} %bitcast.98, s32[1024]{0:T(1024)S(1)} %bitcast.99, s32[1024]{0:T(1024)S(1)} %bitcast.100, ...), kind=kOutput, calls=%fused_computation.37.clone.1 | convolution fusion | flops 167903232 | bytes 868865 | tf_op jit(solution)/shard_map/while/body/eval_jaxpr/dot_general | solution.py:103
  196.2 0.8 dynamic-slice_bitcast_fusion.2
  197.1 0.2 compare_reduce_fusion.17
  197.3 10.3 %convolution_add_fusion.4 = f32[512,128]{1,0:T(8,128)} fusion(s32[1024]{0:T(1024)S(1)} %bitcast.94, s32[1024]{0:T(1024)S(1)} %bitcast.95, s32[1024]{0:T(1024)S(1)} %bitcast.96, s32[1024]{0:T(1024)S(1)} %bitcast.97, s32[1024]{0:T(1024)S(1)} %bitcast.98, s32[1024]{0:T(1024)S(1)} %bitcast.99, s32[1024]{0:T(1024)S(1)} %bitcast.100, ...), kind=kOutput, calls=%fused_computation.37.clone.1 | convolution fusion | flops 167903232 | bytes 868865 | tf_op jit(solution)/shard_map/while/body/eval_jaxpr/dot_general | solution.py:103
  207.7 4.1 convolution_multiply_fusion
  211.8 57.2 %all-reduce.6.cloned.1.call-done = f32[512,128]{1,0:T(8,128)} async-done(((f32[512,128]{1,0:T(8,128)}), f32[512,128]{1,0:T(8,128)}) %all-reduce.6.cloned.1.call-update) | async-done | bytes 262160 | tf_op jit(solution)/shard_map/psum | solution.py:115
  269.0 1.1 multiply_reduce_fusion
  270.1 0.6 sqrt_add_fusion
  270.7 1.8 divide_subtract_fusion
  272.5 295.0 %all-reduce.8.cloned.1.call-done = (f32[512,3456]{1,0:T(8,128)}, f32[512,3456]{1,0:T(8,128)}) async-done(((f32[512,3456]{1,0:T(8,128)}, f32[512,3456]{1,0:T(8,128)}), (f32[512,3456]{1,0:T(8,128)}, f32[512,3456]{1,0:T(8,128)})) %all-reduce.8.cloned.1.call-update) | async-done | bytes 14155792
  567.5 1.6 constant_dynamic-slice_fusion.1
  (38 shorter events, 0.7 us)
Async XLA Ops:
  7.2 16.9 %copy-start = (s32[128,26,16]{0,2,1:T(8,128)S(1)}, s32[128,26,16]{0,2,1:T(8,128)}, u32[]{:S(2)}) copy-start(s32[128,26,16]{0,2,1:T(8,128)} %param.18) | copy-start | bytes 638980
  11.3 20.8 %all-to-all-start.1 = ((s32[128,32,2]{0,2,1:T(2,128)}), s32[128,32,2]{0,2,1:T(2,128)S(1)}, u32[]{:S(2)}, u32[]{:S(2)}) async-start(s32[128,32,2]{0,2,1:T(2,128)} %select_select_fusion), calls=%async_computation.1 | async-start | bytes 65536 | tf_op jit(solution)/shard_map/all_to_all | solution.py:65
  24.0 1.2 copy-start.1
  25.2 3.4 copy-start.3
  25.2 3.4 copy-start.4
  28.6 1.8 copy-start.7
  32.1 22.3 %all-to-all-start = ((s32[128,64,16]{0,2,1:T(8,128)}), s32[128,64,16]{0,2,1:T(8,128)S(1)}, u32[]{:S(2)}, u32[]{:S(2)}) async-start(s32[128,64,16]{0,2,1:T(8,128)} %select_bitcast_fusion.1), calls=%async_computation | async-start | bytes 1048576 | tf_op jit(solution)/shard_map/all_to_all | solution.py:64
  40.6 3.5 copy-start.2
  40.6 3.6 copy-start.6
  54.4 0.8 copy-start.5
  55.2 57.5 %all-to-all-start.2 = ((bf16[128,64,128]{2,0,1:T(8,128)(2,1)}), bf16[128,64,128]{2,0,1:T(8,128)(2,1)S(1)}, u32[]{:S(2)}, u32[]{:S(2)}) async-start(bf16[128,64,128]{2,0,1:T(8,128)(2,1)} %select_bitcast_fusion), calls=%async_computation.2 | async-start | bytes 4194304 | tf_op jit(solution)/shard_map/all_to_all | solution.py:63
  63.1 205.9 %all-reduce.6.cloned.1.call-start = ((), (), s32[]{:S(2)}) async-start(), calls=%async_computation.3 | async-start | bytes 524288 | tf_op jit(solution)/shard_map/psum | solution.py:115
  207.7 359.8 %all-reduce.8.cloned.1.call-start = ((), (), s32[]{:S(2)}) async-start(), calls=%async_computation.4 | async-start | bytes 28311552
  211.8 58.3 %copy-start.9 = (f32[512]{0:T(512)S(1)}, f32[512]{0:T(512)}, u32[]{:S(2)}) copy-start(f32[512]{0:T(512)} %param.22) | copy-start | bytes 6148
  211.8 58.3 %copy-start.10 = (s32[512]{0:T(512)S(1)}, s32[512]{0:T(512)}, u32[]{:S(2)}) copy-start(s32[512]{0:T(512)} %param.23) | copy-start | bytes 6148
  211.8 58.9 %copy-start.8 = (f32[512,128]{1,0:T(8,128)S(1)}, f32[512,128]{1,0:T(8,128)}, u32[]{:S(2)}) copy-start(f32[512,128]{1,0:T(8,128)} %param.21) | copy-start | bytes 786436
Sparse Core Ops, SparseCore 0:
  207.8 61.1 all-reduce.5
  275.8 291.6 all-reduce.7
where the time goes:
time: 578 us; the launch traced here: 576 us
  waiting for transfers between devices  386 us (67%)
  matrix products  101 us (17%)
  local copies, waits for them, and re-layouts  33.5 us (6%)
  starting transfers between devices  28.6 us (5%)
  between operations  14.2 us (2%)
  other arithmetic  12.5 us (2%)
    unnamed x3, waiting for transfers between devices  295 us
    dot_general x8, matrix products, add_block(): lax.dot_general(counts, grad_block, (((0,), (0,)), ((), ())), preferred_e...  82.6 us
    psum x1, waiting for transfers between devices, local(): total_grad = lax.psum(local_grad, 'narrow')  57.2 us
    all_to_all x1, waiting for transfers between devices, local(): lax.all_to_all(send_grad, 'wide', split_axis=1, concat_axis=0, tiled=True)  30 us
    all_to_all x1, starting transfers between devices, local(): lax.all_to_all(send_lengths, 'wide', split_axis=1, concat_axis=0, tiled=T...  12 us
  transfers between devices with their start and end apart: 5, of which 5 were waited for; matrix products, arithmetic and copies ran while one was open for 8% of the time, Pallas kernels for 0%

commit v1 on v0

v1 whole, which is shorter than its diff:
```python
import math

import jax
import jax.numpy as jnp
import numpy as np
from jax import lax
from jax.experimental import pallas as pl
from jax.experimental.pallas import tpu as pltpu
from jax.sharding import Mesh
from jax.sharding import PartitionSpec as P

NY, NZ, NX, NC = 4, 8, 4, 2
NW = NY * NZ
EMB, TABLES, RANK, UNIQ, BAG = 128, 26, 512, 512, 16
COLS = 27
XB = 7
S = 128
HALF = RANK // NC
ROWB = UNIQ // (NX * NC)
F32, BF16 = jnp.float32, jnp.bfloat16
WIDE = ("y", "z")
NARROW = ("x", "c")
ALL = WIDE + NARROW
VMEM = pl.BlockSpec(memory_space=pltpu.VMEM)
SMEM = pl.BlockSpec(memory_space=pltpu.SMEM)
SWAP = [(0, 1), (1, 0)]


def rank_order():
    order = np.arange(RANK).reshape(NW, NX, NC, 2).transpose(2, 0, 1, 3).reshape(-1)
    return np.eye(RANK, dtype=np.float32)[order]


def params():
    return pltpu.CompilerParams(vmem_limit_bytes=48 * 1024 * 1024)


def bag_kernel(core, ids_own, ids_sib, pooled_own, pooled_sib, out):
    mine = core[0]
    places = lax.broadcasted_iota(jnp.int32, (ROWB, 2 * S), 0)

    @pl.loop(0, TABLES)
    def _(t):
        ids = jnp.concatenate([ids_own[t], ids_sib[t]], axis=1)
        low = jnp.bitwise_and(ids, ROWB - 1)
        part = jnp.bitwise_and(lax.shift_right_arithmetic(ids, 6), 1)
        field = jnp.bitwise_and(lax.shift_right_arithmetic(ids, 7), 3)
        value = jnp.where(
            (ids >= 0) & (part == mine), lax.shift_left(jnp.ones_like(ids), field * 8), 0
        )
        packed = jnp.zeros((ROWB, 2 * S), jnp.int32)
        for j in range(BAG):
            packed = packed + jnp.where(places == low[j : j + 1], value[j : j + 1], 0)
        counts = jnp.concatenate(
            [
                jnp.bitwise_and(lax.shift_right_logical(packed, 8 * f), 255).astype(F32).astype(BF16)
                for f in range(NX)
            ],
            axis=0,
        )
        at = pl.multiple_of(t * EMB, EMB)
        grads = jnp.concatenate([pooled_own[:, pl.ds(at, EMB)], pooled_sib[:, pl.ds(at, EMB)]], axis=0)
        sums = jnp.dot(counts, grads, preferred_element_type=F32).astype(BF16)
        for f in range(NX):
            out[f, t] = sums[f * ROWB : (f + 1) * ROWB]


def bag_sums(core, ids_own, ids_sib, pooled_own, pooled_sib):
    return pl.pallas_call(
        bag_kernel,
        out_shape=jax.ShapeDtypeStruct((NX, TABLES, ROWB, EMB), BF16),
        in_specs=[SMEM, VMEM, VMEM, VMEM, VMEM],
        out_specs=VMEM,
        compiler_params=params(),
        name="bag_sums",
    )(core, ids_own, ids_sib, pooled_own, pooled_sib)


def dense_kernel(place, own, sib, low0, low1, low2, low3, out, wide_x, wide_low):
    me = place[0]
    lows = (low0, low1, low2, low3)
    for g in range(2):
        for k in range(NX):
            src = lax.rem(me - k + NX, NX)
            for s, ref in enumerate((own, sib)):
                at = (k * 2 + s) * S
                wide_low[g, :, at : at + S] = lows[k][s, g]
                for j in range(XB):
                    wide_x[g, at : at + S, j * EMB : (j + 1) * EMB] = ref[src, g, j]

    @pl.loop(0, XB)
    def _(j):
        cols = pl.ds(pl.multiple_of(j * EMB, EMB), EMB)
        both = []
        for g in range(2):
            part = jnp.dot(wide_low[g], wide_x[g, :, cols], preferred_element_type=F32)
            both.append(part.reshape(NW, 8, EMB))
        out[:, pl.ds(pl.multiple_of(j * 16, 16), 16), :] = jnp.concatenate(both, axis=1).astype(BF16)


def dense_sums(place, own, sib, lows):
    return pl.pallas_call(
        dense_kernel,
        out_shape=jax.ShapeDtypeStruct((NW, 16 * XB, EMB), BF16),
        in_specs=[SMEM] + [VMEM] * 6,
        out_specs=VMEM,
        scratch_shapes=[
            pltpu.VMEM((2, NX * NC * S, XB * EMB), BF16),
            pltpu.VMEM((2, HALF, NX * NC * S), BF16),
        ],
        compiler_params=params(),
        name="dense_sums",
    )(place, own, sib, *lows)


def owner_kernel(owner, got, out, total):
    total[...] = jnp.zeros_like(total)

    @pl.loop(0, TABLES)
    def _(t):
        one = got[0, t].astype(F32)
        for k in range(1, NX):
            one = one + got[k, t].astype(F32)
        to = owner[t]
        total[to] = total[to] + one

    out[...] = total[...].astype(BF16)


def owner_sums(owner, got):
    return pl.pallas_call(
        owner_kernel,
        out_shape=jax.ShapeDtypeStruct((NW, ROWB, EMB), BF16),
        in_specs=[SMEM, VMEM],
        out_specs=VMEM,
        scratch_shapes=[pltpu.VMEM((NW, ROWB, EMB), F32)],
        compiler_params=params(),
        name="owner_sums",
    )(owner, got)


def adagrad_rows(rows, accum, admitted, grad):
    begin_acc = jnp.where(admitted == 1, jnp.float32(0.1), accum)
    new_acc = begin_acc + jnp.mean(grad * grad, axis=1)
    new_values = rows - 0.5 * grad / (jnp.sqrt(new_acc)[:, None] + 1e-08)
    return (new_values, new_acc)


def local(
    cross_input,
    upstream,
    cross_down,
    cross_up,
    cross_bias,
    bag_rows,
    bag_lengths,
    table_owner,
    table_rows,
    row_accum,
    admitted,
):
    me_x, me_c = lax.axis_index("x"), lax.axis_index("c")
    position = lax.broadcasted_iota(jnp.int32, (TABLES, BAG, S), 1)
    ids = jnp.where(
        position < bag_lengths.T[:, None, :], jnp.transpose(bag_rows, (1, 2, 0)), -1
    )
    ids_sib = lax.ppermute(ids, "c", SWAP)

    d_scale = (upstream.astype(F32) * cross_input.astype(F32)).astype(BF16)

    def blocks(a):
        padded = jnp.pad(a, ((0, 0), (0, (NX * XB - COLS) * EMB)))
        return jnp.transpose(padded.reshape(S, NX, XB, EMB), (1, 2, 0, 3))

    pair = jnp.stack([blocks(d_scale), blocks(cross_input)], axis=1)
    own = lax.all_to_all(pair, "x", split_axis=0, concat_axis=0, tiled=True)
    sib = lax.ppermute(own, "c", SWAP)

    low_t = lax.dot_general(
        cross_down, cross_input, (((1,), (1,)), ((), ())), preferred_element_type=F32
    ).astype(BF16)
    d_low_t = lax.dot_general(
        cross_up, d_scale, (((1,), (1,)), ((), ())), preferred_element_type=F32
    ).astype(BF16)
    order = jnp.asarray(rank_order(), BF16)
    halves = jnp.dot(
        order, jnp.concatenate([low_t, d_low_t], axis=1), preferred_element_type=F32
    ).astype(BF16)
    halves = jnp.transpose(halves.reshape(NC, HALF, 2, S), (0, 2, 1, 3))
    keep = jnp.where(me_c == 0, halves[0], halves[1])
    give = jnp.where(me_c == 0, halves[1], halves[0])
    low0 = jnp.stack([keep, lax.ppermute(give, "c", SWAP)])
    lows = [low0] + [
        lax.ppermute(low0, "x", [(i, (i + k) % NX) for i in range(NX)]) for k in range(1, NX)
    ]

    scale_tail = lax.dot_general(
        low_t, cross_up[:, EMB:], (((0,), (0,)), ((), ())), preferred_element_type=F32
    ) + cross_bias[EMB:].astype(F32)
    tail_grad = upstream[:, EMB:].astype(F32) * (scale_tail + 1.0) + lax.dot_general(
        d_low_t, cross_down[:, EMB:], (((0,), (0,)), ((), ())), preferred_element_type=F32
    )
    pooled = tail_grad.astype(BF16)
    pooled_sib = lax.ppermute(pooled, "c", SWAP)

    core = me_c.astype(jnp.int32).reshape(1)
    sums = bag_sums(core, ids, ids_sib, pooled, pooled_sib)
    got = lax.all_to_all(sums, "x", split_axis=0, concat_axis=0, tiled=True)
    dense = dense_sums(me_x.astype(jnp.int32).reshape(1), own, sib, lows)
    rows = owner_sums(table_owner, got)

    merged = jnp.concatenate([rows, dense], axis=1)
    merged = lax.all_to_all(merged, WIDE, split_axis=0, concat_axis=0, tiled=True)
    total = jnp.sum(merged.astype(F32), axis=0)
    row_part = jnp.broadcast_to(total[:ROWB], (NX, NC, ROWB, EMB))
    dense_part = total[ROWB:].reshape(XB * 2, NX, 2, EMB)
    dense_part = jnp.transpose(dense_part, (1, 0, 2, 3)).reshape(NX, 1, XB * 4, EMB)
    dense_part = jnp.broadcast_to(dense_part, (NX, NC, XB * 4, EMB))
    final = jnp.concatenate([row_part, dense_part], axis=2).reshape(NX * NC, ROWB + XB * 4, EMB)
    final = lax.all_to_all(final, NARROW, split_axis=0, concat_axis=0, tiled=True)
    row_grad = final[:, :ROWB].reshape(UNIQ, EMB)
    new_rows, new_accum = adagrad_rows(table_rows, row_accum, admitted, row_grad)

    norm_scale = 1.0 / math.sqrt(S * NW * NX * NC)
    grads = final[:, ROWB:].reshape(NX, NC, XB, 2, 2, EMB)
    grads = jnp.where(me_c == 0, grads[:, 0], grads[:, 1])
    grads = jnp.transpose(grads, (2, 3, 0, 1, 4)).reshape(2, 2, NX * XB * EMB)
    grads = grads[:, :, : COLS * EMB] * norm_scale
    return (new_rows, new_accum, grads[0], grads[1])


def solution(mesh):
    inner = Mesh(mesh.devices.reshape(NY, NZ, NX, NC), ALL)
    return jax.shard_map(
        local,
        mesh=inner,
        in_specs=(
            P(ALL, None),
            P(ALL, None),
            P(),
            P(),
            P(),
            P(ALL, None, None),
            P(ALL, None),
            P(),
            P(WIDE, None),
            P(WIDE),
            P(WIDE),
        ),
        out_specs=(
            P(WIDE, None),
            P(WIDE),
            P(ALL, None),
            P(ALL, None),
        ),
        check_vma=False,
    )
```

time: 578 us -> 158 us (0.27)
  waiting for transfers between devices: 386 us -> 34.9 us
  matrix products: 101 us -> 8.4 us
  blocking collectives: 0 us -> 59.4 us
  local copies, waits for them, and re-layouts: 33.5 us -> 13.3 us
  Pallas kernels: 0 us -> 15.8 us
  between operations: 14.2 us -> 1.01 us
  starting transfers between devices: 28.6 us -> 18.8 us
  other arithmetic: 12.5 us -> 5.39 us
    unnamed x3 -> x0, waiting for transfers between devices: 295 us -> none
    dot_general x14 -> x5, matrix products: 101 us -> 8.4 us  [the longest x1 3.63 us: local(): lax.dot_general(cross_down, cross_input, (((1,), (1,)), ((), ())), prefer...]
    all_to_all x0 -> x2, blocking collectives: none -> 59.4 us  [the longest x1 45.1 us: local(): lax.all_to_all(merged, WIDE, split_axis=0, concat_axis=0, tiled=True)]
    psum x1 -> x0, waiting for transfers between devices: 57.2 us -> none  [local(): total_grad = lax.psum(local_grad, 'narrow')]
    all_to_all x3 -> x2, starting transfers between devices: 28.5 us -> 8.42 us  [the longest x1 4.84 us: local(): own = lax.all_to_all(pair, 'x', split_axis=0, concat_axis=0, tiled=True)]
    pallas_call x0 -> x3, Pallas kernels: none -> 15.8 us  [the longest x1 9.07 us: bag_sums(): pl.pallas_call(bag_kernel, out_shape=jax.ShapeDtypeStruct((NX, TABLES, RO...]
    ppermute x0 -> x7, waiting for transfers between devices: none -> 15 us  [the longest x3 10.3 us: local(): lax.ppermute(low0, 'x', [(i, (i + k) % NX) for i in range(NX)])]
    all_to_all x3 -> x2, waiting for transfers between devices: 33.4 us -> 19.9 us  [the longest x1 11.8 us: local(): own = lax.all_to_all(pair, 'x', split_axis=0, concat_axis=0, tiled=True)]
  transfers between devices with their start and end apart: 5 -> 9, of which waited for: 5 -> 6; matrix products, arithmetic and copies ran while one was open for 8% -> 9% of each run, Pallas kernels for 0% -> 6%
where the time goes in v1:
time: 158 us; the launch traced here: 157 us
  blocking collectives  59.4 us (38%)
  waiting for transfers between devices  34.9 us (22%)
  starting transfers between devices  18.8 us (12%)
  Pallas kernels  15.8 us (10%)
  local copies, waits for them, and re-layouts  13.3 us (8%)
  matrix products  8.4 us (5%)
  other arithmetic  5.39 us (3%)
    all_to_all x1, blocking collectives, local(): lax.all_to_all(merged, WIDE, split_axis=0, concat_axis=0, tiled=True)  45.1 us
    all_to_all x1, blocking collectives, local(): lax.all_to_all(final, NARROW, split_axis=0, concat_axis=0, tiled=True)  14.3 us
    all_to_all x1, waiting for transfers between devices, local(): own = lax.all_to_all(pair, 'x', split_axis=0, concat_axis=0, tiled=True)  11.8 us
    ppermute x3, waiting for transfers between devices, local(): lax.ppermute(low0, 'x', [(i, (i + k) % NX) for i in range(NX)])  10.3 us
    pallas_call x1, Pallas kernels, bag_sums(): pl.pallas_call(bag_kernel, out_shape=jax.ShapeDtypeStruct((NX, TABLES, RO...  9.07 us
    all_to_all x1, waiting for transfers between devices, local(): got = lax.all_to_all(sums, 'x', split_axis=0, concat_axis=0, tiled=True)  8.14 us
    pallas_call x1, Pallas kernels, dense_sums(): pl.pallas_call(dense_kernel, out_shape=jax.ShapeDtypeStruct((NW, 16 * XB,...  5.67 us
    unnamed x30, local copies, waits for them, and re-layouts  5.63 us
  transfers between devices with their start and end apart: 9, of which 6 were waited for; matrix products, arithmetic and copies ran while one was open for 9% of the time, Pallas kernels for 6%

profile of v1, /device:TPU:1, one launch (start us, length us, event | category | flops | bytes accessed | tf_op | source)
XLA Modules:
  0.0 156.9 jit_solution(312611329085409877)
XLA Ops:
  0.6 0.0 copy-start.4
  0.6 2.0 %copy.26 = bf16[128,3456]{0,1:T(8,128)(2,1)S(1)} copy(bf16[128,3456]{1,0:T(8,128)(2,1)} %param.12) | data formatting | bytes 1769472 | tf_op args[0]
  2.6 1.0 copy.25
  3.6 0.2 multiply_convert_fusion
  3.9 1.0 pad.8
  4.9 0.1 pad.7
  4.9 0.6 copy.27
  5.6 1.6 %copy.29 = bf16[128,4,7,128]{3,0,2,1:T(8,128)(2,1)S(1)} copy(bf16[128,4,7,128]{0,3,2,1:T(8,128)(2,1)} %bitcast.48) | data formatting | bytes 1835008 | tf_op jit(solution)/shard_map/reshape | solution.py:173
  7.2 1.4 pad_maximum_fusion
  8.6 4.8 %all-to-all-start.1 = ((bf16[4,2,7,128,128]{4,3,2,1,0:T(8,128)(2,1)}), bf16[4,2,7,128,128]{4,3,2,1,0:T(8,128)(2,1)S(1)}, u32[]{:S(2)}, u32[]{:S(2)}) async-start(bf16[4,2,7,128,128]{4,3,2,1,0:T(8,128)(2,1)} %pad_maximum_fusion), calls=%async_computation.1 | async-start | bytes 3670016 | tf_op jit(solution)/shard_map/all_to_all | solution.py:176
  13.5 3.6 %convolution_convert_fusion.2 = bf16[512,128]{0,1:T(8,128)(2,1)S(1)} fusion(bf16[512,3456]{1,0:T(8,128)(2,1)} %param.14, bf16[128,3456]{1,0:T(8,128)(2,1)} %param.12), kind=kOutput, calls=%fused_computation.14 | convolution fusion | flops 453050368 | bytes 4554752 | tf_op jit(solution)/shard_map/dot_general | solution.py:179
  17.1 0.0 copy-done.10
  17.1 0.0 copy-start.13
  17.1 0.0 copy-start.5
  17.1 1.3 convolution_convert_fusion.1
  18.5 0.0 copy-start.3
  18.5 0.6 fusion.1
  19.1 0.0 copy-done.6
  19.1 1.4 copy-done.3
  20.5 0.6 fusion.2.pooled_own
  21.2 2.1 %collective-permute-start.1 = (bf16[128,3328]{1,0:T(8,128)(2,1)S(1)}, bf16[128,3328]{1,0:T(8,128)(2,1)}, u32[]{:S(2)}, u32[]{:S(2)}) collective-permute-start(bf16[128,3328]{1,0:T(8,128)(2,1)S(1)} %fusion.2.pooled_own), channel_id=1, source_target_pairs={{0,1},{1,0},{2,3},{3,2},{4,5},{5,4},{6,7},{7,6},{8,9},{9,8},{10,11... | collective-permute-start | bytes 2555912 | tf_op jit(solution)/shard_map/ppermute | solution.py:204
  23.3 11.8 %all-to-all-done.1.own = bf16[4,2,7,128,128]{4,3,2,1,0:T(8,128)(2,1)S(1)} async-done(((bf16[4,2,7,128,128]{4,3,2,1,0:T(8,128)(2,1)}), bf16[4,2,7,128,128]{4,3,2,1,0:T(8,128)(2,1)S(1)}, u32[]{:S(2)}, u32[]{:S(2)}) %all-to-all-start.1) | async-done | bytes 1835040 | tf_op jit(solution)/shard_map/all_to_all | solution.py:176
  35.0 2.9 %collective-permute-start.2 = (bf16[4,2,7,128,128]{4,3,2,1,0:T(8,128)(2,1)S(1)}, bf16[4,2,7,128,128]{4,3,2,1,0:T(8,128)(2,1)}, u32[]{:S(2)}, u32[]{:S(2)}) collective-permute-start(bf16[4,2,7,128,128]{4,3,2,1,0:T(8,128)(2,1)S(1)} %all-to-all-done.1.own), channel_id=1, source_target_pairs={{0,1},{1,0},{2,3},{3,2},{4,5},{5,4},{6,7},{7,6},{8,9},{9,8},{10,11... | collective-permute-start | bytes 5505032 | tf_op jit(solution)/shard_map/ppermute | solution.py:177
  37.9 0.0 copy-done.9
  38.0 0.1 collective-permute-start
  38.1 3.4 %collective-permute-done.ids_sib = s32[26,16,128]{2,1,0:T(8,128)S(1)} collective-permute-done((s32[26,16,128]{2,1,0:T(8,128)S(1)}, s32[26,16,128]{2,1,0:T(8,128)S(1)}, u32[]{:S(2)}, u32[]{:S(2)}) %collective-permute-start) | collective-permute-done | bytes 213024 | tf_op jit(solution)/shard_map/ppermute | solution.py:167
  41.5 0.0 collective-permute-done.1.pooled_sib
  41.5 9.1 %bag_sums.1 = bf16[4,26,64,128]{3,2,1,0:T(8,128)(2,1)S(1)} custom-call(s32[1]{0:T(128)} %bitcast.core, s32[26,16,128]{2,1,0:T(8,128)S(1)} %bitcast_select_fusion.ids_own, s32[26,16,128]{2,1,0:T(8,128)S(1)} %collective-permute-done.ids_sib, bf16[128,3328]{1,0:T(8,128)(2,1)S(1)} %fusion.2.pooled_own, bf16[128,3328]{1,0:T(8,128)(2,1)} %collective-permute-done.1.pooled_sib), custom_call_target="tpu_custom_call" | custom-call | tf_op jit(solution)/shard_map/bag_sums/pallas_call | solution.py:69
  50.6 0.0 copy-start
  50.6 1.2 copy-done
  51.8 3.6 %all-to-all-start = ((bf16[4,26,64,128]{3,2,1,0:T(8,128)(2,1)}), bf16[4,26,64,128]{3,2,1,0:T(8,128)(2,1)S(1)}, u32[]{:S(2)}, u32[]{:S(2)}) async-start(bf16[4,26,64,128]{3,2,1,0:T(8,128)(2,1)} %copy-done), calls=%async_computation | async-start | bytes 3407872 | tf_op jit(solution)/shard_map/all_to_all | solution.py:208
  55.4 0.0 copy-start.1
  55.4 2.2 %fusion.5 = bf16[512,256]{0,1:T(8,128)(2,1)} fusion(bf16[512,512]{1,0:T(8,128)(2,1)} %constant.33.clone, bf16[512,128]{0,1:T(8,128)(2,1)} %bitcast.52, bf16[512,128]{0,1:T(8,128)(2,1)} %copy-done.13), kind=kOutput, calls=%fused_computation.12 | convolution fusion | flops 134873088 | bytes 1048576 | tf_op jit(solution)/shard_map/dot_general | solution.py:186
  57.6 1.7 %reshape.60 = bf16[2,256,2,128]{1,0,3,2:T(2,128)(2,1)} reshape(bf16[512,256]{0,1:T(8,128)(2,1)} %fusion.5) | data formatting | bytes 524288 | tf_op jit(solution)/shard_map/reshape | solution.py:189
  59.3 1.8 %copy.31 = bf16[2,256,2,128]{3,1,2,0:T(8,128)(2,1)} copy(bf16[2,256,2,128]{1,0,3,2:T(2,128)(2,1)} %reshape.60) | data formatting | bytes 524288 | tf_op jit(solution)/shard_map/reshape | solution.py:189
  61.1 1.0 broadcast_select_fusion
  62.1 0.2 collective-permute-start.3
  62.4 1.2 collective-permute-done.3
  63.6 0.7 pad_maximum_fusion.3.low0
  64.3 1.5 collective-permute-start.4
  65.8 2.4 %collective-permute-start.5 = (bf16[2,2,256,128]{3,2,1,0:T(8,128)(2,1)}, bf16[2,2,256,128]{3,2,1,0:T(8,128)(2,1)}, u32[]{:S(2)}, u32[]{:S(2)}) collective-permute-start(bf16[2,2,256,128]{3,2,1,0:T(8,128)(2,1)} %pad_maximum_fusion.3.low0), channel_id=1, source_target_pairs={{0,4},{2,6},{4,0},{6,2},{1,5},{3,7},{5,1},{7,3},{8,12},{10,14},{12... | collective-permute-start | bytes 786440 | tf_op jit(solution)/shard_map/ppermute | solution.py:194
  68.2 1.2 collective-permute-start.6
  69.4 8.1 %all-to-all-done.got = bf16[4,26,64,128]{3,2,1,0:T(8,128)(2,1)S(1)} async-done(((bf16[4,26,64,128]{3,2,1,0:T(8,128)(2,1)}), bf16[4,26,64,128]{3,2,1,0:T(8,128)(2,1)S(1)}, u32[]{:S(2)}, u32[]{:S(2)}) %all-to-all-start) | async-done | bytes 1703968 | tf_op jit(solution)/shard_map/all_to_all | solution.py:208
  77.5 1.0 owner_sums.1
  78.5 4.9 %collective-permute-done.4.low1 = bf16[2,2,256,128]{3,2,1,0:T(8,128)(2,1)} collective-permute-done((bf16[2,2,256,128]{3,2,1,0:T(8,128)(2,1)}, bf16[2,2,256,128]{3,2,1,0:T(8,128)(2,1)}, u32[]{:S(2)}, u32[]{:S(2)}) %collective-permute-start.4) | collective-permute-done | bytes 262176 | tf_op jit(solution)/shard_map/ppermute | solution.py:194
  83.4 5.5 %collective-permute-done.5.low2 = bf16[2,2,256,128]{3,2,1,0:T(8,128)(2,1)} collective-permute-done((bf16[2,2,256,128]{3,2,1,0:T(8,128)(2,1)}, bf16[2,2,256,128]{3,2,1,0:T(8,128)(2,1)}, u32[]{:S(2)}, u32[]{:S(2)}) %collective-permute-start.5) | collective-permute-done | bytes 262176 | tf_op jit(solution)/shard_map/ppermute | solution.py:194
  88.8 0.0 collective-permute-done.6.low3
  88.8 0.0 collective-permute-done.2.sib
  88.9 5.7 %dense_sums.1 = bf16[32,112,128]{2,1,0:T(8,128)(2,1)S(1)} custom-call(s32[1]{0:T(128)} %bitcast.3.place, bf16[4,2,7,128,128]{4,3,2,1,0:T(8,128)(2,1)S(1)} %all-to-all-done.1.own, bf16[4,2,7,128,128]{4,3,2,1,0:T(8,128)(2,1)} %collective-permute-done.2.sib, bf16[2,2,256,128]{3,2,1,0:T(8,128)(2,1)} %pad_maximum_fusion.3.low0, ...), custom_call_target="tpu_custom_call" | custom-call | tf_op jit(solution)/shard_map/dense_sums/pallas_call | solution.py:102
  94.5 0.1 pad_maximum_fusion.1
  94.6 45.1 %all_to_all.20 = bf16[32,176,128]{2,1,0:T(8,128)(2,1)S(1)} all-to-all(bf16[32,176,128]{2,1,0:T(8,128)(2,1)S(1)} %pad_maximum_fusion.1), channel_id=1, replica_groups=mesh['y'=4,'z'=8,'x'=4,'c'=2] {'y','z'}, dimensions={0} | all-to-all | bytes 2883584 | tf_op jit(solution)/shard_map/all_to_all | solution.py:213
  139.7 0.2 convert_reduce_fusion
  140.0 0.0 copy-start.11
  140.0 0.0 copy-start.12
  140.0 0.0 copy-start.7
  140.1 14.3 %all_to_all.21 = f32[8,92,128]{2,1,0:T(8,128)S(1)} all-to-all(f32[8,92,128]{2,1,0:T(8,128)S(1)} %bitcast.50), channel_id=1, replica_groups=mesh['y'=4,'z'=8,'x'=4,'c'=2] {'x','c'}, dimensions={0} | all-to-all | bytes 753664 | tf_op jit(solution)/shard_map/all_to_all | solution.py:220
  154.4 0.1 multiply_reduce_fusion
  154.5 0.1 div.18
  154.6 0.1 copy.34
  154.7 0.1 broadcast_select_fusion.1
  154.9 0.6 slice_bitcast_fusion
  155.5 0.0 copy-done.12
  155.5 0.6 sqrt_add_fusion
  156.1 0.8 fusion.9
  (27 shorter events, 0.2 us)
Async XLA Ops:
  0.6 2.0 %copy-start.4 = (bf16[128,3456]{1,0:T(8,128)(2,1)S(1)}, bf16[128,3456]{1,0:T(8,128)(2,1)}, u32[]{:S(2)}) copy-start(bf16[128,3456]{1,0:T(8,128)(2,1)} %param.13) | copy-start | bytes 2654212
  8.6 26.4 %all-to-all-start.1 = ((bf16[4,2,7,128,128]{4,3,2,1,0:T(8,128)(2,1)}), bf16[4,2,7,128,128]{4,3,2,1,0:T(8,128)(2,1)S(1)}, u32[]{:S(2)}, u32[]{:S(2)}) async-start(bf16[4,2,7,128,128]{4,3,2,1,0:T(8,128)(2,1)} %pad_maximum_fusion), calls=%async_computation.1 | async-start | bytes 3670016 | tf_op jit(solution)/shard_map/all_to_all | solution.py:176
  13.4 3.6 %copy-start.10 = (bf16[3456]{0:T(1024)(128)(2,1)S(1)}, bf16[3456]{0:T(1024)(128)(2,1)}, u32[]{:S(2)}) copy-start(bf16[3456]{0:T(1024)(128)(2,1)} %param.16) | copy-start | bytes 20740
  13.5 3.7 %copy-start.2 = (bf16[512,3456]{1,0:T(8,128)(2,1)S(1)}, bf16[512,3456]{1,0:T(8,128)(2,1)}, u32[]{:S(2)}) copy-start(bf16[512,3456]{1,0:T(8,128)(2,1)} %param.15) | copy-start | bytes 10616836
  17.1 1.4 copy-start.13
  17.1 1.3 copy-start.5
  18.5 0.7 copy-start.6
  18.5 2.1 %copy-start.3 = (bf16[512,3456]{1,0:T(8,128)(2,1)S(1)}, bf16[512,3456]{1,0:T(8,128)(2,1)}, u32[]{:S(2)}) copy-start(bf16[512,3456]{1,0:T(8,128)(2,1)} %param.14) | copy-start | bytes 10616836
  20.5 17.4 %copy-start.8 = (s32[128,26,16]{0,2,1:T(8,128)S(1)}, s32[128,26,16]{0,2,1:T(8,128)}, u32[]{:S(2)}) copy-start(s32[128,26,16]{0,2,1:T(8,128)} %param.17) | copy-start | bytes 638980
  20.5 17.4 %copy-start.9 = (s32[128,26]{0,1:T(8,128)S(1)}, s32[128,26]{0,1:T(8,128)}, u32[]{:S(2)}) copy-start(s32[128,26]{0,1:T(8,128)} %param.18) | copy-start | bytes 39940
  21.2 20.3 %collective-permute-start.1 = (bf16[128,3328]{1,0:T(8,128)(2,1)S(1)}, bf16[128,3328]{1,0:T(8,128)(2,1)}, u32[]{:S(2)}, u32[]{:S(2)}) collective-permute-start(bf16[128,3328]{1,0:T(8,128)(2,1)S(1)} %fusion.2.pooled_own), channel_id=1, source_target_pairs={{0,1},{1,0},{2,3},{3,2},{4,5},{5,4},{6,7},{7,6},{8,9},{9,8},{10,11... | collective-permute-start | bytes 2555912 | tf_op jit(solution)/shard_map/ppermute | solution.py:204
  35.0 53.8 %collective-permute-start.2 = (bf16[4,2,7,128,128]{4,3,2,1,0:T(8,128)(2,1)S(1)}, bf16[4,2,7,128,128]{4,3,2,1,0:T(8,128)(2,1)}, u32[]{:S(2)}, u32[]{:S(2)}) collective-permute-start(bf16[4,2,7,128,128]{4,3,2,1,0:T(8,128)(2,1)S(1)} %all-to-all-done.1.own), channel_id=1, source_target_pairs={{0,1},{1,0},{2,3},{3,2},{4,5},{5,4},{6,7},{7,6},{8,9},{9,8},{10,11... | collective-permute-start | bytes 5505032 | tf_op jit(solution)/shard_map/ppermute | solution.py:177
  38.0 3.6 %collective-permute-start = (s32[26,16,128]{2,1,0:T(8,128)S(1)}, s32[26,16,128]{2,1,0:T(8,128)S(1)}, u32[]{:S(2)}, u32[]{:S(2)}) collective-permute-start(s32[26,16,128]{2,1,0:T(8,128)S(1)} %bitcast_select_fusion.ids_own), channel_id=1, source_target_pairs={{0,1},{1,0},{2,3},{3,2},{4,5},{5,4},{6,7},{7,6},{8,9},{9,8},{10,11... | collective-permute-start | bytes 638984 | tf_op jit(solution)/shard_map/ppermute | solution.py:167
  50.6 1.2 copy-start
  51.8 25.7 %all-to-all-start = ((bf16[4,26,64,128]{3,2,1,0:T(8,128)(2,1)}), bf16[4,26,64,128]{3,2,1,0:T(8,128)(2,1)S(1)}, u32[]{:S(2)}, u32[]{:S(2)}) async-start(bf16[4,26,64,128]{3,2,1,0:T(8,128)(2,1)} %copy-done), calls=%async_computation | async-start | bytes 3407872 | tf_op jit(solution)/shard_map/all_to_all | solution.py:208
  55.4 22.1 %copy-start.1 = (s32[26]{0:T(128)S(1)}, s32[26]{0:T(128)}, u32[]{:S(2)}) copy-start(s32[26]{0:T(128)} %owner.1) | copy-start | bytes 316
  62.1 1.4 collective-permute-start.3
  64.3 19.1 %collective-permute-start.4 = (bf16[2,2,256,128]{3,2,1,0:T(8,128)(2,1)}, bf16[2,2,256,128]{3,2,1,0:T(8,128)(2,1)}, u32[]{:S(2)}, u32[]{:S(2)}) collective-permute-start(bf16[2,2,256,128]{3,2,1,0:T(8,128)(2,1)} %pad_maximum_fusion.3.low0), channel_id=1, source_target_pairs={{0,2},{2,4},{4,6},{6,0},{1,3},{3,5},{5,7},{7,1},{8,10},{10,12},{12... | collective-permute-start | bytes 786440 | tf_op jit(solution)/shard_map/ppermute | solution.py:194
  65.8 23.1 %collective-permute-start.5 = (bf16[2,2,256,128]{3,2,1,0:T(8,128)(2,1)}, bf16[2,2,256,128]{3,2,1,0:T(8,128)(2,1)}, u32[]{:S(2)}, u32[]{:S(2)}) collective-permute-start(bf16[2,2,256,128]{3,2,1,0:T(8,128)(2,1)} %pad_maximum_fusion.3.low0), channel_id=1, source_target_pairs={{0,4},{2,6},{4,0},{6,2},{1,5},{3,7},{5,1},{7,3},{8,12},{10,14},{12... | collective-permute-start | bytes 786440 | tf_op jit(solution)/shard_map/ppermute | solution.py:194
  68.2 20.7 %collective-permute-start.6 = (bf16[2,2,256,128]{3,2,1,0:T(8,128)(2,1)}, bf16[2,2,256,128]{3,2,1,0:T(8,128)(2,1)}, u32[]{:S(2)}, u32[]{:S(2)}) collective-permute-start(bf16[2,2,256,128]{3,2,1,0:T(8,128)(2,1)} %pad_maximum_fusion.3.low0), channel_id=1, source_target_pairs={{0,6},{2,0},{4,2},{6,4},{1,7},{3,1},{5,3},{7,5},{8,14},{10,8},{12,... | collective-permute-start | bytes 786440 | tf_op jit(solution)/shard_map/ppermute | solution.py:194
  140.0 15.6 %copy-start.11 = (f32[512]{0:T(512)S(1)}, f32[512]{0:T(512)}, u32[]{:S(2)}) copy-start(f32[512]{0:T(512)} %param.21) | copy-start | bytes 6148
  140.0 15.5 %copy-start.12 = (s32[512]{0:T(512)S(1)}, s32[512]{0:T(512)}, u32[]{:S(2)}) copy-start(s32[512]{0:T(512)} %param.22) | copy-start | bytes 6148
  140.0 16.1 %copy-start.7 = (f32[512,128]{1,0:T(8,128)S(1)}, f32[512,128]{1,0:T(8,128)}, u32[]{:S(2)}) copy-start(f32[512,128]{1,0:T(8,128)} %param.20) | copy-start | bytes 786436

commit v2 on v1

v2 whole, which is shorter than its diff:
```python
import math

import jax
import jax.numpy as jnp
import numpy as np
from jax import lax
from jax.experimental import pallas as pl
from jax.experimental.pallas import tpu as pltpu
from jax.sharding import Mesh
from jax.sharding import PartitionSpec as P

NY, NZ, NX, NC = 4, 8, 4, 2
NW = NY * NZ
EMB, TABLES, RANK, UNIQ, BAG = 128, 26, 512, 512, 16
COLS = 27
XB = 7
S = 128
HALF = RANK // NC
ROWB = UNIQ // (NX * NC)
PIECE = ROWB // NY
DROWS = XB * 4
MROWS = 48
F32, BF16 = jnp.float32, jnp.bfloat16
WIDE = ("y", "z")
ALL = ("y", "z", "x", "c")
VMEM = pl.BlockSpec(memory_space=pltpu.VMEM)
SMEM = pl.BlockSpec(memory_space=pltpu.SMEM)


def rank_order():
    order = np.arange(RANK).reshape(NY, NZ, NX, NC, 2).transpose(3, 2, 1, 0, 4).reshape(-1)
    return np.eye(RANK, dtype=np.float32)[order]


def params(mib=24):
    return pltpu.CompilerParams(vmem_limit_bytes=mib * 1024 * 1024)


def cost(us):
    return pl.CostEstimate(flops=int(us * 1e9), bytes_accessed=int(us * 1e5), transcendentals=0)


def pack_kernel(x, u, ids, lengths, pair, scaled, masked):
    ds = (u[...].astype(F32) * x[...].astype(F32)).astype(BF16)
    scaled[...] = ds
    for b in range(NY):
        size = min(XB, COLS - b * XB) * EMB
        cols = slice(b * XB * EMB, b * XB * EMB + size)
        pair[b, 0, :, :size] = ds[:, cols]
        pair[b, 1, :, :size] = x[:, cols]
        if size < XB * EMB:
            pair[b, :, :, size:] = jnp.zeros((2, ds.shape[0], XB * EMB - size), BF16)

    @pl.when(pl.program_id(0) == 0)
    def _():
        position = lax.broadcasted_iota(jnp.int32, (BAG, S), 0)
        for t in range(TABLES):
            masked[t] = jnp.where(position < lengths[t : t + 1], ids[t], -1)


def pack(x, u, ids, lengths):
    steps = 4
    rows = S // steps
    wide = pl.BlockSpec((rows, x.shape[1]), lambda i: (i, 0))
    every = pl.BlockSpec((TABLES, BAG, S), lambda i: (0, 0, 0))
    return pl.pallas_call(
        pack_kernel,
        grid=(steps,),
        out_shape=(
            jax.ShapeDtypeStruct((NY, 2, S, XB * EMB), BF16),
            jax.ShapeDtypeStruct(x.shape, BF16),
            jax.ShapeDtypeStruct((TABLES, BAG, S), jnp.int32),
        ),
        in_specs=[wide, wide, every, pl.BlockSpec((TABLES, S), lambda i: (0, 0))],
        out_specs=(
            pl.BlockSpec((NY, 2, rows, XB * EMB), lambda i: (0, 0, i, 0)),
            wide,
            every,
        ),
        compiler_params=params(60),
        cost_estimate=cost(1.5),
        name="pack",
    )(x, u, ids, lengths)


def halves_kernel(core, order, low, d_low, keep, give):
    for to, at in ((keep, core[0]), (give, 1 - core[0])):
        pick = order[pl.ds(pl.multiple_of(at * HALF, HALF), HALF), :]
        to[0] = jnp.dot(pick, low[...], preferred_element_type=F32).astype(BF16)
        to[1] = jnp.dot(pick, d_low[...], preferred_element_type=F32).astype(BF16)


def rank_halves(core, low, d_low):
    part = jax.ShapeDtypeStruct((2, HALF, S), BF16)
    return pl.pallas_call(
        halves_kernel,
        out_shape=(part, part),
        in_specs=[SMEM, VMEM, VMEM, VMEM],
        out_specs=(VMEM, VMEM),
        compiler_params=params(),
        cost_estimate=cost(0.5),
        name="rank_halves",
    )(core, jnp.asarray(rank_order(), BF16), low, d_low)


def bag_kernel(place, ids_own, ids_sib, pooled_own, pooled_sib, out, stage, sems):
    mine = place[3]
    places = lax.broadcasted_iota(jnp.int32, (ROWB, 2 * S), 0)

    def table(t):
        ids = jnp.concatenate([ids_own[t], ids_sib[t]], axis=1)
        low = jnp.bitwise_and(ids, ROWB - 1)
        part = jnp.bitwise_and(lax.shift_right_arithmetic(ids, 6), 1)
        field = jnp.bitwise_and(lax.shift_right_arithmetic(ids, 7), 3)
        value = jnp.where(
            (ids >= 0) & (part == mine), lax.shift_left(jnp.ones_like(ids), field * 8), 0
        )
        packed = jnp.zeros((ROWB, 2 * S), jnp.int32)
        for j in range(BAG):
            packed = packed + jnp.where(places == low[j : j + 1], value[j : j + 1], 0)
        counts = jnp.concatenate(
            [
                jnp.bitwise_and(lax.shift_right_logical(packed, 8 * f), 255).astype(F32).astype(BF16)
                for f in range(NX)
            ],
            axis=0,
        )
        at = pl.multiple_of(t * EMB, EMB)
        grads = jnp.concatenate([pooled_own[:, pl.ds(at, EMB)], pooled_sib[:, pl.ds(at, EMB)]], axis=0)
        sums = jnp.dot(counts, grads, preferred_element_type=F32).astype(BF16)
        for k in range(NX):
            for m in range(NY):
                at = (k * NY + m) * PIECE
                stage[m * NX + k, t] = sums[at : at + PIECE]

    ends = (0, 8, 16, 22, TABLES)
    copies = []
    for i in range(4):
        pl.loop(ends[i], ends[i + 1], unroll=2)(table)
        part = pl.ds(ends[i], ends[i + 1] - ends[i])
        copies.append(pltpu.make_async_copy(stage.at[:, part], out.at[:, part], sems.at[i]))
        copies[-1].start()
    for copy in copies:
        copy.wait()


def bag_sums(place, ids_own, ids_sib, pooled_own, pooled_sib):
    return pl.pallas_call(
        bag_kernel,
        out_shape=jax.ShapeDtypeStruct((NY * NX, TABLES, PIECE, EMB), BF16),
        in_specs=[SMEM, VMEM, VMEM, VMEM, VMEM],
        out_specs=pl.BlockSpec(memory_space=pl.ANY),
        scratch_shapes=[
            pltpu.VMEM((NY * NX, TABLES, PIECE, EMB), BF16),
            pltpu.SemaphoreType.DMA((4,)),
        ],
        compiler_params=params(58),
        cost_estimate=cost(1),
        name="bag_sums",
    )(place, ids_own, ids_sib, pooled_own, pooled_sib)


def gather_side(me_y, side, lows, ref, wide_x, wide_low):
    for g in range(2):
        for k in range(NY):
            src = lax.rem(me_y - k + NY, NY)
            wide_low[g, :, k * S : (k + 1) * S] = lows[k][side, g]
            wide_x[g, k * S : (k + 1) * S] = ref[src, g]


def dense_own_kernel(place, own, low0, low1, low2, low3, out, wide_x, wide_low):
    gather_side(place[1], 0, (low0, low1, low2, low3), own, wide_x, wide_low)
    for g in range(2):
        out[g] = jnp.dot(wide_low[g], wide_x[g], preferred_element_type=F32)


def dense_both_kernel(place, first, sib, low0, low1, low2, low3, out0, out1, out2, out3, wide_x, wide_low, stage):
    gather_side(place[1], 1, (low0, low1, low2, low3), sib, wide_x, wide_low)
    both = [
        first[g] + jnp.dot(wide_low[g], wide_x[g], preferred_element_type=F32) for g in range(2)
    ]
    for j in range(XB):
        pieces = [b[:, j * EMB : (j + 1) * EMB].reshape(NX, NZ, 8, EMB) for b in both]
        stage[:, :, j * 16 : (j + 1) * 16, :] = jnp.concatenate(pieces, axis=2).astype(BF16)

    for k, out in enumerate((out0, out1, out2, out3)):
        out[...] = stage[lax.rem(place[0] + k, NX)]


WIDE_SIDE = [
    pltpu.VMEM((2, NY * S, XB * EMB), BF16),
    pltpu.VMEM((2, HALF, NY * S), BF16),
]


def dense_own(place, own, lows):
    return pl.pallas_call(
        dense_own_kernel,
        out_shape=jax.ShapeDtypeStruct((2, HALF, XB * EMB), F32),
        in_specs=[SMEM] + [VMEM] * 5,
        out_specs=VMEM,
        scratch_shapes=WIDE_SIDE,
        compiler_params=params(),
        cost_estimate=cost(20),
        name="dense_own",
    )(place, own, *lows)


def dense_both(place, first, sib, lows):
    part = jax.ShapeDtypeStruct((NZ, 16 * XB, EMB), BF16)
    return pl.pallas_call(
        dense_both_kernel,
        out_shape=(part,) * NX,
        in_specs=[SMEM] + [VMEM] * 6,
        out_specs=(VMEM,) * NX,
        scratch_shapes=WIDE_SIDE + [pltpu.VMEM((NX, NZ, 16 * XB, EMB), BF16)],
        compiler_params=params(),
        cost_estimate=cost(0),
        name="dense_both",
    )(place, first, sib, *lows)


def merge_kernel(owner, got, *refs):
    parts, out, total, dense = refs[:NX], *refs[NX:]
    total[...] = jnp.zeros_like(total)

    @pl.loop(0, TABLES)
    def _(t):
        one = got[0, t].astype(F32)
        for k in range(1, NY * NX):
            one = one + got[k, t].astype(F32)
        to = owner[t]
        total[to, :PIECE] = total[to, :PIECE] + one

    add = parts[0][...].astype(F32)
    for part in parts[1:]:
        add = add + part[...].astype(F32)
    dense[...] = add
    for y in range(NY):
        for j in range(XB):
            for g in range(2):
                at, src = PIECE + j * 4 + g * 2, j * 16 + g * 8 + y * 2
                total[y * NZ : (y + 1) * NZ, at : at + 2] = dense[:, src : src + 2]
    out[...] = total[...].astype(BF16)


def merge(owner, got, parts):
    return pl.pallas_call(
        merge_kernel,
        out_shape=jax.ShapeDtypeStruct((NW, MROWS, EMB), BF16),
        in_specs=[SMEM] + [VMEM] * (1 + NX),
        out_specs=VMEM,
        scratch_shapes=[
            pltpu.VMEM((NW, MROWS, EMB), F32),
            pltpu.VMEM((NZ, 16 * XB, EMB), F32),
        ],
        compiler_params=params(),
        cost_estimate=cost(0),
        name="merge",
    )(owner, got, *parts)


def split_kernel(got, rows, up, down, stage):
    for y in range(NY):
        one = got[y * NZ].astype(F32)
        for z in range(1, NZ):
            one = one + got[y * NZ + z].astype(F32)
        for n in range(NX * NC):
            rows[n, y * PIECE : (y + 1) * PIECE] = one[:PIECE]
        stage[y] = one[PIECE:] * (1.0 / math.sqrt(S * NW * NX * NC))
    for y in range(NY):
        for j in range(XB):
            at = (y * XB + j) * EMB
            if at < COLS * EMB:
                for g, to in enumerate((up, down)):
                    to[:, at : at + EMB] = stage[y, j * 4 + g * 2 : j * 4 + g * 2 + 2]


def split(got):
    grad = jax.ShapeDtypeStruct((2, COLS * EMB), F32)
    return pl.pallas_call(
        split_kernel,
        out_shape=(jax.ShapeDtypeStruct((NX * NC, ROWB, EMB), F32), grad, grad),
        in_specs=[VMEM],
        out_specs=(VMEM, VMEM, VMEM),
        scratch_shapes=[pltpu.VMEM((NY, MROWS - PIECE, EMB), F32)],
        compiler_params=params(),
        cost_estimate=cost(0),
        name="split",
    )(got)


def adagrad_rows(rows, accum, admitted, grad):
    begin_acc = jnp.where(admitted == 1, jnp.float32(0.1), accum)
    new_acc = begin_acc + jnp.mean(grad * grad, axis=1)
    new_values = rows - 0.5 * grad / (jnp.sqrt(new_acc)[:, None] + 1e-08)
    return (new_values, new_acc)


def local(
    cross_input,
    upstream,
    cross_down,
    cross_up,
    cross_bias,
    bag_rows,
    bag_lengths,
    table_owner,
    table_rows,
    row_accum,
    admitted,
):
    me_y, me_z, me_x, me_c = (lax.axis_index(a).astype(jnp.int32) for a in ALL)
    core, place = me_c.reshape(1), jnp.stack([me_x, me_y, me_z, me_c])

    def send(a, axis, k):
        size = lax.axis_size(axis)
        return lax.ppermute(a, axis, [(i, (i + k) % size) for i in range(size)])

    pair, d_scale, ids = pack(
        cross_input, upstream, jnp.transpose(bag_rows, (1, 2, 0)), bag_lengths.T
    )
    own = lax.all_to_all(pair, "y", split_axis=0, concat_axis=0, tiled=True)
    ids_sib = send(ids, "c", 1)

    low_t = lax.dot_general(
        cross_down, cross_input, (((1,), (1,)), ((), ())), preferred_element_type=F32
    ).astype(BF16)
    d_low_t = lax.dot_general(
        cross_up, d_scale, (((1,), (1,)), ((), ())), preferred_element_type=F32
    ).astype(BF16)
    scale_tail = lax.dot_general(
        low_t, cross_up[:, EMB:], (((0,), (0,)), ((), ())), preferred_element_type=F32
    ) + cross_bias[EMB:].astype(F32)
    tail_grad = upstream[:, EMB:].astype(F32) * (scale_tail + 1.0) + lax.dot_general(
        d_low_t, cross_down[:, EMB:], (((0,), (0,)), ((), ())), preferred_element_type=F32
    )
    pooled = tail_grad.astype(BF16)
    pooled_sib = send(pooled, "c", 1)

    keep, give = rank_halves(core, low_t, d_low_t)
    low0 = jnp.stack([keep, send(give, "c", 1)])
    low0, pooled_sib = lax.optimization_barrier((low0, pooled_sib))
    lows = [low0] + [send(low0, "y", k) for k in range(1, NY)]

    sums = bag_sums(place, ids, ids_sib, pooled, pooled_sib)
    own, sums = lax.optimization_barrier((own, sums))
    sib = send(own, "c", 1)
    got = lax.all_to_all(sums, ("y", "x"), split_axis=0, concat_axis=0, tiled=True)
    parts = dense_both(place, dense_own(place, own, lows), sib, lows)
    parts = [parts[0]] + [send(parts[k], "x", k) for k in range(1, NX)]
    merged = merge(table_owner, got, parts)
    merged = lax.all_to_all(merged, WIDE, split_axis=0, concat_axis=0, tiled=True)
    rows, grad_up, grad_down = split(merged)
    rows = lax.all_to_all(rows, ("x", "c"), split_axis=0, concat_axis=0, tiled=True)
    new_rows, new_accum = adagrad_rows(
        table_rows, row_accum, admitted, rows.reshape(UNIQ, EMB)
    )
    return (new_rows, new_accum, grad_up, grad_down)


def solution(mesh):
    inner = Mesh(mesh.devices.reshape(NY, NZ, NX, NC), ALL)
    return jax.shard_map(
        local,
        mesh=inner,
        in_specs=(
            P(ALL, None),
            P(ALL, None),
            P(),
            P(),
            P(),
            P(ALL, None, None),
            P(ALL, None),
            P(),
            P(WIDE, None),
            P(WIDE),
            P(WIDE),
        ),
        out_specs=(
            P(WIDE, None),
            P(WIDE),
            P(ALL, None),
            P(ALL, None),
        ),
        check_vma=False,
    )
```

time: 158 us -> 115 us (0.73)
  blocking collectives: 59.4 us -> 39 us
  waiting for transfers between devices: 34.9 us -> 19.8 us
  local copies, waits for them, and re-layouts: 13.3 us -> 2.29 us
  starting transfers between devices: 18.8 us -> 24 us
  Pallas kernels: 15.8 us -> 19.6 us
  matrix products: 8.4 us -> 5.84 us
  other arithmetic: 5.39 us -> 2.92 us
    all_to_all x1, blocking collectives: 45.1 us -> 21.2 us  [local(): lax.all_to_all(merged, WIDE, split_axis=0, concat_axis=0, tiled=True)]
    all_to_all x2, waiting for transfers between devices: 19.9 us -> 9.28 us  [the longest x1 9.28 us: local(): lax.all_to_all(sums, ('y', 'x'), split_axis=0, concat_axis=0, tiled=True)]
    reshape x5 -> x0, local copies, waits for them, and re-layouts: 5.78 us -> none  [the longest x2 3.53 us: local(): halves = jnp.transpose(halves.reshape(NC, HALF, 2, S), (0, 2, 1, 3))]
    ppermute x7 -> x10, waiting for transfers between devices: 15 us -> 10.5 us  [send(): return lax.ppermute(a, axis, [(i, (i + k) % size) for i in range(size)])]
    pallas_call x3 -> x7, Pallas kernels: 15.8 us -> 19.6 us  [the longest x1 8.86 us: bag_sums(): pl.pallas_call(bag_kernel, out_shape=jax.ShapeDtypeStruct((NY * NX, TABLE...]
    ppermute x7 -> x10, starting transfers between devices: 10.4 us -> 13.9 us  [send(): return lax.ppermute(a, axis, [(i, (i + k) % size) for i in range(size)])]
    all_to_all x1, blocking collectives: 14.3 us -> 17.8 us  [local(): lax.all_to_all(rows, ('x', 'c'), split_axis=0, concat_axis=0, tiled=True)]
    unnamed x30 -> x26, local copies, waits for them, and re-layouts: 5.63 us -> 2.22 us
  transfers between devices with their start and end apart: 9 -> 12, of which waited for: 6 -> 5; matrix products, arithmetic and copies ran while one was open for 9% -> 6% of each run, Pallas kernels for 6% -> 12%
where the time goes in v2:
time: 115 us; the launch traced here: 114 us
  blocking collectives  39 us (34%)
  starting transfers between devices  24 us (21%)
  waiting for transfers between devices  19.8 us (17%)
  Pallas kernels  19.6 us (17%)
  matrix products  5.84 us (5%)
  other arithmetic  2.92 us (3%)
  local copies, waits for them, and re-layouts  2.29 us (2%)
    all_to_all x1, blocking collectives, local(): lax.all_to_all(merged, WIDE, split_axis=0, concat_axis=0, tiled=True)  21.2 us
    all_to_all x1, blocking collectives, local(): lax.all_to_all(rows, ('x', 'c'), split_axis=0, concat_axis=0, tiled=True)  17.8 us
    ppermute x10, starting transfers between devices, send(): return lax.ppermute(a, axis, [(i, (i + k) % size) for i in range(size)])  13.9 us
    ppermute x10, waiting for transfers between devices, send(): return lax.ppermute(a, axis, [(i, (i + k) % size) for i in range(size)])  10.5 us
    all_to_all x1, waiting for transfers between devices, local(): lax.all_to_all(sums, ('y', 'x'), split_axis=0, concat_axis=0, tiled=True)  9.28 us
    pallas_call x1, Pallas kernels, bag_sums(): pl.pallas_call(bag_kernel, out_shape=jax.ShapeDtypeStruct((NY * NX, TABLE...  8.86 us
    all_to_all x1, starting transfers between devices, local(): lax.all_to_all(sums, ('y', 'x'), split_axis=0, concat_axis=0, tiled=True)  5.12 us
    all_to_all x1, starting transfers between devices, local(): own = lax.all_to_all(pair, 'y', split_axis=0, concat_axis=0, tiled=True)  5.02 us
  transfers between devices with their start and end apart: 12, of which 5 were waited for; matrix products, arithmetic and copies ran while one was open for 6% of the time, Pallas kernels for 12%

profile of v2, /device:TPU:1, one launch (start us, length us, event | category | flops | bytes accessed | tf_op | source)
XLA Modules:
  0.0 114.3 jit_solution(12996978168495094019)
XLA Ops:
  0.6 4.3 %pack.1 = (bf16[4,2,128,896]{3,2,1,0:T(8,128)(2,1)}, bf16[128,3456]{1,0:T(8,128)(2,1)}, s32[26,16,128]{2,1,0:T(8,128)}) custom-call(bf16[128,3456]{1,0:T(8,128)(2,1)} %x.1, bf16[128,3456]{1,0:T(8,128)(2,1)} %u.1, s32[26,16,128]{2,1,0:T(8,128)} %bitcast.22, s32[26,128]{1,0:T(8,128)} %bitcast.23), custom_call_target="tpu_custom_call" | custom-call | flops 1500000000 | bytes 150000 | tf_op jit(solution)/shard_map/pack/pallas_call | solution.py:66
  4.9 0.0 copy-start.10
  4.9 5.0 %all-to-all-start = ((bf16[4,2,128,896]{3,2,1,0:T(8,128)(2,1)}), bf16[4,2,128,896]{3,2,1,0:T(8,128)(2,1)S(1)}, u32[]{:S(2)}, u32[]{:S(2)}) async-start(bf16[4,2,128,896]{3,2,1,0:T(8,128)(2,1)} %get-tuple-element.20), calls=%async_computation | async-start | bytes 3670016 | tf_op jit(solution)/shard_map/all_to_all | solution.py:323
  9.9 0.0 copy-done.10
  9.9 0.0 copy-start.3
  9.9 0.0 copy-start.6
  10.0 3.5 %convolution_convert_fusion.1.low = bf16[512,128]{1,0:T(8,128)(2,1)S(1)} fusion(bf16[512,3456]{1,0:T(8,128)(2,1)} %param.14, bf16[128,3456]{1,0:T(8,128)(2,1)} %x.1), kind=kOutput, calls=%fused_computation.8 | convolution fusion | flops 453050368 | bytes 4554752 | tf_op jit(solution)/shard_map/dot_general | solution.py:326
  13.4 0.0 copy-done.3
  13.4 0.1 copy-done.6
  13.5 1.1 convolution_convert_fusion
  14.6 0.1 copy-done.7
  14.7 0.7 fusion.1
  15.3 1.3 %copy-done.5 = bf16[512,3456]{1,0:T(8,128)(2,1)S(1)} copy-done((bf16[512,3456]{1,0:T(8,128)(2,1)S(1)}, bf16[512,3456]{1,0:T(8,128)(2,1)}, u32[]{:S(2)}) %copy-start.5) | copy-done | bytes 3538968
  16.7 0.6 fusion.2.pooled_own
  17.3 0.0 copy-start.4
  17.3 1.9 %collective-permute-start.2 = (bf16[128,3328]{1,0:T(8,128)(2,1)S(1)}, bf16[128,3328]{1,0:T(8,128)(2,1)}, u32[]{:S(2)}, u32[]{:S(2)}) collective-permute-start(bf16[128,3328]{1,0:T(8,128)(2,1)S(1)} %fusion.2.pooled_own), channel_id=1, source_target_pairs={{0,1},{1,0},{2,3},{3,2},{4,5},{5,4},{6,7},{7,6},{8,9},{9,8},{10,11... | collective-permute-start | bytes 2555912 | tf_op jit(solution)/shard_map/ppermute | solution.py:318
  19.3 0.0 copy-done.2
  19.3 0.4 rank_halves.1
  19.7 0.4 collective-permute-start.1
  20.1 0.2 collective-permute-start
  20.3 1.4 %collective-permute-done.1 = bf16[2,256,128]{2,1,0:T(8,128)(2,1)S(1)} collective-permute-done((bf16[2,256,128]{2,1,0:T(8,128)(2,1)S(1)}, bf16[2,256,128]{2,1,0:T(8,128)(2,1)S(1)}, u32[]{:S(2)}, u32[]{:S(2)}) %collective-permute-start.1) | collective-permute-done | bytes 131104 | tf_op jit(solution)/shard_map/ppermute | solution.py:318
  21.6 0.7 pad_maximum_fusion.low0
  22.4 0.0 collective-permute-done.2.pooled_sib
  22.4 2.9 %collective-permute-start.5 = (bf16[2,2,256,128]{3,2,1,0:T(8,128)(2,1)}, bf16[2,2,256,128]{3,2,1,0:T(8,128)(2,1)}, u32[]{:S(2)}, u32[]{:S(2)}) collective-permute-start(bf16[2,2,256,128]{3,2,1,0:T(8,128)(2,1)} %pad_maximum_fusion.low0), channel_id=1, source_target_pairs={{0,192},{64,0},{128,64},{192,128},{1,193},{65,1},{129,65},{193,129... | collective-permute-start | bytes 786440 | tf_op jit(solution)/shard_map/ppermute | solution.py:318
  25.3 0.6 collective-permute-start.4
  25.8 0.6 collective-permute-start.3
  26.4 0.6 pad_add_fusion.place
  27.0 0.0 collective-permute-done.ids_sib
  27.0 0.0 copy-done.4
  27.0 0.7 copy-done.9
  27.7 8.9 %bag_sums.1 = bf16[16,26,16,128]{3,2,1,0:T(8,128)(2,1)} custom-call(s32[4]{0:T(128)} %pad_add_fusion.place, s32[26,16,128]{2,1,0:T(8,128)} %get-tuple-element.21.ids_own, s32[26,16,128]{2,1,0:T(8,128)} %copy-done.9, bf16[128,3328]{1,0:T(8,128)(2,1)} %copy-done.4, bf16[128,3328]{1,0:T(8,128)(2,1)} %collective-permute-done.2.pooled_sib), custom_call_target="tpu_custom_call" | custom-call | flops 1000000000 | bytes 100000 | tf_op jit(solution)/shard_map/bag_sums/pallas_call | solution.py:148
  36.6 0.0 copy-start
  36.6 0.0 all-to-all-done.own
  36.6 5.1 %all-to-all-start.1 = ((bf16[16,26,16,128]{3,2,1,0:T(8,128)(2,1)}), bf16[16,26,16,128]{3,2,1,0:T(8,128)(2,1)S(1)}, u32[]{:S(2)}, u32[]{:S(2)}) async-start(bf16[16,26,16,128]{3,2,1,0:T(8,128)(2,1)} %bag_sums.1), calls=%async_computation.1 | async-start | bytes 3407872 | tf_op jit(solution)/shard_map/all_to_all | solution.py:349
  41.7 2.1 %collective-permute-start.6 = (bf16[4,2,128,896]{3,2,1,0:T(8,128)(2,1)S(1)}, bf16[4,2,128,896]{3,2,1,0:T(8,128)(2,1)S(1)}, u32[]{:S(2)}, u32[]{:S(2)}) collective-permute-start(bf16[4,2,128,896]{3,2,1,0:T(8,128)(2,1)S(1)} %all-to-all-done.own), channel_id=1, source_target_pairs={{0,1},{1,0},{2,3},{3,2},{4,5},{5,4},{6,7},{7,6},{8,9},{9,8},{10,11... | collective-permute-start | bytes 5505032 | tf_op jit(solution)/shard_map/ppermute | solution.py:318
  43.8 0.0 collective-permute-done.5.low3
  43.8 0.0 collective-permute-done.4.low2
  43.8 1.4 %collective-permute-done.3.low1 = bf16[2,2,256,128]{3,2,1,0:T(8,128)(2,1)} collective-permute-done((bf16[2,2,256,128]{3,2,1,0:T(8,128)(2,1)}, bf16[2,2,256,128]{3,2,1,0:T(8,128)(2,1)}, u32[]{:S(2)}, u32[]{:S(2)}) %collective-permute-start.3) | collective-permute-done | bytes 262176 | tf_op jit(solution)/shard_map/ppermute | solution.py:318
  45.2 0.0 copy-done
  45.3 1.9 %dense_own.1.first = f32[2,256,896]{2,1,0:T(8,128)S(1)} custom-call(s32[4]{0:T(128)S(1)} %copy-done, bf16[4,2,128,896]{3,2,1,0:T(8,128)(2,1)S(1)} %all-to-all-done.own, bf16[2,2,256,128]{3,2,1,0:T(8,128)(2,1)} %pad_maximum_fusion.low0, bf16[2,2,256,128]{3,2,1,0:T(8,128)(2,1)} %collective-permute-done.3.low1, ...), custom_call_target="tpu_custom_call" | custom-call | flops 20000000000 | bytes 2000000 | tf_op jit(solution)/shard_map/dense_own/pallas_call | solution.py:197
  47.2 0.0 copy-start.1
  47.2 0.0 collective-permute-done.6.sib
  47.2 2.0 %dense_both.1 = (bf16[8,112,128]{2,1,0:T(8,128)(2,1)S(1)}, bf16[8,112,128]{2,1,0:T(8,128)(2,1)S(1)}, bf16[8,112,128]{2,1,0:T(8,128)(2,1)S(1)}, bf16[8,112,128]{2,1,0:T(8,128)(2,1)S(1)}) custom-call(s32[4]{0:T(128)S(1)} %copy-done, f32[2,256,896]{2,1,0:T(8,128)S(1)} %dense_own.1.first, bf16[4,2,128,896]{3,2,1,0:T(8,128)(2,1)S(1)} %collective-permute-done.6.sib, ...), custom_call_target="tpu_custom_call" | custom-call | tf_op jit(solution)/shard_map/dense_both/pallas_call | solution.py:211
  49.3 1.6 %collective-permute-start.7 = (bf16[8,112,128]{2,1,0:T(8,128)(2,1)S(1)}, bf16[8,112,128]{2,1,0:T(8,128)(2,1)S(1)}, u32[]{:S(2)}, u32[]{:S(2)}) collective-permute-start(bf16[8,112,128]{2,1,0:T(8,128)(2,1)S(1)} %get-tuple-element.30), channel_id=1, source_target_pairs={{0,2},{2,4},{4,6},{6,0},{1,3},{3,5},{5,7},{7,1},{8,10},{10,12},{12... | collective-permute-start | bytes 688136 | tf_op jit(solution)/shard_map/ppermute | solution.py:318
  50.9 2.4 %collective-permute-start.8 = (bf16[8,112,128]{2,1,0:T(8,128)(2,1)S(1)}, bf16[8,112,128]{2,1,0:T(8,128)(2,1)S(1)}, u32[]{:S(2)}, u32[]{:S(2)}) collective-permute-start(bf16[8,112,128]{2,1,0:T(8,128)(2,1)S(1)} %get-tuple-element.31), channel_id=1, source_target_pairs={{0,4},{2,6},{4,0},{6,2},{1,5},{3,7},{5,1},{7,3},{8,12},{10,14},{12... | collective-permute-start | bytes 688136 | tf_op jit(solution)/shard_map/ppermute | solution.py:318
  53.3 1.2 %collective-permute-start.9 = (bf16[8,112,128]{2,1,0:T(8,128)(2,1)S(1)}, bf16[8,112,128]{2,1,0:T(8,128)(2,1)S(1)}, u32[]{:S(2)}, u32[]{:S(2)}) collective-permute-start(bf16[8,112,128]{2,1,0:T(8,128)(2,1)S(1)} %get-tuple-element.32), channel_id=1, source_target_pairs={{0,6},{2,0},{4,2},{6,4},{1,7},{3,1},{5,3},{7,5},{8,14},{10,8},{12,... | collective-permute-start | bytes 688136 | tf_op jit(solution)/shard_map/ppermute | solution.py:318
  54.5 9.3 %all-to-all-done.1.got = bf16[16,26,16,128]{3,2,1,0:T(8,128)(2,1)S(1)} async-done(((bf16[16,26,16,128]{3,2,1,0:T(8,128)(2,1)}), bf16[16,26,16,128]{3,2,1,0:T(8,128)(2,1)S(1)}, u32[]{:S(2)}, u32[]{:S(2)}) %all-to-all-start.1) | async-done | bytes 1703968 | tf_op jit(solution)/shard_map/all_to_all | solution.py:349
  63.8 6.4 %collective-permute-done.7.refs_1_ = bf16[8,112,128]{2,1,0:T(8,128)(2,1)S(1)} collective-permute-done((bf16[8,112,128]{2,1,0:T(8,128)(2,1)S(1)}, bf16[8,112,128]{2,1,0:T(8,128)(2,1)S(1)}, u32[]{:S(2)}, u32[]{:S(2)}) %collective-permute-start.7) | collective-permute-done | bytes 229408 | tf_op jit(solution)/shard_map/ppermute | solution.py:318
  70.2 1.2 %collective-permute-done.8.refs_2_ = bf16[8,112,128]{2,1,0:T(8,128)(2,1)S(1)} collective-permute-done((bf16[8,112,128]{2,1,0:T(8,128)(2,1)S(1)}, bf16[8,112,128]{2,1,0:T(8,128)(2,1)S(1)}, u32[]{:S(2)}, u32[]{:S(2)}) %collective-permute-start.8) | collective-permute-done | bytes 229408 | tf_op jit(solution)/shard_map/ppermute | solution.py:318
  71.4 0.0 collective-permute-done.9.refs_3_
  71.4 0.0 copy-done.1
  71.4 1.5 %merge.1 = bf16[32,48,128]{2,1,0:T(8,128)(2,1)S(1)} custom-call(s32[26]{0:T(128)S(1)} %copy-done.1, bf16[16,26,16,128]{3,2,1,0:T(8,128)(2,1)S(1)} %all-to-all-done.1.got, bf16[8,112,128]{2,1,0:T(8,128)(2,1)S(1)} %get-tuple-element.29.refs_0_, bf16[8,112,128]{2,1,0:T(8,128)(2,1)S(1)} %collective-permute-done.7.refs_1_, ...), custom_call_target="tpu_custom_call" | custom-call | tf_op jit(solution)/shard_map/merge/pallas_call | solution.py:248
  72.9 0.0 copy-start.11
  72.9 0.0 copy-start.12
  72.9 0.0 copy-start.8
  72.9 21.2 %all_to_all.20.got = bf16[32,48,128]{2,1,0:T(8,128)(2,1)S(1)} all-to-all(bf16[32,48,128]{2,1,0:T(8,128)(2,1)S(1)} %merge.1), channel_id=1, replica_groups=mesh['y'=4,'z'=8,'x'=4,'c'=2] {'y','z'}, dimensions={0} | all-to-all | bytes 786432 | tf_op jit(solution)/shard_map/all_to_all | solution.py:353
  94.1 0.7 split.1
  94.8 17.8 %all_to_all.21 = f32[8,64,128]{2,1,0:T(8,128)S(1)} all-to-all(f32[8,64,128]{2,1,0:T(8,128)S(1)} %get-tuple-element.33), channel_id=1, replica_groups=mesh['y'=4,'z'=8,'x'=4,'c'=2] {'x','c'}, dimensions={0} | all-to-all | bytes 524288 | tf_op jit(solution)/shard_map/all_to_all | solution.py:355
  112.7 0.1 multiply_reduce_fusion
  112.8 0.1 div.18
  112.9 0.0 copy-done.11
  112.9 0.0 copy-done.12
  112.9 0.6 sqrt_add_fusion
  113.5 0.8 fusion.5
  (7 shorter events, 0.0 us)
Async XLA Ops:
  4.9 5.0 %copy-start.10 = (bf16[3456]{0:T(1024)(128)(2,1)S(1)}, bf16[3456]{0:T(1024)(128)(2,1)}, u32[]{:S(2)}) copy-start(bf16[3456]{0:T(1024)(128)(2,1)} %param.16) | copy-start | bytes 20740
  4.9 31.7 %all-to-all-start = ((bf16[4,2,128,896]{3,2,1,0:T(8,128)(2,1)}), bf16[4,2,128,896]{3,2,1,0:T(8,128)(2,1)S(1)}, u32[]{:S(2)}, u32[]{:S(2)}) async-start(bf16[4,2,128,896]{3,2,1,0:T(8,128)(2,1)} %get-tuple-element.20), calls=%async_computation | async-start | bytes 3670016 | tf_op jit(solution)/shard_map/all_to_all | solution.py:323
  9.9 3.5 %copy-start.3 = (bf16[512,3456]{1,0:T(8,128)(2,1)S(1)}, bf16[512,3456]{1,0:T(8,128)(2,1)}, u32[]{:S(2)}) copy-start(bf16[512,3456]{1,0:T(8,128)(2,1)} %param.15) | copy-start | bytes 10616836
  9.9 3.6 %copy-start.6 = (bf16[128,3456]{1,0:T(8,128)(2,1)S(1)}, bf16[128,3456]{1,0:T(8,128)(2,1)}, u32[]{:S(2)}) copy-start(bf16[128,3456]{1,0:T(8,128)(2,1)} %get-tuple-element.22) | copy-start | bytes 2654212
  13.5 1.2 %copy-start.7 = (bf16[128,3456]{1,0:T(8,128)(2,1)S(1)}, bf16[128,3456]{1,0:T(8,128)(2,1)}, u32[]{:S(2)}) copy-start(bf16[128,3456]{1,0:T(8,128)(2,1)} %u.1) | copy-start | bytes 2654212
  14.7 2.0 %copy-start.5 = (bf16[512,3456]{1,0:T(8,128)(2,1)S(1)}, bf16[512,3456]{1,0:T(8,128)(2,1)}, u32[]{:S(2)}) copy-start(bf16[512,3456]{1,0:T(8,128)(2,1)} %param.14) | copy-start | bytes 10616836
  16.7 2.6 %copy-start.2 = (bf16[512,512]{1,0:T(8,128)(2,1)S(1)}, bf16[512,512]{1,0:T(8,128)(2,1)}, u32[]{:S(2)}) copy-start(bf16[512,512]{1,0:T(8,128)(2,1)} %constant.33.clone.order) | copy-start | bytes 1572868
  17.3 9.7 %copy-start.4 = (bf16[128,3328]{1,0:T(8,128)(2,1)}, bf16[128,3328]{1,0:T(8,128)(2,1)S(1)}, u32[]{:S(2)}) copy-start(bf16[128,3328]{1,0:T(8,128)(2,1)S(1)} %fusion.2.pooled_own) | copy-start | bytes 2555908
  17.3 5.0 %collective-permute-start.2 = (bf16[128,3328]{1,0:T(8,128)(2,1)S(1)}, bf16[128,3328]{1,0:T(8,128)(2,1)}, u32[]{:S(2)}, u32[]{:S(2)}) collective-permute-start(bf16[128,3328]{1,0:T(8,128)(2,1)S(1)} %fusion.2.pooled_own), channel_id=1, source_target_pairs={{0,1},{1,0},{2,3},{3,2},{4,5},{5,4},{6,7},{7,6},{8,9},{9,8},{10,11... | collective-permute-start | bytes 2555912 | tf_op jit(solution)/shard_map/ppermute | solution.py:318
  19.7 2.0 %collective-permute-start.1 = (bf16[2,256,128]{2,1,0:T(8,128)(2,1)S(1)}, bf16[2,256,128]{2,1,0:T(8,128)(2,1)S(1)}, u32[]{:S(2)}, u32[]{:S(2)}) collective-permute-start(bf16[2,256,128]{2,1,0:T(8,128)(2,1)S(1)} %get-tuple-element.24), channel_id=1, source_target_pairs={{0,1},{1,0},{2,3},{3,2},{4,5},{5,4},{6,7},{7,6},{8,9},{9,8},{10,11... | collective-permute-start | bytes 393224 | tf_op jit(solution)/shard_map/ppermute | solution.py:318
  20.1 7.0 %collective-permute-start = (s32[26,16,128]{2,1,0:T(8,128)}, s32[26,16,128]{2,1,0:T(8,128)S(1)}, u32[]{:S(2)}, u32[]{:S(2)}) collective-permute-start(s32[26,16,128]{2,1,0:T(8,128)} %get-tuple-element.21.ids_own), channel_id=1, source_target_pairs={{0,1},{1,0},{2,3},{3,2},{4,5},{5,4},{6,7},{7,6},{8,9},{9,8},{10,11... | collective-permute-start | bytes 638984 | tf_op jit(solution)/shard_map/ppermute | solution.py:318
  22.4 21.5 %collective-permute-start.5 = (bf16[2,2,256,128]{3,2,1,0:T(8,128)(2,1)}, bf16[2,2,256,128]{3,2,1,0:T(8,128)(2,1)}, u32[]{:S(2)}, u32[]{:S(2)}) collective-permute-start(bf16[2,2,256,128]{3,2,1,0:T(8,128)(2,1)} %pad_maximum_fusion.low0), channel_id=1, source_target_pairs={{0,192},{64,0},{128,64},{192,128},{1,193},{65,1},{129,65},{193,129... | collective-permute-start | bytes 786440 | tf_op jit(solution)/shard_map/ppermute | solution.py:318
  25.3 18.6 %collective-permute-start.4 = (bf16[2,2,256,128]{3,2,1,0:T(8,128)(2,1)}, bf16[2,2,256,128]{3,2,1,0:T(8,128)(2,1)}, u32[]{:S(2)}, u32[]{:S(2)}) collective-permute-start(bf16[2,2,256,128]{3,2,1,0:T(8,128)(2,1)} %pad_maximum_fusion.low0), channel_id=1, source_target_pairs={{0,128},{64,192},{128,0},{192,64},{1,129},{65,193},{129,1},{193,65... | collective-permute-start | bytes 786440 | tf_op jit(solution)/shard_map/ppermute | solution.py:318
  25.8 19.4 %collective-permute-start.3 = (bf16[2,2,256,128]{3,2,1,0:T(8,128)(2,1)}, bf16[2,2,256,128]{3,2,1,0:T(8,128)(2,1)}, u32[]{:S(2)}, u32[]{:S(2)}) collective-permute-start(bf16[2,2,256,128]{3,2,1,0:T(8,128)(2,1)} %pad_maximum_fusion.low0), channel_id=1, source_target_pairs={{0,64},{64,128},{128,192},{192,0},{1,65},{65,129},{129,193},{193,1... | collective-permute-start | bytes 786440 | tf_op jit(solution)/shard_map/ppermute | solution.py:318
  27.0 0.7 copy-start.9
  36.6 8.7 %copy-start = (s32[4]{0:T(128)S(1)}, s32[4]{0:T(128)}, u32[]{:S(2)}) copy-start(s32[4]{0:T(128)} %pad_add_fusion.place) | copy-start | bytes 52
  36.6 27.1 %all-to-all-start.1 = ((bf16[16,26,16,128]{3,2,1,0:T(8,128)(2,1)}), bf16[16,26,16,128]{3,2,1,0:T(8,128)(2,1)S(1)}, u32[]{:S(2)}, u32[]{:S(2)}) async-start(bf16[16,26,16,128]{3,2,1,0:T(8,128)(2,1)} %bag_sums.1), calls=%async_computation.1 | async-start | bytes 3407872 | tf_op jit(solution)/shard_map/all_to_all | solution.py:349
  41.7 5.5 %collective-permute-start.6 = (bf16[4,2,128,896]{3,2,1,0:T(8,128)(2,1)S(1)}, bf16[4,2,128,896]{3,2,1,0:T(8,128)(2,1)S(1)}, u32[]{:S(2)}, u32[]{:S(2)}) collective-permute-start(bf16[4,2,128,896]{3,2,1,0:T(8,128)(2,1)S(1)} %all-to-all-done.own), channel_id=1, source_target_pairs={{0,1},{1,0},{2,3},{3,2},{4,5},{5,4},{6,7},{7,6},{8,9},{9,8},{10,11... | collective-permute-start | bytes 5505032 | tf_op jit(solution)/shard_map/ppermute | solution.py:318
  47.2 24.2 %copy-start.1 = (s32[26]{0:T(128)S(1)}, s32[26]{0:T(128)}, u32[]{:S(2)}) copy-start(s32[26]{0:T(128)} %owner.1) | copy-start | bytes 316
  49.3 20.9 %collective-permute-start.7 = (bf16[8,112,128]{2,1,0:T(8,128)(2,1)S(1)}, bf16[8,112,128]{2,1,0:T(8,128)(2,1)S(1)}, u32[]{:S(2)}, u32[]{:S(2)}) collective-permute-start(bf16[8,112,128]{2,1,0:T(8,128)(2,1)S(1)} %get-tuple-element.30), channel_id=1, source_target_pairs={{0,2},{2,4},{4,6},{6,0},{1,3},{3,5},{5,7},{7,1},{8,10},{10,12},{12... | collective-permute-start | bytes 688136 | tf_op jit(solution)/shard_map/ppermute | solution.py:318
  50.9 20.5 %collective-permute-start.8 = (bf16[8,112,128]{2,1,0:T(8,128)(2,1)S(1)}, bf16[8,112,128]{2,1,0:T(8,128)(2,1)S(1)}, u32[]{:S(2)}, u32[]{:S(2)}) collective-permute-start(bf16[8,112,128]{2,1,0:T(8,128)(2,1)S(1)} %get-tuple-element.31), channel_id=1, source_target_pairs={{0,4},{2,6},{4,0},{6,2},{1,5},{3,7},{5,1},{7,3},{8,12},{10,14},{12... | collective-permute-start | bytes 688136 | tf_op jit(solution)/shard_map/ppermute | solution.py:318
  53.3 18.1 %collective-permute-start.9 = (bf16[8,112,128]{2,1,0:T(8,128)(2,1)S(1)}, bf16[8,112,128]{2,1,0:T(8,128)(2,1)S(1)}, u32[]{:S(2)}, u32[]{:S(2)}) collective-permute-start(bf16[8,112,128]{2,1,0:T(8,128)(2,1)S(1)} %get-tuple-element.32), channel_id=1, source_target_pairs={{0,6},{2,0},{4,2},{6,4},{1,7},{3,1},{5,3},{7,5},{8,14},{10,8},{12,... | collective-permute-start | bytes 688136 | tf_op jit(solution)/shard_map/ppermute | solution.py:318
  72.9 40.0 %copy-start.11 = (f32[512]{0:T(512)S(1)}, f32[512]{0:T(512)}, u32[]{:S(2)}) copy-start(f32[512]{0:T(512)} %param.21) | copy-start | bytes 6148
  72.9 40.0 %copy-start.12 = (s32[512]{0:T(512)S(1)}, s32[512]{0:T(512)}, u32[]{:S(2)}) copy-start(s32[512]{0:T(512)} %param.22) | copy-start | bytes 6148
  72.9 40.6 %copy-start.8 = (f32[512,128]{1,0:T(8,128)S(1)}, f32[512,128]{1,0:T(8,128)}, u32[]{:S(2)}) copy-start(f32[512,128]{1,0:T(8,128)} %param.20) | copy-start | bytes 786436

commit v3 on v2

v3 whole, which is shorter than its diff:
```python
import math

import jax
import jax.numpy as jnp
import numpy as np
from jax import lax
from jax.experimental import pallas as pl
from jax.experimental.pallas import tpu as pltpu
from jax.sharding import Mesh
from jax.sharding import PartitionSpec as P

NY, NZ, NX, NC = 4, 8, 4, 2
NW = NY * NZ
EMB, TABLES, RANK, UNIQ, BAG = 128, 26, 512, 512, 16
COLS = 27
XB = 7
S = 128
HALF = RANK // NC
ROWB = UNIQ // (NX * NC)
PIECE = ROWB // NY
DROWS = XB * 4
MROWS = 48
TX = 7
NONE = 256.0
F32, BF16 = jnp.float32, jnp.bfloat16
WIDE = ("y", "z")
ALL = ("y", "z", "x", "c")
VMEM = pl.BlockSpec(memory_space=pltpu.VMEM)
SMEM = pl.BlockSpec(memory_space=pltpu.SMEM)


def rank_order():
    order = np.arange(RANK).reshape(NW, NX, NC, 2).transpose(2, 1, 3, 0).reshape(-1)
    return np.eye(RANK, dtype=np.float32)[order]


def params(mib=24):
    return pltpu.CompilerParams(vmem_limit_bytes=mib * 1024 * 1024)


def cost(us):
    return pl.CostEstimate(flops=int(us * 1e9), bytes_accessed=int(us * 1e5), transcendentals=0)


def axis(name):
    return lax.axis_index(name).astype(jnp.int32)


def pack_kernel(x, u, ids, lengths, pair, coded):
    ds = (u[...].astype(F32) * x[...].astype(F32)).astype(BF16)
    for b in range(NY):
        size = min(XB, COLS - b * XB) * EMB
        cols = slice(b * XB * EMB, b * XB * EMB + size)
        pair[b, 0, :, :size] = ds[:, cols]
        pair[b, 1, :, :size] = x[:, cols]
        if size < XB * EMB:
            pair[b, :, :, size:] = jnp.zeros((2, ds.shape[0], XB * EMB - size), BF16)

    @pl.when(pl.program_id(0) == 0)
    def _():
        position = lax.broadcasted_iota(jnp.int32, (BAG, S), 0)
        for t in range(TABLES):
            code = jnp.where(position < lengths[t : t + 1], (ids[t] - 256).astype(F32), NONE)
            coded[t] = code.astype(BF16)


def pack(x, u, ids, lengths):
    steps = 4
    rows = S // steps
    wide = pl.BlockSpec((rows, x.shape[1]), lambda i: (i, 0))
    every = pl.BlockSpec((TABLES, BAG, S), lambda i: (0, 0, 0))
    return pl.pallas_call(
        pack_kernel,
        grid=(steps,),
        out_shape=(
            jax.ShapeDtypeStruct((NY, 2, S, XB * EMB), BF16),
            jax.ShapeDtypeStruct((TABLES, BAG, S), BF16),
        ),
        in_specs=[wide, wide, every, pl.BlockSpec((TABLES, S), lambda i: (0, 0))],
        out_specs=(
            pl.BlockSpec((NY, 2, rows, XB * EMB), lambda i: (0, 0, i, 0)),
            every,
        ),
        compiler_params=params(60),
        cost_estimate=cost(1.5),
        name="pack",
    )(x, u, ids, lengths)


def cross_kernel(
    x_in, u_in, down_in, up_in, bias, order, coded, keep, give, out0, out1, out2, out3, x, u, down, up, pooled, sems
):
    spans = [(at, min(at + XB * EMB, COLS * EMB)) for at in range(0, COLS * EMB, XB * EMB)]
    first = [pltpu.make_async_copy(x_in, x, sems.at[0]), pltpu.make_async_copy(u_in, u, sems.at[1])]
    loads = []
    for w, (src, to) in enumerate(((down_in, down), (up_in, up))):
        loads.append([])
        for i, (begin, end) in enumerate(spans):
            at = pl.ds(begin, end - begin)
            loads[w].append(
                pltpu.make_async_copy(src.at[:, at], to.at[:, at], sems.at[2 + w * NY + i])
            )
    for copy in first[:1] + loads[0] + first[1:] + loads[1]:
        copy.start()

    def low_of(weight, copies, piece):
        total = jnp.zeros((RANK, S), F32)
        for copy, (begin, end) in zip(copies, spans):
            copy.wait()
            total = total + lax.dot_general(
                weight[:, begin:end], piece(begin, end), (((1,), (1,)), ((), ())), preferred_element_type=F32
            )
        return total.astype(BF16)

    first[0].wait()
    low = low_of(down, loads[0], lambda begin, end: x[:, begin:end])
    first[1].wait()
    d_low = low_of(
        up,
        loads[1],
        lambda begin, end: (u[:, begin:end].astype(F32) * x[:, begin:end].astype(F32)).astype(BF16),
    )
    for to, at in ((keep, axis("c")), (give, 1 - axis("c"))):
        pick = order[pl.ds(pl.multiple_of(at * HALF, HALF), HALF), :]
        for g, one in enumerate((low, d_low)):
            to[g] = jnp.dot(pick, one, preferred_element_type=F32).astype(BF16)
    low, d_low = low.T, d_low.T
    size = 2 * 256
    for at in range(EMB, COLS * EMB, size):
        cols = slice(at, min(at + size, COLS * EMB))
        scale = jnp.dot(low, up[:, cols], preferred_element_type=F32) + bias[cols].astype(F32)[None, :]
        back = jnp.dot(d_low, down[:, cols], preferred_element_type=F32)
        grad = u[:, cols].astype(F32) * (scale + 1.0) + back
        pooled[:, cols.start - EMB : cols.stop - EMB] = grad.astype(BF16)
    for k, out in enumerate((out0, out1, out2, out3)):
        to = lax.rem(axis("x") + k, NX)
        for i in range(TX):

            def put(out=out, to=to, i=i):
                t = to * TX + i
                out[i, :S] = pooled[:, pl.ds(pl.multiple_of(t * EMB, EMB), EMB)]
                out[i, S:] = coded[t]

            def blank(out=out, i=i):
                out[i, :S] = jnp.zeros((S, EMB), BF16)
                out[i, S:] = jnp.full((BAG, S), NONE, BF16)

            if (NX - 1) * TX + i < TABLES:
                put()
            else:
                pl.when(to < NX - 1)(put)
                pl.when(to == NX - 1)(blank)


def cross(x, u, down, up, bias, coded):
    half = jax.ShapeDtypeStruct((2, HALF, S), BF16)
    part = jax.ShapeDtypeStruct((TX, S + BAG, EMB), BF16)
    anywhere = pl.BlockSpec(memory_space=pl.ANY)
    return pl.pallas_call(
        cross_kernel,
        out_shape=(half, half) + (part,) * NX,
        in_specs=[anywhere] * 4 + [VMEM] * 3,
        out_specs=(VMEM,) * (2 + NX),
        scratch_shapes=[
            pltpu.VMEM(x.shape, BF16),
            pltpu.VMEM(x.shape, BF16),
            pltpu.VMEM(down.shape, BF16),
            pltpu.VMEM(down.shape, BF16),
            pltpu.VMEM((S, TABLES * EMB), BF16),
            pltpu.SemaphoreType.DMA((2 + 2 * NY,)),
        ],
        compiler_params=params(54),
        cost_estimate=cost(5),
        name="cross",
    )(x, u, down, up, bias, jnp.asarray(rank_order(), BF16), coded)


def bag_kernel(block0, block1, block2, block3, keep, give):
    blocks = (block0, block1, block2, block3)
    places = lax.broadcasted_iota(jnp.int32, (ROWB, NX * S), 0)

    @pl.loop(0, TX)
    def _(i):
        ids = jnp.concatenate([b[i, S:].astype(F32) for b in blocks], axis=1).astype(jnp.int32) + 256
        low = jnp.bitwise_and(ids, ROWB - 1)
        part = jnp.bitwise_and(lax.shift_right_arithmetic(ids, 6), 1)
        field = jnp.bitwise_and(lax.shift_right_arithmetic(ids, 7), 3)
        value = jnp.where(ids < UNIQ, lax.shift_left(jnp.ones_like(ids), field * 8), 0)
        grads = jnp.concatenate([b[i, :S] for b in blocks], axis=0)
        for out, mine in ((keep, axis("c")), (give, 1 - axis("c"))):
            worth = jnp.where(part == mine, value, 0)
            packed = jnp.zeros((ROWB, NX * S), jnp.int32)
            for j in range(BAG):
                packed = packed + jnp.where(places == low[j : j + 1], worth[j : j + 1], 0)
            counts = jnp.concatenate(
                [
                    jnp.bitwise_and(lax.shift_right_logical(packed, 8 * f), 255)
                    .astype(F32)
                    .astype(BF16)
                    for f in range(NX)
                ],
                axis=0,
            )
            out[i] = jnp.dot(counts, grads, preferred_element_type=F32).astype(out.dtype)


def bag_sums(blocks):
    shape = (TX, NX * ROWB, EMB)
    return pl.pallas_call(
        bag_kernel,
        out_shape=(jax.ShapeDtypeStruct(shape, F32), jax.ShapeDtypeStruct(shape, BF16)),
        in_specs=[VMEM] * NX,
        out_specs=(VMEM, VMEM),
        compiler_params=params(),
        cost_estimate=cost(10),
        name="bag_sums",
    )(*blocks)


def bag_add_kernel(keep, got, dense, out):
    sums = (keep[...] + got[...].astype(F32)).astype(BF16)
    for k in range(NX):
        for m in range(NY):
            at = (k * NY + m) * PIECE
            for i in range(TX):
                out[m * NX + k, i * PIECE : (i + 1) * PIECE] = sums[i, at : at + PIECE]
    out[:, TX * PIECE :] = dense[...]


def bag_add(keep, got, dense):
    return pl.pallas_call(
        bag_add_kernel,
        out_shape=jax.ShapeDtypeStruct((NY * NX, TX * PIECE + XB * NW, EMB), BF16),
        in_specs=[VMEM] * 3,
        out_specs=VMEM,
        compiler_params=params(),
        cost_estimate=cost(0),
        name="bag_add",
    )(keep, got, dense)


def gather_side(me_y, side, lows, ref, wide_x, wide_low):
    for g in range(2):
        for k in range(NY):
            src = lax.rem(me_y - k + NY, NY)
            wide_low[g, :, k * S : (k + 1) * S] = lows[k][side, g]
            wide_x[g, k * S : (k + 1) * S] = ref[src, g]


def dense_own_kernel(own, low0, low1, low2, low3, out, wide_x, wide_low):
    gather_side(axis("y"), 0, (low0, low1, low2, low3), own, wide_x, wide_low)
    for g in range(2):
        out[g] = jnp.dot(wide_low[g], wide_x[g], preferred_element_type=F32)


def dense_both_kernel(first, sib, low0, low1, low2, low3, out, wide_x, wide_low):
    gather_side(axis("y"), 1, (low0, low1, low2, low3), sib, wide_x, wide_low)
    for g in range(2):
        sums = first[g] + jnp.dot(wide_low[g], wide_x[g], preferred_element_type=F32)
        sums = sums.astype(BF16)
        for x in range(NX):
            for p in range(2):
                at = (x * 2 + p) * NW
                for j in range(XB):
                    out[(g * 2 + p) * NX + x, j * NW : (j + 1) * NW] = sums[
                        at : at + NW, j * EMB : (j + 1) * EMB
                    ]


WIDE_SIDE = [
    pltpu.VMEM((2, NY * S, XB * EMB), BF16),
    pltpu.VMEM((2, HALF, NY * S), BF16),
]


def dense_own(own, lows):
    return pl.pallas_call(
        dense_own_kernel,
        out_shape=jax.ShapeDtypeStruct((2, HALF, XB * EMB), F32),
        in_specs=[VMEM] * 5,
        out_specs=VMEM,
        scratch_shapes=WIDE_SIDE,
        compiler_params=params(),
        cost_estimate=cost(10),
        name="dense_own",
    )(own, *lows)


def dense_both(first, sib, lows):
    return pl.pallas_call(
        dense_both_kernel,
        out_shape=jax.ShapeDtypeStruct((NY * NX, XB * NW, EMB), BF16),
        in_specs=[VMEM] * 6,
        out_specs=VMEM,
        scratch_shapes=WIDE_SIDE,
        compiler_params=params(),
        cost_estimate=cost(0),
        name="dense_both",
    )(first, sib, *lows)


def merge_kernel(owner, got, out, total):
    total[...] = jnp.zeros_like(total)
    for t in range(TABLES):
        x, i = t // TX, t % TX
        one = got[x, i * PIECE : (i + 1) * PIECE].astype(F32)
        for y in range(1, NY):
            one = one + got[y * NX + x, i * PIECE : (i + 1) * PIECE].astype(F32)
        to = owner[t]
        total[to, :PIECE] = total[to, :PIECE] + one
    for y in range(NY):
        for j in range(XB):
            at = TX * PIECE + j * NW
            one = got[y * NX, at : at + NW].astype(F32)
            for x in range(1, NX):
                one = one + got[y * NX + x, at : at + NW].astype(F32)
            total[:, PIECE + y * XB + j, :] = one
    out[...] = total[...].astype(BF16)


def merge(owner, got):
    return pl.pallas_call(
        merge_kernel,
        out_shape=jax.ShapeDtypeStruct((NW, MROWS, EMB), BF16),
        in_specs=[SMEM, VMEM],
        out_specs=VMEM,
        scratch_shapes=[pltpu.VMEM((NW, MROWS, EMB), F32)],
        compiler_params=params(),
        cost_estimate=cost(0),
        name="merge",
    )(owner, got)


def split_kernel(got, rows, up, down, stage):
    for y in range(NY):
        one = got[y * NZ].astype(F32)
        for z in range(1, NZ):
            one = one + got[y * NZ + z].astype(F32)
        for n in range(NX * NC):
            rows[n, y * PIECE : (y + 1) * PIECE] = one[:PIECE]
        stage[y] = one[PIECE:] * (1.0 / math.sqrt(S * NW * NX * NC))
    for y in range(NY):
        for j in range(XB):
            at = (y * XB + j) * EMB
            if at < COLS * EMB:
                for g, to in enumerate((up, down)):
                    for p in range(2):
                        to[p : p + 1, at : at + EMB] = stage[g * 2 + p, y * XB + j : y * XB + j + 1]


def split(got):
    grad = jax.ShapeDtypeStruct((2, COLS * EMB), F32)
    return pl.pallas_call(
        split_kernel,
        out_shape=(jax.ShapeDtypeStruct((NX * NC, ROWB, EMB), F32), grad, grad),
        in_specs=[VMEM],
        out_specs=(VMEM, VMEM, VMEM),
        scratch_shapes=[pltpu.VMEM((NY, MROWS - PIECE, EMB), F32)],
        compiler_params=params(),
        cost_estimate=cost(0),
        name="split",
    )(got)


def adagrad_rows(rows, accum, admitted, grad):
    begin_acc = jnp.where(admitted == 1, jnp.float32(0.1), accum)
    new_acc = begin_acc + jnp.mean(grad * grad, axis=1)
    new_values = rows - 0.5 * grad / (jnp.sqrt(new_acc)[:, None] + 1e-08)
    return (new_values, new_acc)


def local(
    cross_input,
    upstream,
    cross_down,
    cross_up,
    cross_bias,
    bag_rows,
    bag_lengths,
    table_owner,
    table_rows,
    row_accum,
    admitted,
):
    def send(a, axis, k):
        size = lax.axis_size(axis)
        return lax.ppermute(a, axis, [(i, (i + k) % size) for i in range(size)])

    pair, coded = pack(
        cross_input, upstream, jnp.transpose(bag_rows, (1, 2, 0)), bag_lengths.T
    )
    own = lax.all_to_all(pair, "y", split_axis=0, concat_axis=0, tiled=True)
    keep, give, *blocks = cross(
        cross_input, upstream, cross_down, cross_up, cross_bias, coded
    )
    low0 = jnp.stack([keep, send(give, "c", 1)])
    lows = [low0] + [send(low0, "y", k) for k in range(1, NY)]

    blocks = [blocks[0]] + [send(blocks[k], "x", k) for k in range(1, NX)]
    keep, give = bag_sums(blocks)
    sib = send(own, "c", 1)
    dense = dense_both(dense_own(own, lows), sib, lows)
    got = send(give, "c", 1)
    got, dense = lax.optimization_barrier((got, dense))
    sums = bag_add(keep, got, dense)
    got = lax.all_to_all(sums, ("y", "x"), split_axis=0, concat_axis=0, tiled=True)
    merged = merge(table_owner, got)
    merged = lax.all_to_all(merged, WIDE, split_axis=0, concat_axis=0, tiled=True)
    rows, grad_up, grad_down = split(merged)
    rows = lax.all_to_all(rows, ("x", "c"), split_axis=0, concat_axis=0, tiled=True)
    new_rows, new_accum = adagrad_rows(
        table_rows, row_accum, admitted, rows.reshape(UNIQ, EMB)
    )
    return (new_rows, new_accum, grad_up, grad_down)


def solution(mesh):
    inner = Mesh(mesh.devices.reshape(NY, NZ, NX, NC), ALL)
    return jax.shard_map(
        local,
        mesh=inner,
        in_specs=(
            P(ALL, None),
            P(ALL, None),
            P(),
            P(),
            P(),
            P(ALL, None, None),
            P(ALL, None),
            P(),
            P(WIDE, None),
            P(WIDE),
            P(WIDE),
        ),
        out_specs=(
            P(WIDE, None),
            P(WIDE),
            P(ALL, None),
            P(ALL, None),
        ),
        check_vma=False,
    )
```

time: 115 us -> 109 us (0.948)
  blocking collectives: 39 us -> 59.5 us
  waiting for transfers between devices: 19.8 us -> 2.38 us
  matrix products: 5.84 us -> 0 us
  starting transfers between devices: 24 us -> 19.2 us
  Pallas kernels: 19.6 us -> 23.6 us
  local copies, waits for them, and re-layouts: 2.29 us -> 1.04 us
    all_to_all x0 -> x1, blocking collectives: none -> 26 us  [local(): lax.all_to_all(sums, ('y', 'x'), split_axis=0, concat_axis=0, tiled=True)]
    all_to_all x1 -> x0, waiting for transfers between devices: 9.28 us -> none  [local(): lax.all_to_all(sums, ('y', 'x'), split_axis=0, concat_axis=0, tiled=True)]
    ppermute x10 -> x9, waiting for transfers between devices: 10.5 us -> 2.38 us  [send(): return lax.ppermute(a, axis, [(i, (i + k) % size) for i in range(size)])]
    dot_general x4 -> x0, matrix products: 5.84 us -> none  [the longest x1 3.45 us: local(): lax.dot_general(cross_down, cross_input, (((1,), (1,)), ((), ())), prefer...]
    pallas_call x3 -> x4, Pallas kernels: 11.3 us -> 17.1 us  [the longest x1 9.1 us: cross(): pl.pallas_call(cross_kernel, out_shape=(half, half) + (part,) * NX, in_sp...]
    all_to_all x1 -> x0, starting transfers between devices: 5.12 us -> none  [local(): lax.all_to_all(sums, ('y', 'x'), split_axis=0, concat_axis=0, tiled=True)]
    all_to_all x1, blocking collectives: 17.8 us -> 14.2 us  [local(): lax.all_to_all(rows, ('x', 'c'), split_axis=0, concat_axis=0, tiled=True)]
    all_to_all x1, blocking collectives: 21.2 us -> 19.3 us  [local(): lax.all_to_all(merged, WIDE, split_axis=0, concat_axis=0, tiled=True)]
  transfers between devices with their start and end apart: 12 -> 10, of which waited for: 5 -> 3; matrix products, arithmetic and copies ran while one was open for 6% -> 1% of each run, Pallas kernels for 12% -> 16%
where the time goes in v3:
time: 109 us
  blocking collectives  59.5 us (55%)
  Pallas kernels  23.6 us (22%)
  starting transfers between devices  19.2 us (18%)
  other arithmetic  2.5 us (2%)
  waiting for transfers between devices  2.38 us (2%)
    all_to_all x1, blocking collectives, local(): lax.all_to_all(sums, ('y', 'x'), split_axis=0, concat_axis=0, tiled=True)  26 us
    all_to_all x1, blocking collectives, local(): lax.all_to_all(merged, WIDE, split_axis=0, concat_axis=0, tiled=True)  19.3 us
    ppermute x9, starting transfers between devices, send(): return lax.ppermute(a, axis, [(i, (i + k) % size) for i in range(size)])  14.2 us
    all_to_all x1, blocking collectives, local(): lax.all_to_all(rows, ('x', 'c'), split_axis=0, concat_axis=0, tiled=True)  14.2 us
    pallas_call x1, Pallas kernels, cross(): pl.pallas_call(cross_kernel, out_shape=(half, half) + (part,) * NX, in_sp...  9.1 us
    pallas_call x1, Pallas kernels, bag_sums(): pl.pallas_call(bag_kernel, out_shape=(jax.ShapeDtypeStruct(shape, F32), j...  7.06 us
    all_to_all x1, starting transfers between devices, local(): own = lax.all_to_all(pair, 'y', split_axis=0, concat_axis=0, tiled=True)  5.01 us
    pallas_call x1, Pallas kernels, pack(): pl.pallas_call(pack_kernel, grid=(steps,), out_shape=(jax.ShapeDtypeStruc...  3.97 us
  transfers between devices with their start and end apart: 10, of which 3 were waited for; matrix products, arithmetic and copies ran while one was open for 1% of the time, Pallas kernels for 16%

profile of v3, /device:TPU:1, one launch (start us, length us, event | category | flops | bytes accessed | tf_op | source)
XLA Modules:
  0.0 109.0 jit_solution(4377106549351124052)
XLA Ops:
  0.6 4.0 %pack.1 = (bf16[4,2,128,896]{3,2,1,0:T(8,128)(2,1)}, bf16[26,16,128]{2,1,0:T(8,128)(2,1)}) custom-call(bf16[128,3456]{1,0:T(8,128)(2,1)} %x_in.1, bf16[128,3456]{1,0:T(8,128)(2,1)} %u_in.1, s32[26,16,128]{2,1,0:T(8,128)} %bitcast.10, s32[26,128]{1,0:T(8,128)} %bitcast.11), custom_call_target="tpu_custom_call" | custom-call | flops 1500000000 | bytes 150000 | tf_op jit(solution)/shard_map/pack/pallas_call | solution.py:72
  4.6 5.0 %all-to-all-start = ((bf16[4,2,128,896]{3,2,1,0:T(8,128)(2,1)}), bf16[4,2,128,896]{3,2,1,0:T(8,128)(2,1)S(1)}, u32[]{:S(2)}, u32[]{:S(2)}) async-start(bf16[4,2,128,896]{3,2,1,0:T(8,128)(2,1)} %get-tuple-element.26), calls=%async_computation | async-start | bytes 3670016 | tf_op jit(solution)/shard_map/all_to_all | solution.py:392
  9.6 9.1 %cross.1 = (bf16[2,256,128]{2,1,0:T(8,128)(2,1)}, bf16[2,256,128]{2,1,0:T(8,128)(2,1)}, bf16[7,144,128]{2,1,0:T(8,128)(2,1)}, bf16[7,144,128]{2,1,0:T(8,128)(2,1...) custom-call(bf16[128,3456]{1,0:T(8,128)(2,1)} %x_in.1, bf16[128,3456]{1,0:T(8,128)(2,1)} %u_in.1, ...), custom_call_target="tpu_custom_call" | custom-call | flops 5000000000 | bytes 500000 | tf_op jit(solution)/shard_map/cross/pallas_call | solution.py:159
  18.7 1.3 %collective-permute-start = (bf16[7,144,128]{2,1,0:T(8,128)(2,1)}, bf16[7,144,128]{2,1,0:T(8,128)(2,1)S(1)}, u32[]{:S(2)}, u32[]{:S(2)}) collective-permute-start(bf16[7,144,128]{2,1,0:T(8,128)(2,1)} %get-tuple-element.21), channel_id=1, source_target_pairs={{0,2},{2,4},{4,6},{6,0},{1,3},{3,5},{5,7},{7,1},{8,10},{10,12},{12... | collective-permute-start | bytes 774152 | tf_op jit(solution)/shard_map/ppermute | solution.py:387
  20.0 2.5 %collective-permute-start.1 = (bf16[7,144,128]{2,1,0:T(8,128)(2,1)}, bf16[7,144,128]{2,1,0:T(8,128)(2,1)S(1)}, u32[]{:S(2)}, u32[]{:S(2)}) collective-permute-start(bf16[7,144,128]{2,1,0:T(8,128)(2,1)} %get-tuple-element.22), channel_id=1, source_target_pairs={{0,4},{2,6},{4,0},{6,2},{1,5},{3,7},{5,1},{7,3},{8,12},{10,14},{12... | collective-permute-start | bytes 774152 | tf_op jit(solution)/shard_map/ppermute | solution.py:387
  22.5 1.2 %collective-permute-start.2 = (bf16[7,144,128]{2,1,0:T(8,128)(2,1)}, bf16[7,144,128]{2,1,0:T(8,128)(2,1)}, u32[]{:S(2)}, u32[]{:S(2)}) collective-permute-start(bf16[7,144,128]{2,1,0:T(8,128)(2,1)} %get-tuple-element.23), channel_id=1, source_target_pairs={{0,6},{2,0},{4,2},{6,4},{1,7},{3,1},{5,3},{7,5},{8,14},{10,8},{12,... | collective-permute-start | bytes 774152 | tf_op jit(solution)/shard_map/ppermute | solution.py:387
  23.6 1.8 %collective-permute-start.4 = (bf16[2,256,128]{2,1,0:T(8,128)(2,1)}, bf16[2,256,128]{2,1,0:T(8,128)(2,1)S(1)}, u32[]{:S(2)}, u32[]{:S(2)}) collective-permute-start(bf16[2,256,128]{2,1,0:T(8,128)(2,1)} %get-tuple-element.28), channel_id=1, source_target_pairs={{0,1},{1,0},{2,3},{3,2},{4,5},{5,4},{6,7},{7,6},{8,9},{9,8},{10,11... | collective-permute-start | bytes 393224 | tf_op jit(solution)/shard_map/ppermute | solution.py:387
  25.4 1.2 %collective-permute-done.4 = bf16[2,256,128]{2,1,0:T(8,128)(2,1)S(1)} collective-permute-done((bf16[2,256,128]{2,1,0:T(8,128)(2,1)}, bf16[2,256,128]{2,1,0:T(8,128)(2,1)S(1)}, u32[]{:S(2)}, u32[]{:S(2)}) %collective-permute-start.4) | collective-permute-done | bytes 131104 | tf_op jit(solution)/shard_map/ppermute | solution.py:387
  26.6 0.9 pad_maximum_fusion.low0
  27.5 1.8 %collective-permute-start.5 = (bf16[2,2,256,128]{3,2,1,0:T(8,128)(2,1)S(1)}, bf16[2,2,256,128]{3,2,1,0:T(8,128)(2,1)S(1)}, u32[]{:S(2)}, u32[]{:S(2)}) collective-permute-start(bf16[2,2,256,128]{3,2,1,0:T(8,128)(2,1)S(1)} %pad_maximum_fusion.low0), channel_id=1, source_target_pairs={{0,64},{64,128},{128,192},{192,0},{1,65},{65,129},{129,193},{193,1... | collective-permute-start | bytes 786440 | tf_op jit(solution)/shard_map/ppermute | solution.py:387
  29.4 2.4 %collective-permute-start.6 = (bf16[2,2,256,128]{3,2,1,0:T(8,128)(2,1)S(1)}, bf16[2,2,256,128]{3,2,1,0:T(8,128)(2,1)S(1)}, u32[]{:S(2)}, u32[]{:S(2)}) collective-permute-start(bf16[2,2,256,128]{3,2,1,0:T(8,128)(2,1)S(1)} %pad_maximum_fusion.low0), channel_id=1, source_target_pairs={{0,128},{64,192},{128,0},{192,64},{1,129},{65,193},{129,1},{193,65... | collective-permute-start | bytes 786440 | tf_op jit(solution)/shard_map/ppermute | solution.py:387
  31.8 0.0 collective-permute-done.block1
  31.8 1.2 %collective-permute-start.7 = (bf16[2,2,256,128]{3,2,1,0:T(8,128)(2,1)S(1)}, bf16[2,2,256,128]{3,2,1,0:T(8,128)(2,1)S(1)}, u32[]{:S(2)}, u32[]{:S(2)}) collective-permute-start(bf16[2,2,256,128]{3,2,1,0:T(8,128)(2,1)S(1)} %pad_maximum_fusion.low0), channel_id=1, source_target_pairs={{0,192},{64,0},{128,64},{192,128},{1,193},{65,1},{129,65},{193,129... | collective-permute-start | bytes 786440 | tf_op jit(solution)/shard_map/ppermute | solution.py:387
  33.0 0.6 collective-permute-done.1.block2
  33.5 0.0 all-to-all-done.own
  33.5 1.9 %collective-permute-start.8 = (bf16[4,2,128,896]{3,2,1,0:T(8,128)(2,1)S(1)}, bf16[4,2,128,896]{3,2,1,0:T(8,128)(2,1)S(1)}, u32[]{:S(2)}, u32[]{:S(2)}) collective-permute-start(bf16[4,2,128,896]{3,2,1,0:T(8,128)(2,1)S(1)} %all-to-all-done.own), channel_id=1, source_target_pairs={{0,1},{1,0},{2,3},{3,2},{4,5},{5,4},{6,7},{7,6},{8,9},{9,8},{10,11... | collective-permute-start | bytes 5505032 | tf_op jit(solution)/shard_map/ppermute | solution.py:387
  35.4 0.0 collective-permute-done.2.block3
  35.4 0.0 copy-start.1
  35.4 0.9 copy-done.1
  36.3 7.1 %bag_sums.1 = (f32[7,256,128]{2,1,0:T(8,128)S(1)}, bf16[7,256,128]{2,1,0:T(8,128)(2,1)S(1)}) custom-call(bf16[7,144,128]{2,1,0:T(8,128)(2,1)S(1)} %copy-done.1, bf16[7,144,128]{2,1,0:T(8,128)(2,1)S(1)} %collective-permute-done.block1, bf16[7,144,128]{2,1,0:T(8,128)(2,1)S(1)} %collective-permute-done.1.block2, bf16[7,144,128]{2,1,0:T(8,128)(2,1)} %collective-permute-done.2.block3), custom_call_target="tpu_custom_call" | custom-call | flops 10000000000 | bytes 1000000 | tf_op jit(solution)/shard_map/bag_sums/pallas_call | solution.py:209
  43.4 0.3 collective-permute-start.3
  43.7 0.0 collective-permute-done.5.low1
  43.7 0.6 collective-permute-done.6.low2
  44.3 0.0 collective-permute-done.7.low3
  44.3 0.7 dense_own.1.first
  45.1 0.0 collective-permute-done.8.sib
  45.1 0.8 dense_both.1.dense
  45.8 0.0 collective-permute-done.3.got
  45.8 0.1 bag_add.1
  46.0 0.0 copy-start
  46.0 26.0 %all_to_all.20.got = bf16[16,336,128]{2,1,0:T(8,128)(2,1)S(1)} all-to-all(bf16[16,336,128]{2,1,0:T(8,128)(2,1)S(1)} %bag_add.1), channel_id=1, replica_groups=mesh['y'=4,'z'=8,'x'=4,'c'=2] {'y','x'}, dimensions={0} | all-to-all | bytes 2752512 | tf_op jit(solution)/shard_map/all_to_all | solution.py:406
  72.0 0.0 copy-done
  72.0 0.0 copy-start.3
  72.0 0.0 copy-start.4
  72.0 0.0 copy-start.2
  72.0 1.1 %merge.1 = bf16[32,48,128]{2,1,0:T(8,128)(2,1)S(1)} custom-call(s32[26]{0:T(128)S(1)} %copy-done, bf16[16,336,128]{2,1,0:T(8,128)(2,1)S(1)} %all_to_all.20.got), custom_call_target="tpu_custom_call" | custom-call | tf_op jit(solution)/shard_map/merge/pallas_call | solution.py:322
  73.1 19.3 %all_to_all.21.got = bf16[32,48,128]{2,1,0:T(8,128)(2,1)S(1)} all-to-all(bf16[32,48,128]{2,1,0:T(8,128)(2,1)S(1)} %merge.1), channel_id=1, replica_groups=mesh['y'=4,'z'=8,'x'=4,'c'=2] {'y','z'}, dimensions={0} | all-to-all | bytes 786432 | tf_op jit(solution)/shard_map/all_to_all | solution.py:408
  92.4 0.7 split.1
  93.1 14.2 %all_to_all.22 = f32[8,64,128]{2,1,0:T(8,128)S(1)} all-to-all(f32[8,64,128]{2,1,0:T(8,128)S(1)} %get-tuple-element.31), channel_id=1, replica_groups=mesh['y'=4,'z'=8,'x'=4,'c'=2] {'x','c'}, dimensions={0} | all-to-all | bytes 524288 | tf_op jit(solution)/shard_map/all_to_all | solution.py:410
  107.3 0.1 multiply_reduce_fusion
  107.4 0.1 div.18
  107.5 0.0 copy-done.3
  107.5 0.0 copy-done.4
  107.5 0.6 sqrt_add_fusion
  108.1 0.0 copy-done.2
  108.1 0.8 fusion
  (1 shorter events, 0.0 us)
Async XLA Ops:
  4.6 28.9 %all-to-all-start = ((bf16[4,2,128,896]{3,2,1,0:T(8,128)(2,1)}), bf16[4,2,128,896]{3,2,1,0:T(8,128)(2,1)S(1)}, u32[]{:S(2)}, u32[]{:S(2)}) async-start(bf16[4,2,128,896]{3,2,1,0:T(8,128)(2,1)} %get-tuple-element.26), calls=%async_computation | async-start | bytes 3670016 | tf_op jit(solution)/shard_map/all_to_all | solution.py:392
  18.7 13.0 %collective-permute-start = (bf16[7,144,128]{2,1,0:T(8,128)(2,1)}, bf16[7,144,128]{2,1,0:T(8,128)(2,1)S(1)}, u32[]{:S(2)}, u32[]{:S(2)}) collective-permute-start(bf16[7,144,128]{2,1,0:T(8,128)(2,1)} %get-tuple-element.21), channel_id=1, source_target_pairs={{0,2},{2,4},{4,6},{6,0},{1,3},{3,5},{5,7},{7,1},{8,10},{10,12},{12... | collective-permute-start | bytes 774152 | tf_op jit(solution)/shard_map/ppermute | solution.py:387
  20.0 13.5 %collective-permute-start.1 = (bf16[7,144,128]{2,1,0:T(8,128)(2,1)}, bf16[7,144,128]{2,1,0:T(8,128)(2,1)S(1)}, u32[]{:S(2)}, u32[]{:S(2)}) collective-permute-start(bf16[7,144,128]{2,1,0:T(8,128)(2,1)} %get-tuple-element.22), channel_id=1, source_target_pairs={{0,4},{2,6},{4,0},{6,2},{1,5},{3,7},{5,1},{7,3},{8,12},{10,14},{12... | collective-permute-start | bytes 774152 | tf_op jit(solution)/shard_map/ppermute | solution.py:387
  22.5 12.9 %collective-permute-start.2 = (bf16[7,144,128]{2,1,0:T(8,128)(2,1)}, bf16[7,144,128]{2,1,0:T(8,128)(2,1)}, u32[]{:S(2)}, u32[]{:S(2)}) collective-permute-start(bf16[7,144,128]{2,1,0:T(8,128)(2,1)} %get-tuple-element.23), channel_id=1, source_target_pairs={{0,6},{2,0},{4,2},{6,4},{1,7},{3,1},{5,3},{7,5},{8,14},{10,8},{12,... | collective-permute-start | bytes 774152 | tf_op jit(solution)/shard_map/ppermute | solution.py:387
  23.6 3.0 %collective-permute-start.4 = (bf16[2,256,128]{2,1,0:T(8,128)(2,1)}, bf16[2,256,128]{2,1,0:T(8,128)(2,1)S(1)}, u32[]{:S(2)}, u32[]{:S(2)}) collective-permute-start(bf16[2,256,128]{2,1,0:T(8,128)(2,1)} %get-tuple-element.28), channel_id=1, source_target_pairs={{0,1},{1,0},{2,3},{3,2},{4,5},{5,4},{6,7},{7,6},{8,9},{9,8},{10,11... | collective-permute-start | bytes 393224 | tf_op jit(solution)/shard_map/ppermute | solution.py:387
  27.5 16.1 %collective-permute-start.5 = (bf16[2,2,256,128]{3,2,1,0:T(8,128)(2,1)S(1)}, bf16[2,2,256,128]{3,2,1,0:T(8,128)(2,1)S(1)}, u32[]{:S(2)}, u32[]{:S(2)}) collective-permute-start(bf16[2,2,256,128]{3,2,1,0:T(8,128)(2,1)S(1)} %pad_maximum_fusion.low0), channel_id=1, source_target_pairs={{0,64},{64,128},{128,192},{192,0},{1,65},{65,129},{129,193},{193,1... | collective-permute-start | bytes 786440 | tf_op jit(solution)/shard_map/ppermute | solution.py:387
  29.4 14.9 %collective-permute-start.6 = (bf16[2,2,256,128]{3,2,1,0:T(8,128)(2,1)S(1)}, bf16[2,2,256,128]{3,2,1,0:T(8,128)(2,1)S(1)}, u32[]{:S(2)}, u32[]{:S(2)}) collective-permute-start(bf16[2,2,256,128]{3,2,1,0:T(8,128)(2,1)S(1)} %pad_maximum_fusion.low0), channel_id=1, source_target_pairs={{0,128},{64,192},{128,0},{192,64},{1,129},{65,193},{129,1},{193,65... | collective-permute-start | bytes 786440 | tf_op jit(solution)/shard_map/ppermute | solution.py:387
  31.8 12.5 %collective-permute-start.7 = (bf16[2,2,256,128]{3,2,1,0:T(8,128)(2,1)S(1)}, bf16[2,2,256,128]{3,2,1,0:T(8,128)(2,1)S(1)}, u32[]{:S(2)}, u32[]{:S(2)}) collective-permute-start(bf16[2,2,256,128]{3,2,1,0:T(8,128)(2,1)S(1)} %pad_maximum_fusion.low0), channel_id=1, source_target_pairs={{0,192},{64,0},{128,64},{192,128},{1,193},{65,1},{129,65},{193,129... | collective-permute-start | bytes 786440 | tf_op jit(solution)/shard_map/ppermute | solution.py:387
  33.5 11.5 %collective-permute-start.8 = (bf16[4,2,128,896]{3,2,1,0:T(8,128)(2,1)S(1)}, bf16[4,2,128,896]{3,2,1,0:T(8,128)(2,1)S(1)}, u32[]{:S(2)}, u32[]{:S(2)}) collective-permute-start(bf16[4,2,128,896]{3,2,1,0:T(8,128)(2,1)S(1)} %all-to-all-done.own), channel_id=1, source_target_pairs={{0,1},{1,0},{2,3},{3,2},{4,5},{5,4},{6,7},{7,6},{8,9},{9,8},{10,11... | collective-permute-start | bytes 5505032 | tf_op jit(solution)/shard_map/ppermute | solution.py:387
  35.4 0.9 copy-start.1
  43.4 2.4 %collective-permute-start.3 = (bf16[7,256,128]{2,1,0:T(8,128)(2,1)S(1)}, bf16[7,256,128]{2,1,0:T(8,128)(2,1)S(1)}, u32[]{:S(2)}, u32[]{:S(2)}) collective-permute-start(bf16[7,256,128]{2,1,0:T(8,128)(2,1)S(1)} %get-tuple-element.25), channel_id=1, source_target_pairs={{0,1},{1,0},{2,3},{3,2},{4,5},{5,4},{6,7},{7,6},{8,9},{9,8},{10,11... | collective-permute-start | bytes 1376264 | tf_op jit(solution)/shard_map/ppermute | solution.py:387
  46.0 26.0 %copy-start = (s32[26]{0:T(128)S(1)}, s32[26]{0:T(128)}, u32[]{:S(2)}) copy-start(s32[26]{0:T(128)} %owner.1) | copy-start | bytes 316
  72.0 35.5 %copy-start.3 = (f32[512]{0:T(512)S(1)}, f32[512]{0:T(512)}, u32[]{:S(2)}) copy-start(f32[512]{0:T(512)} %param.21) | copy-start | bytes 6148
  72.0 35.5 %copy-start.4 = (s32[512]{0:T(512)S(1)}, s32[512]{0:T(512)}, u32[]{:S(2)}) copy-start(s32[512]{0:T(512)} %param.22) | copy-start | bytes 6148
  72.0 36.1 %copy-start.2 = (f32[512,128]{1,0:T(8,128)S(1)}, f32[512,128]{1,0:T(8,128)}, u32[]{:S(2)}) copy-start(f32[512,128]{1,0:T(8,128)} %param.20) | copy-start | bytes 786436

commit v4 on v3

--- a/solution.py
+++ b/solution.py
@@ -30,7 +30,7 @@
 
 
 def rank_order():
-    order = np.arange(RANK).reshape(NW, NX, NC, 2).transpose(2, 1, 3, 0).reshape(-1)
+    order = np.arange(RANK).reshape(NY, NZ, NX, NC, 2).transpose(3, 2, 1, 0, 4).reshape(-1)
     return np.eye(RANK, dtype=np.float32)[order]
 
 
@@ -217,26 +217,24 @@
     )(*blocks)
 
 
-def bag_add_kernel(keep, got, dense, out):
+def bag_add_kernel(keep, got, out):
     sums = (keep[...] + got[...].astype(F32)).astype(BF16)
     for k in range(NX):
         for m in range(NY):
             at = (k * NY + m) * PIECE
-            for i in range(TX):
-                out[m * NX + k, i * PIECE : (i + 1) * PIECE] = sums[i, at : at + PIECE]
-    out[:, TX * PIECE :] = dense[...]
-
-
-def bag_add(keep, got, dense):
+            out[m * NX + k] = sums[:, at : at + PIECE]
+
+
+def bag_add(keep, got):
     return pl.pallas_call(
         bag_add_kernel,
-        out_shape=jax.ShapeDtypeStruct((NY * NX, TX * PIECE + XB * NW, EMB), BF16),
-        in_specs=[VMEM] * 3,
+        out_shape=jax.ShapeDtypeStruct((NY * NX, TX, PIECE, EMB), BF16),
+        in_specs=[VMEM, VMEM],
         out_specs=VMEM,
         compiler_params=params(),
         cost_estimate=cost(0),
         name="bag_add",
-    )(keep, got, dense)
+    )(keep, got)
 
 
 def gather_side(me_y, side, lows, ref, wide_x, wide_low):
@@ -253,18 +251,17 @@
         out[g] = jnp.dot(wide_low[g], wide_x[g], preferred_element_type=F32)
 
 
-def dense_both_kernel(first, sib, low0, low1, low2, low3, out, wide_x, wide_low):
+def dense_both_kernel(first, sib, low0, low1, low2, low3, out0, out1, out2, out3, wide_x, wide_low, stage):
     gather_side(axis("y"), 1, (low0, low1, low2, low3), sib, wide_x, wide_low)
-    for g in range(2):
-        sums = first[g] + jnp.dot(wide_low[g], wide_x[g], preferred_element_type=F32)
-        sums = sums.astype(BF16)
-        for x in range(NX):
-            for p in range(2):
-                at = (x * 2 + p) * NW
-                for j in range(XB):
-                    out[(g * 2 + p) * NX + x, j * NW : (j + 1) * NW] = sums[
-                        at : at + NW, j * EMB : (j + 1) * EMB
-                    ]
+    both = [
+        first[g] + jnp.dot(wide_low[g], wide_x[g], preferred_element_type=F32) for g in range(2)
+    ]
+    for j in range(XB):
+        pieces = [b[:, j * EMB : (j + 1) * EMB].reshape(NX, NZ, 8, EMB) for b in both]
+        stage[:, :, j * 16 : (j + 1) * 16, :] = jnp.concatenate(pieces, axis=2).astype(BF16)
+
+    for k, out in enumerate((out0, out1, out2, out3)):
+        out[...] = stage[lax.rem(axis("x") + k, NX)]
 
 
 WIDE_SIDE = [
@@ -287,48 +284,69 @@
 
 
 def dense_both(first, sib, lows):
+    part = jax.ShapeDtypeStruct((NZ, 16 * XB, EMB), BF16)
     return pl.pallas_call(
         dense_both_kernel,
-        out_shape=jax.ShapeDtypeStruct((NY * NX, XB * NW, EMB), BF16),
+        out_shape=(part,) * NX,
         in_specs=[VMEM] * 6,
-        out_specs=VMEM,
-        scratch_shapes=WIDE_SIDE,
+        out_specs=(VMEM,) * NX,
+        scratch_shapes=WIDE_SIDE + [pltpu.VMEM((NX, NZ, 16 * XB, EMB), BF16)],
         compiler_params=params(),
         cost_estimate=cost(0),
         name="dense_both",
     )(first, sib, *lows)
 
 
-def merge_kernel(owner, got, out, total):
+def across_kernel(part0, part1, part2, part3, out):
+    total = part0[...].astype(F32) + part1[...].astype(F32)
+    out[...] = total + (part2[...].astype(F32) + part3[...].astype(F32))
+
+
+def across(parts):
+    return pl.pallas_call(
+        across_kernel,
+        out_shape=jax.ShapeDtypeStruct((NZ, 16 * XB, EMB), F32),
+        in_specs=[VMEM] * NX,
+        out_specs=VMEM,
+        compiler_params=params(),
+        cost_estimate=cost(10),
+        name="across",
+    )(*parts)
+
+
+def merge_kernel(owner, got, dense, *refs):
+    out, total = refs
     total[...] = jnp.zeros_like(total)
+
     for t in range(TABLES):
         x, i = t // TX, t % TX
-        one = got[x, i * PIECE : (i + 1) * PIECE].astype(F32)
+        one = got[x, i].astype(F32)
         for y in range(1, NY):
-            one = one + got[y * NX + x, i * PIECE : (i + 1) * PIECE].astype(F32)
+            one = one + got[y * NX + x, i].astype(F32)
         to = owner[t]
         total[to, :PIECE] = total[to, :PIECE] + one
+
     for y in range(NY):
         for j in range(XB):
-            at = TX * PIECE + j * NW
-            one = got[y * NX, at : at + NW].astype(F32)
-            for x in range(1, NX):
-                one = one + got[y * NX + x, at : at + NW].astype(F32)
-            total[:, PIECE + y * XB + j, :] = one
+            for g in range(2):
+                at, src = PIECE + j * 4 + g * 2, j * 16 + g * 8 + y * 2
+                total[y * NZ : (y + 1) * NZ, at : at + 2] = dense[:, src : src + 2]
     out[...] = total[...].astype(BF16)
 
 
-def merge(owner, got):
+def merge(owner, got, dense):
     return pl.pallas_call(
         merge_kernel,
         out_shape=jax.ShapeDtypeStruct((NW, MROWS, EMB), BF16),
-        in_specs=[SMEM, VMEM],
+        in_specs=[SMEM] + [VMEM] * 2,
         out_specs=VMEM,
-        scratch_shapes=[pltpu.VMEM((NW, MROWS, EMB), F32)],
+        scratch_shapes=[
+            pltpu.VMEM((NW, MROWS, EMB), F32),
+        ],
         compiler_params=params(),
         cost_estimate=cost(0),
         name="merge",
-    )(owner, got)
+    )(owner, got, dense)
 
 
 def split_kernel(got, rows, up, down, stage):
@@ -344,8 +362,7 @@
             at = (y * XB + j) * EMB
             if at < COLS * EMB:
                 for g, to in enumerate((up, down)):
-                    for p in range(2):
-                        to[p : p + 1, at : at + EMB] = stage[g * 2 + p, y * XB + j : y * XB + j + 1]
+                    to[:, at : at + EMB] = stage[y, j * 4 + g * 2 : j * 4 + g * 2 + 2]
 
 
 def split(got):
@@ -399,12 +416,13 @@
     blocks = [blocks[0]] + [send(blocks[k], "x", k) for k in range(1, NX)]
     keep, give = bag_sums(blocks)
     sib = send(own, "c", 1)
-    dense = dense_both(dense_own(own, lows), sib, lows)
+    parts = dense_both(dense_own(own, lows), sib, lows)
     got = send(give, "c", 1)
-    got, dense = lax.optimization_barrier((got, dense))
-    sums = bag_add(keep, got, dense)
+    got, parts = lax.optimization_barrier((got, parts))
+    parts = [parts[0]] + [send(parts[k], "x", k) for k in range(1, NX)]
+    sums = bag_add(keep, got)
     got = lax.all_to_all(sums, ("y", "x"), split_axis=0, concat_axis=0, tiled=True)
-    merged = merge(table_owner, got)
+    merged = merge(table_owner, got, across(parts))
     merged = lax.all_to_all(merged, WIDE, split_axis=0, concat_axis=0, tiled=True)
     rows, grad_up, grad_down = split(merged)
     rows = lax.all_to_all(rows, ("x", "c"), split_axis=0, concat_axis=0, tiled=True)

time: 109 us -> 105 us (0.963)
  blocking collectives: 59.5 us -> 35.3 us
  starting transfers between devices: 19.2 us -> 29 us
  waiting for transfers between devices: 2.38 us -> 11.8 us
    all_to_all x1 -> x0, blocking collectives: 26 us -> none  [local(): lax.all_to_all(sums, ('y', 'x'), split_axis=0, concat_axis=0, tiled=True)]
    all_to_all x0 -> x1, waiting for transfers between devices: none -> 7.05 us  [local(): lax.all_to_all(sums, ('y', 'x'), split_axis=0, concat_axis=0, tiled=True)]
    all_to_all x0 -> x1, starting transfers between devices: none -> 5.76 us  [local(): lax.all_to_all(sums, ('y', 'x'), split_axis=0, concat_axis=0, tiled=True)]
    ppermute x9 -> x12, starting transfers between devices: 14.2 us -> 18.2 us  [send(): return lax.ppermute(a, axis, [(i, (i + k) % size) for i in range(size)])]
    ppermute x9 -> x12, waiting for transfers between devices: 2.38 us -> 4.79 us  [send(): return lax.ppermute(a, axis, [(i, (i + k) % size) for i in range(size)])]
    all_to_all x1, blocking collectives: 14.2 us -> 15.8 us  [local(): lax.all_to_all(rows, ('x', 'c'), split_axis=0, concat_axis=0, tiled=True)]
  transfers between devices with their start and end apart: 10 -> 14, of which waited for: 3 -> 6; matrix products, arithmetic and copies ran while one was open for 1% -> 1% of each run, Pallas kernels for 16% -> 18%
where the time goes in v4:
time: 105 us
  blocking collectives  35.3 us (34%)
  starting transfers between devices  29 us (28%)
  Pallas kernels  24.3 us (23%)
  waiting for transfers between devices  11.8 us (11%)
  other arithmetic  2.5 us (2%)
  local copies, waits for them, and re-layouts  1.05 us (1%)
    all_to_all x1, blocking collectives, local(): lax.all_to_all(merged, WIDE, split_axis=0, concat_axis=0, tiled=True)  19.5 us
    ppermute x12, starting transfers between devices, send(): return lax.ppermute(a, axis, [(i, (i + k) % size) for i in range(size)])  18.2 us
    all_to_all x1, blocking collectives, local(): lax.all_to_all(rows, ('x', 'c'), split_axis=0, concat_axis=0, tiled=True)  15.8 us
    pallas_call x1, Pallas kernels, cross(): pl.pallas_call(cross_kernel, out_shape=(half, half) + (part,) * NX, in_sp...  9.08 us
    pallas_call x1, Pallas kernels, bag_sums(): pl.pallas_call(bag_kernel, out_shape=(jax.ShapeDtypeStruct(shape, F32), j...  7.06 us
    all_to_all x1, waiting for transfers between devices, local(): lax.all_to_all(sums, ('y', 'x'), split_axis=0, concat_axis=0, tiled=True)  7.05 us
    all_to_all x1, starting transfers between devices, local(): lax.all_to_all(sums, ('y', 'x'), split_axis=0, concat_axis=0, tiled=True)  5.76 us
    all_to_all x1, starting transfers between devices, local(): own = lax.all_to_all(pair, 'y', split_axis=0, concat_axis=0, tiled=True)  5.01 us
  transfers between devices with their start and end apart: 14, of which 6 were waited for; matrix products, arithmetic and copies ran while one was open for 1% of the time, Pallas kernels for 18%

profile of v4, /device:TPU:1, one launch (start us, length us, event | category | flops | bytes accessed | tf_op | source)
XLA Modules:
  0.0 104.8 jit_solution(11967234414502525304)
XLA Ops:
  0.6 4.0 %pack.1 = (bf16[4,2,128,896]{3,2,1,0:T(8,128)(2,1)}, bf16[26,16,128]{2,1,0:T(8,128)(2,1)}) custom-call(bf16[128,3456]{1,0:T(8,128)(2,1)} %x_in.1, bf16[128,3456]{1,0:T(8,128)(2,1)} %u_in.1, s32[26,16,128]{2,1,0:T(8,128)} %bitcast.10, s32[26,128]{1,0:T(8,128)} %bitcast.11), custom_call_target="tpu_custom_call" | custom-call | flops 1500000000 | bytes 150000 | tf_op jit(solution)/shard_map/pack/pallas_call | solution.py:72
  4.7 5.0 %all-to-all-start = ((bf16[4,2,128,896]{3,2,1,0:T(8,128)(2,1)}), bf16[4,2,128,896]{3,2,1,0:T(8,128)(2,1)S(1)}, u32[]{:S(2)}, u32[]{:S(2)}) async-start(bf16[4,2,128,896]{3,2,1,0:T(8,128)(2,1)} %get-tuple-element.33), calls=%async_computation | async-start | bytes 3670016 | tf_op jit(solution)/shard_map/all_to_all | solution.py:409
  9.7 9.1 %cross.1 = (bf16[2,256,128]{2,1,0:T(8,128)(2,1)}, bf16[2,256,128]{2,1,0:T(8,128)(2,1)}, bf16[7,144,128]{2,1,0:T(8,128)(2,1)}, bf16[7,144,128]{2,1,0:T(8,128)(2,1...) custom-call(bf16[128,3456]{1,0:T(8,128)(2,1)} %x_in.1, bf16[128,3456]{1,0:T(8,128)(2,1)} %u_in.1, ...), custom_call_target="tpu_custom_call" | custom-call | flops 5000000000 | bytes 500000 | tf_op jit(solution)/shard_map/cross/pallas_call | solution.py:159
  18.8 1.3 %collective-permute-start = (bf16[7,144,128]{2,1,0:T(8,128)(2,1)}, bf16[7,144,128]{2,1,0:T(8,128)(2,1)S(1)}, u32[]{:S(2)}, u32[]{:S(2)}) collective-permute-start(bf16[7,144,128]{2,1,0:T(8,128)(2,1)} %get-tuple-element.28), channel_id=1, source_target_pairs={{0,2},{2,4},{4,6},{6,0},{1,3},{3,5},{5,7},{7,1},{8,10},{10,12},{12... | collective-permute-start | bytes 774152 | tf_op jit(solution)/shard_map/ppermute | solution.py:404
  20.0 2.5 %collective-permute-start.1 = (bf16[7,144,128]{2,1,0:T(8,128)(2,1)}, bf16[7,144,128]{2,1,0:T(8,128)(2,1)S(1)}, u32[]{:S(2)}, u32[]{:S(2)}) collective-permute-start(bf16[7,144,128]{2,1,0:T(8,128)(2,1)} %get-tuple-element.29), channel_id=1, source_target_pairs={{0,4},{2,6},{4,0},{6,2},{1,5},{3,7},{5,1},{7,3},{8,12},{10,14},{12... | collective-permute-start | bytes 774152 | tf_op jit(solution)/shard_map/ppermute | solution.py:404
  22.5 1.1 %collective-permute-start.2 = (bf16[7,144,128]{2,1,0:T(8,128)(2,1)}, bf16[7,144,128]{2,1,0:T(8,128)(2,1)}, u32[]{:S(2)}, u32[]{:S(2)}) collective-permute-start(bf16[7,144,128]{2,1,0:T(8,128)(2,1)} %get-tuple-element.30), channel_id=1, source_target_pairs={{0,6},{2,0},{4,2},{6,4},{1,7},{3,1},{5,3},{7,5},{8,14},{10,8},{12,... | collective-permute-start | bytes 774152 | tf_op jit(solution)/shard_map/ppermute | solution.py:404
  23.6 1.8 %collective-permute-start.4 = (bf16[2,256,128]{2,1,0:T(8,128)(2,1)}, bf16[2,256,128]{2,1,0:T(8,128)(2,1)S(1)}, u32[]{:S(2)}, u32[]{:S(2)}) collective-permute-start(bf16[2,256,128]{2,1,0:T(8,128)(2,1)} %get-tuple-element.35), channel_id=1, source_target_pairs={{0,1},{1,0},{2,3},{3,2},{4,5},{5,4},{6,7},{7,6},{8,9},{9,8},{10,11... | collective-permute-start | bytes 393224 | tf_op jit(solution)/shard_map/ppermute | solution.py:404
  25.4 1.2 %collective-permute-done.4 = bf16[2,256,128]{2,1,0:T(8,128)(2,1)S(1)} collective-permute-done((bf16[2,256,128]{2,1,0:T(8,128)(2,1)}, bf16[2,256,128]{2,1,0:T(8,128)(2,1)S(1)}, u32[]{:S(2)}, u32[]{:S(2)}) %collective-permute-start.4) | collective-permute-done | bytes 131104 | tf_op jit(solution)/shard_map/ppermute | solution.py:404
  26.6 0.9 pad_maximum_fusion.low0
  27.6 1.8 %collective-permute-start.5 = (bf16[2,2,256,128]{3,2,1,0:T(8,128)(2,1)S(1)}, bf16[2,2,256,128]{3,2,1,0:T(8,128)(2,1)S(1)}, u32[]{:S(2)}, u32[]{:S(2)}) collective-permute-start(bf16[2,2,256,128]{3,2,1,0:T(8,128)(2,1)S(1)} %pad_maximum_fusion.low0), channel_id=1, source_target_pairs={{0,64},{64,128},{128,192},{192,0},{1,65},{65,129},{129,193},{193,1... | collective-permute-start | bytes 786440 | tf_op jit(solution)/shard_map/ppermute | solution.py:404
  29.4 2.4 %collective-permute-start.6 = (bf16[2,2,256,128]{3,2,1,0:T(8,128)(2,1)S(1)}, bf16[2,2,256,128]{3,2,1,0:T(8,128)(2,1)S(1)}, u32[]{:S(2)}, u32[]{:S(2)}) collective-permute-start(bf16[2,2,256,128]{3,2,1,0:T(8,128)(2,1)S(1)} %pad_maximum_fusion.low0), channel_id=1, source_target_pairs={{0,128},{64,192},{128,0},{192,64},{1,129},{65,193},{129,1},{193,65... | collective-permute-start | bytes 786440 | tf_op jit(solution)/shard_map/ppermute | solution.py:404
  31.8 0.0 collective-permute-done.block1
  31.8 1.2 %collective-permute-start.7 = (bf16[2,2,256,128]{3,2,1,0:T(8,128)(2,1)S(1)}, bf16[2,2,256,128]{3,2,1,0:T(8,128)(2,1)S(1)}, u32[]{:S(2)}, u32[]{:S(2)}) collective-permute-start(bf16[2,2,256,128]{3,2,1,0:T(8,128)(2,1)S(1)} %pad_maximum_fusion.low0), channel_id=1, source_target_pairs={{0,192},{64,0},{128,64},{192,128},{1,193},{65,1},{129,65},{193,129... | collective-permute-start | bytes 786440 | tf_op jit(solution)/shard_map/ppermute | solution.py:404
  33.0 0.6 collective-permute-done.1.block2
  33.5 0.0 all-to-all-done.own
  33.5 1.9 %collective-permute-start.8 = (bf16[4,2,128,896]{3,2,1,0:T(8,128)(2,1)S(1)}, bf16[4,2,128,896]{3,2,1,0:T(8,128)(2,1)S(1)}, u32[]{:S(2)}, u32[]{:S(2)}) collective-permute-start(bf16[4,2,128,896]{3,2,1,0:T(8,128)(2,1)S(1)} %all-to-all-done.own), channel_id=1, source_target_pairs={{0,1},{1,0},{2,3},{3,2},{4,5},{5,4},{6,7},{7,6},{8,9},{9,8},{10,11... | collective-permute-start | bytes 5505032 | tf_op jit(solution)/shard_map/ppermute | solution.py:404
  35.4 0.0 collective-permute-done.2.block3
  35.4 0.0 copy-start.1
  35.4 0.9 copy-done.1
  36.4 7.1 %bag_sums.1 = (f32[7,256,128]{2,1,0:T(8,128)S(1)}, bf16[7,256,128]{2,1,0:T(8,128)(2,1)S(1)}) custom-call(bf16[7,144,128]{2,1,0:T(8,128)(2,1)S(1)} %copy-done.1, bf16[7,144,128]{2,1,0:T(8,128)(2,1)S(1)} %collective-permute-done.block1, bf16[7,144,128]{2,1,0:T(8,128)(2,1)S(1)} %collective-permute-done.1.block2, bf16[7,144,128]{2,1,0:T(8,128)(2,1)} %collective-permute-done.2.block3), custom_call_target="tpu_custom_call" | custom-call | flops 10000000000 | bytes 1000000 | tf_op jit(solution)/shard_map/bag_sums/pallas_call | solution.py:209
  43.4 0.3 collective-permute-start.3
  43.7 0.0 collective-permute-done.5.low1
  43.7 0.6 collective-permute-done.6.low2
  44.3 0.0 collective-permute-done.7.low3
  44.3 0.7 dense_own.1.first
  45.1 0.0 collective-permute-done.8.sib
  45.1 0.8 dense_both.1
  45.9 0.0 collective-permute-done.3.got
  46.0 2.5 %collective-permute-start.10 = (bf16[8,112,128]{2,1,0:T(8,128)(2,1)S(1)}, bf16[8,112,128]{2,1,0:T(8,128)(2,1)S(1)}, u32[]{:S(2)}, u32[]{:S(2)}) collective-permute-start(bf16[8,112,128]{2,1,0:T(8,128)(2,1)S(1)} %get-tuple-element.43), channel_id=1, source_target_pairs={{0,4},{2,6},{4,0},{6,2},{1,5},{3,7},{5,1},{7,3},{8,12},{10,14},{12... | collective-permute-start | bytes 688136 | tf_op jit(solution)/shard_map/ppermute | solution.py:404
  48.5 0.8 collective-permute-start.11
  49.3 0.6 collective-permute-start.9
  50.0 0.9 bag_add.1
  50.8 5.8 %all-to-all-start.1 = ((bf16[16,7,16,128]{3,2,1,0:T(8,128)(2,1)}), bf16[16,7,16,128]{3,2,1,0:T(8,128)(2,1)S(1)}, u32[]{:S(2)}, u32[]{:S(2)}) async-start(bf16[16,7,16,128]{3,2,1,0:T(8,128)(2,1)} %bag_add.1), calls=%async_computation.1 | async-start | bytes 917504 | tf_op jit(solution)/shard_map/all_to_all | solution.py:424
  56.6 0.0 copy-start
  56.6 0.0 collective-permute-done.10.part2
  56.6 2.0 %collective-permute-done.11.part3 = bf16[8,112,128]{2,1,0:T(8,128)(2,1)S(1)} collective-permute-done((bf16[8,112,128]{2,1,0:T(8,128)(2,1)S(1)}, bf16[8,112,128]{2,1,0:T(8,128)(2,1)S(1)}, u32[]{:S(2)}, u32[]{:S(2)}) %collective-permute-start.11) | collective-permute-done | bytes 229408 | tf_op jit(solution)/shard_map/ppermute | solution.py:404
  58.7 0.3 collective-permute-done.9.part1
  59.0 0.1 across.1.dense
  59.1 0.0 copy-start.3
  59.1 0.0 copy-start.4
  59.1 0.0 copy-start.2
  59.2 7.1 %all-to-all-done.1.got = bf16[16,7,16,128]{3,2,1,0:T(8,128)(2,1)S(1)} async-done(((bf16[16,7,16,128]{3,2,1,0:T(8,128)(2,1)}), bf16[16,7,16,128]{3,2,1,0:T(8,128)(2,1)S(1)}, u32[]{:S(2)}, u32[]{:S(2)}) %all-to-all-start.1) | async-done | bytes 458784 | tf_op jit(solution)/shard_map/all_to_all | solution.py:424
  66.2 0.0 copy-done
  66.2 0.9 merge.1
  67.1 19.5 %all_to_all.20.got = bf16[32,48,128]{2,1,0:T(8,128)(2,1)S(1)} all-to-all(bf16[32,48,128]{2,1,0:T(8,128)(2,1)S(1)} %merge.1), channel_id=1, replica_groups=mesh['y'=4,'z'=8,'x'=4,'c'=2] {'y','z'}, dimensions={0} | all-to-all | bytes 786432 | tf_op jit(solution)/shard_map/all_to_all | solution.py:426
  86.6 0.7 split.1
  87.3 15.8 %all_to_all.21 = f32[8,64,128]{2,1,0:T(8,128)S(1)} all-to-all(f32[8,64,128]{2,1,0:T(8,128)S(1)} %get-tuple-element.45), channel_id=1, replica_groups=mesh['y'=4,'z'=8,'x'=4,'c'=2] {'x','c'}, dimensions={0} | all-to-all | bytes 524288 | tf_op jit(solution)/shard_map/all_to_all | solution.py:428
  103.1 0.1 multiply_reduce_fusion
  103.3 0.1 div.18
  103.4 0.0 copy-done.3
  103.4 0.0 copy-done.4
  103.4 0.6 sqrt_add_fusion
  104.0 0.0 copy-done.2
  104.0 0.8 fusion
  (1 shorter events, 0.0 us)
Async XLA Ops:
  4.7 28.9 %all-to-all-start = ((bf16[4,2,128,896]{3,2,1,0:T(8,128)(2,1)}), bf16[4,2,128,896]{3,2,1,0:T(8,128)(2,1)S(1)}, u32[]{:S(2)}, u32[]{:S(2)}) async-start(bf16[4,2,128,896]{3,2,1,0:T(8,128)(2,1)} %get-tuple-element.33), calls=%async_computation | async-start | bytes 3670016 | tf_op jit(solution)/shard_map/all_to_all | solution.py:409
  18.8 13.0 %collective-permute-start = (bf16[7,144,128]{2,1,0:T(8,128)(2,1)}, bf16[7,144,128]{2,1,0:T(8,128)(2,1)S(1)}, u32[]{:S(2)}, u32[]{:S(2)}) collective-permute-start(bf16[7,144,128]{2,1,0:T(8,128)(2,1)} %get-tuple-element.28), channel_id=1, source_target_pairs={{0,2},{2,4},{4,6},{6,0},{1,3},{3,5},{5,7},{7,1},{8,10},{10,12},{12... | collective-permute-start | bytes 774152 | tf_op jit(solution)/shard_map/ppermute | solution.py:404
  20.0 13.5 %collective-permute-start.1 = (bf16[7,144,128]{2,1,0:T(8,128)(2,1)}, bf16[7,144,128]{2,1,0:T(8,128)(2,1)S(1)}, u32[]{:S(2)}, u32[]{:S(2)}) collective-permute-start(bf16[7,144,128]{2,1,0:T(8,128)(2,1)} %get-tuple-element.29), channel_id=1, source_target_pairs={{0,4},{2,6},{4,0},{6,2},{1,5},{3,7},{5,1},{7,3},{8,12},{10,14},{12... | collective-permute-start | bytes 774152 | tf_op jit(solution)/shard_map/ppermute | solution.py:404
  22.5 12.9 %collective-permute-start.2 = (bf16[7,144,128]{2,1,0:T(8,128)(2,1)}, bf16[7,144,128]{2,1,0:T(8,128)(2,1)}, u32[]{:S(2)}, u32[]{:S(2)}) collective-permute-start(bf16[7,144,128]{2,1,0:T(8,128)(2,1)} %get-tuple-element.30), channel_id=1, source_target_pairs={{0,6},{2,0},{4,2},{6,4},{1,7},{3,1},{5,3},{7,5},{8,14},{10,8},{12,... | collective-permute-start | bytes 774152 | tf_op jit(solution)/shard_map/ppermute | solution.py:404
  23.6 3.0 %collective-permute-start.4 = (bf16[2,256,128]{2,1,0:T(8,128)(2,1)}, bf16[2,256,128]{2,1,0:T(8,128)(2,1)S(1)}, u32[]{:S(2)}, u32[]{:S(2)}) collective-permute-start(bf16[2,256,128]{2,1,0:T(8,128)(2,1)} %get-tuple-element.35), channel_id=1, source_target_pairs={{0,1},{1,0},{2,3},{3,2},{4,5},{5,4},{6,7},{7,6},{8,9},{9,8},{10,11... | collective-permute-start | bytes 393224 | tf_op jit(solution)/shard_map/ppermute | solution.py:404
  27.6 16.1 %collective-permute-start.5 = (bf16[2,2,256,128]{3,2,1,0:T(8,128)(2,1)S(1)}, bf16[2,2,256,128]{3,2,1,0:T(8,128)(2,1)S(1)}, u32[]{:S(2)}, u32[]{:S(2)}) collective-permute-start(bf16[2,2,256,128]{3,2,1,0:T(8,128)(2,1)S(1)} %pad_maximum_fusion.low0), channel_id=1, source_target_pairs={{0,64},{64,128},{128,192},{192,0},{1,65},{65,129},{129,193},{193,1... | collective-permute-start | bytes 786440 | tf_op jit(solution)/shard_map/ppermute | solution.py:404
  29.4 14.9 %collective-permute-start.6 = (bf16[2,2,256,128]{3,2,1,0:T(8,128)(2,1)S(1)}, bf16[2,2,256,128]{3,2,1,0:T(8,128)(2,1)S(1)}, u32[]{:S(2)}, u32[]{:S(2)}) collective-permute-start(bf16[2,2,256,128]{3,2,1,0:T(8,128)(2,1)S(1)} %pad_maximum_fusion.low0), channel_id=1, source_target_pairs={{0,128},{64,192},{128,0},{192,64},{1,129},{65,193},{129,1},{193,65... | collective-permute-start | bytes 786440 | tf_op jit(solution)/shard_map/ppermute | solution.py:404
  31.8 12.5 %collective-permute-start.7 = (bf16[2,2,256,128]{3,2,1,0:T(8,128)(2,1)S(1)}, bf16[2,2,256,128]{3,2,1,0:T(8,128)(2,1)S(1)}, u32[]{:S(2)}, u32[]{:S(2)}) collective-permute-start(bf16[2,2,256,128]{3,2,1,0:T(8,128)(2,1)S(1)} %pad_maximum_fusion.low0), channel_id=1, source_target_pairs={{0,192},{64,0},{128,64},{192,128},{1,193},{65,1},{129,65},{193,129... | collective-permute-start | bytes 786440 | tf_op jit(solution)/shard_map/ppermute | solution.py:404
  33.5 11.5 %collective-permute-start.8 = (bf16[4,2,128,896]{3,2,1,0:T(8,128)(2,1)S(1)}, bf16[4,2,128,896]{3,2,1,0:T(8,128)(2,1)S(1)}, u32[]{:S(2)}, u32[]{:S(2)}) collective-permute-start(bf16[4,2,128,896]{3,2,1,0:T(8,128)(2,1)S(1)} %all-to-all-done.own), channel_id=1, source_target_pairs={{0,1},{1,0},{2,3},{3,2},{4,5},{5,4},{6,7},{7,6},{8,9},{9,8},{10,11... | collective-permute-start | bytes 5505032 | tf_op jit(solution)/shard_map/ppermute | solution.py:404
  35.4 0.9 copy-start.1
  43.4 2.5 %collective-permute-start.3 = (bf16[7,256,128]{2,1,0:T(8,128)(2,1)S(1)}, bf16[7,256,128]{2,1,0:T(8,128)(2,1)S(1)}, u32[]{:S(2)}, u32[]{:S(2)}) collective-permute-start(bf16[7,256,128]{2,1,0:T(8,128)(2,1)S(1)} %get-tuple-element.32), channel_id=1, source_target_pairs={{0,1},{1,0},{2,3},{3,2},{4,5},{5,4},{6,7},{7,6},{8,9},{9,8},{10,11... | collective-permute-start | bytes 1376264 | tf_op jit(solution)/shard_map/ppermute | solution.py:404
  46.0 10.6 %collective-permute-start.10 = (bf16[8,112,128]{2,1,0:T(8,128)(2,1)S(1)}, bf16[8,112,128]{2,1,0:T(8,128)(2,1)S(1)}, u32[]{:S(2)}, u32[]{:S(2)}) collective-permute-start(bf16[8,112,128]{2,1,0:T(8,128)(2,1)S(1)} %get-tuple-element.43), channel_id=1, source_target_pairs={{0,4},{2,6},{4,0},{6,2},{1,5},{3,7},{5,1},{7,3},{8,12},{10,14},{12... | collective-permute-start | bytes 688136 | tf_op jit(solution)/shard_map/ppermute | solution.py:404
  48.5 10.2 %collective-permute-start.11 = (bf16[8,112,128]{2,1,0:T(8,128)(2,1)S(1)}, bf16[8,112,128]{2,1,0:T(8,128)(2,1)S(1)}, u32[]{:S(2)}, u32[]{:S(2)}) collective-permute-start(bf16[8,112,128]{2,1,0:T(8,128)(2,1)S(1)} %get-tuple-element.44), channel_id=1, source_target_pairs={{0,6},{2,0},{4,2},{6,4},{1,7},{3,1},{5,3},{7,5},{8,14},{10,8},{12,... | collective-permute-start | bytes 688136 | tf_op jit(solution)/shard_map/ppermute | solution.py:404
  49.3 9.7 %collective-permute-start.9 = (bf16[8,112,128]{2,1,0:T(8,128)(2,1)S(1)}, bf16[8,112,128]{2,1,0:T(8,128)(2,1)S(1)}, u32[]{:S(2)}, u32[]{:S(2)}) collective-permute-start(bf16[8,112,128]{2,1,0:T(8,128)(2,1)S(1)} %get-tuple-element.42), channel_id=1, source_target_pairs={{0,2},{2,4},{4,6},{6,0},{1,3},{3,5},{5,7},{7,1},{8,10},{10,12},{12... | collective-permute-start | bytes 688136 | tf_op jit(solution)/shard_map/ppermute | solution.py:404
  50.8 15.4 %all-to-all-start.1 = ((bf16[16,7,16,128]{3,2,1,0:T(8,128)(2,1)}), bf16[16,7,16,128]{3,2,1,0:T(8,128)(2,1)S(1)}, u32[]{:S(2)}, u32[]{:S(2)}) async-start(bf16[16,7,16,128]{3,2,1,0:T(8,128)(2,1)} %bag_add.1), calls=%async_computation.1 | async-start | bytes 917504 | tf_op jit(solution)/shard_map/all_to_all | solution.py:424
  56.6 9.6 %copy-start = (s32[26]{0:T(128)S(1)}, s32[26]{0:T(128)}, u32[]{:S(2)}) copy-start(s32[26]{0:T(128)} %owner.1) | copy-start | bytes 316
  59.1 44.3 %copy-start.3 = (f32[512]{0:T(512)S(1)}, f32[512]{0:T(512)}, u32[]{:S(2)}) copy-start(f32[512]{0:T(512)} %param.21) | copy-start | bytes 6148
  59.1 44.3 %copy-start.4 = (s32[512]{0:T(512)S(1)}, s32[512]{0:T(512)}, u32[]{:S(2)}) copy-start(s32[512]{0:T(512)} %param.22) | copy-start | bytes 6148
  59.1 44.8 %copy-start.2 = (f32[512,128]{1,0:T(8,128)S(1)}, f32[512,128]{1,0:T(8,128)}, u32[]{:S(2)}) copy-start(f32[512,128]{1,0:T(8,128)} %param.20) | copy-start | bytes 786436

commit v5 on v4

--- a/solution.py
+++ b/solution.py
@@ -46,41 +46,77 @@
     return lax.axis_index(name).astype(jnp.int32)
 
 
-def pack_kernel(x, u, ids, lengths, pair, coded):
-    ds = (u[...].astype(F32) * x[...].astype(F32)).astype(BF16)
-    for b in range(NY):
-        size = min(XB, COLS - b * XB) * EMB
-        cols = slice(b * XB * EMB, b * XB * EMB + size)
-        pair[b, 0, :, :size] = ds[:, cols]
-        pair[b, 1, :, :size] = x[:, cols]
-        if size < XB * EMB:
-            pair[b, :, :, size:] = jnp.zeros((2, ds.shape[0], XB * EMB - size), BF16)
-
-    @pl.when(pl.program_id(0) == 0)
-    def _():
-        position = lax.broadcasted_iota(jnp.int32, (BAG, S), 0)
-        for t in range(TABLES):
-            code = jnp.where(position < lengths[t : t + 1], (ids[t] - 256).astype(F32), NONE)
-            coded[t] = code.astype(BF16)
+PACKS = 4
+
+
+def pack_kernel(x_in, u_in, ids_in, lengths_in, pair, coded, x, u, ids, lengths, stage, in_sems, out_sems):
+    rows = S // PACKS
+    loads, stores = [], []
+    for i in range(PACKS):
+        at = pl.ds(i * rows, rows)
+        loads.append(
+            [
+                pltpu.make_async_copy(x_in.at[at], x.at[at], in_sems.at[2 * i]),
+                pltpu.make_async_copy(u_in.at[at], u.at[at], in_sems.at[2 * i + 1]),
+            ]
+        )
+        stores.append(
+            [
+                pltpu.make_async_copy(
+                    stage.at[b, :, at], pair.at[b, :, at], out_sems.at[i * NY + b]
+                )
+                for b in range(NY)
+            ]
+        )
+    small = [
+        pltpu.make_async_copy(ids_in, ids, in_sems.at[2 * PACKS]),
+        pltpu.make_async_copy(lengths_in, lengths, in_sems.at[2 * PACKS + 1]),
+    ]
+    for copy in sum(loads, []) + small:
+        copy.start()
+    for i in range(PACKS):
+        at = slice(i * rows, (i + 1) * rows)
+        for copy in loads[i]:
+            copy.wait()
+        for b in range(NY):
+            size = min(XB, COLS - b * XB) * EMB
+            cols = slice(b * XB * EMB, b * XB * EMB + size)
+            one = x[at, cols]
+            stage[b, 0, at, :size] = (u[at, cols].astype(F32) * one.astype(F32)).astype(BF16)
+            stage[b, 1, at, :size] = one
+            if size < XB * EMB:
+                stage[b, :, at, size:] = jnp.zeros((2, rows, XB * EMB - size), BF16)
+            stores[i][b].start()
+    for copy in small:
+        copy.wait()
+    position = lax.broadcasted_iota(jnp.int32, (BAG, S), 0)
+    for t in range(TABLES):
+        code = jnp.where(position < lengths[t : t + 1], (ids[t] - 256).astype(F32), NONE)
+        coded[t] = code.astype(BF16)
+    for copy in sum(stores, []):
+        copy.wait()
 
 
 def pack(x, u, ids, lengths):
-    steps = 4
-    rows = S // steps
-    wide = pl.BlockSpec((rows, x.shape[1]), lambda i: (i, 0))
-    every = pl.BlockSpec((TABLES, BAG, S), lambda i: (0, 0, 0))
+    anywhere = pl.BlockSpec(memory_space=pl.ANY)
+    shape = (NY, 2, S, XB * EMB)
     return pl.pallas_call(
         pack_kernel,
-        grid=(steps,),
         out_shape=(
-            jax.ShapeDtypeStruct((NY, 2, S, XB * EMB), BF16),
+            jax.ShapeDtypeStruct(shape, BF16),
             jax.ShapeDtypeStruct((TABLES, BAG, S), BF16),
         ),
-        in_specs=[wide, wide, every, pl.BlockSpec((TABLES, S), lambda i: (0, 0))],
-        out_specs=(
-            pl.BlockSpec((NY, 2, rows, XB * EMB), lambda i: (0, 0, i, 0)),
-            every,
-        ),
+        in_specs=[anywhere] * 4,
+        out_specs=(anywhere, VMEM),
+        scratch_shapes=[
+            pltpu.VMEM(x.shape, BF16),
+            pltpu.VMEM(x.shape, BF16),
+            pltpu.VMEM((TABLES, BAG, S), jnp.int32),
+            pltpu.VMEM((TABLES, S), jnp.int32),
+            pltpu.VMEM(shape, BF16),
+            pltpu.SemaphoreType.DMA((2 * PACKS + 2,)),
+            pltpu.SemaphoreType.DMA((PACKS * NY,)),
+        ],
         compiler_params=params(60),
         cost_estimate=cost(1.5),
         name="pack",

time: 105 us -> 105 us (level)
  no operation moved by 1% of the time
where the time goes in v5:
time: 105 us; the launch traced here: 104 us
  blocking collectives  35.3 us (34%)
  starting transfers between devices  29 us (28%)
  Pallas kernels  23.6 us (22%)
  waiting for transfers between devices  11.8 us (11%)
  other arithmetic  2.5 us (2%)
  local copies, waits for them, and re-layouts  1.05 us (1%)
    all_to_all x1, blocking collectives, local(): lax.all_to_all(merged, WIDE, split_axis=0, concat_axis=0, tiled=True)  19.5 us
    ppermute x12, starting transfers between devices, send(): return lax.ppermute(a, axis, [(i, (i + k) % size) for i in range(size)])  18.2 us
    all_to_all x1, blocking collectives, local(): lax.all_to_all(rows, ('x', 'c'), split_axis=0, concat_axis=0, tiled=True)  15.8 us
    pallas_call x1, Pallas kernels, cross(): pl.pallas_call(cross_kernel, out_shape=(half, half) + (part,) * NX, in_sp...  9.09 us
    pallas_call x1, Pallas kernels, bag_sums(): pl.pallas_call(bag_kernel, out_shape=(jax.ShapeDtypeStruct(shape, F32), j...  7.06 us
    all_to_all x1, waiting for transfers between devices, local(): lax.all_to_all(sums, ('y', 'x'), split_axis=0, concat_axis=0, tiled=True)  7.06 us
    all_to_all x1, starting transfers between devices, local(): lax.all_to_all(sums, ('y', 'x'), split_axis=0, concat_axis=0, tiled=True)  5.76 us
    all_to_all x1, starting transfers between devices, local(): own = lax.all_to_all(pair, 'y', split_axis=0, concat_axis=0, tiled=True)  5.02 us
  transfers between devices with their start and end apart: 14, of which 6 were waited for; matrix products, arithmetic and copies ran while one was open for 1% of the time, Pallas kernels for 18%

profile of v5, /device:TPU:1, one launch (start us, length us, event | category | flops | bytes accessed | tf_op | source)
XLA Modules:
  0.0 104.1 jit_solution(5252591771040745763)
XLA Ops:
  0.6 3.3 %pack.1 = (bf16[4,2,128,896]{3,2,1,0:T(8,128)(2,1)}, bf16[26,16,128]{2,1,0:T(8,128)(2,1)}) custom-call(bf16[128,3456]{1,0:T(8,128)(2,1)} %x_in.3, bf16[128,3456]{1,0:T(8,128)(2,1)} %u_in.3, s32[26,16,128]{2,1,0:T(8,128)} %bitcast.10, s32[26,128]{1,0:T(8,128)} %bitcast.11), custom_call_target="tpu_custom_call" | custom-call | flops 1500000000 | bytes 150000 | tf_op jit(solution)/shard_map/pack/pallas_call | solution.py:103
  3.9 5.0 %all-to-all-start = ((bf16[4,2,128,896]{3,2,1,0:T(8,128)(2,1)}), bf16[4,2,128,896]{3,2,1,0:T(8,128)(2,1)S(1)}, u32[]{:S(2)}, u32[]{:S(2)}) async-start(bf16[4,2,128,896]{3,2,1,0:T(8,128)(2,1)} %get-tuple-element.33), calls=%async_computation | async-start | bytes 3670016 | tf_op jit(solution)/shard_map/all_to_all | solution.py:445
  8.9 9.1 %cross.1 = (bf16[2,256,128]{2,1,0:T(8,128)(2,1)}, bf16[2,256,128]{2,1,0:T(8,128)(2,1)}, bf16[7,144,128]{2,1,0:T(8,128)(2,1)}, bf16[7,144,128]{2,1,0:T(8,128)(2,1...) custom-call(bf16[128,3456]{1,0:T(8,128)(2,1)} %x_in.3, bf16[128,3456]{1,0:T(8,128)(2,1)} %u_in.3, ...), custom_call_target="tpu_custom_call" | custom-call | flops 5000000000 | bytes 500000 | tf_op jit(solution)/shard_map/cross/pallas_call | solution.py:195
  18.0 1.3 %collective-permute-start = (bf16[7,144,128]{2,1,0:T(8,128)(2,1)}, bf16[7,144,128]{2,1,0:T(8,128)(2,1)S(1)}, u32[]{:S(2)}, u32[]{:S(2)}) collective-permute-start(bf16[7,144,128]{2,1,0:T(8,128)(2,1)} %get-tuple-element.28), channel_id=1, source_target_pairs={{0,2},{2,4},{4,6},{6,0},{1,3},{3,5},{5,7},{7,1},{8,10},{10,12},{12... | collective-permute-start | bytes 774152 | tf_op jit(solution)/shard_map/ppermute | solution.py:440
  19.3 2.5 %collective-permute-start.1 = (bf16[7,144,128]{2,1,0:T(8,128)(2,1)}, bf16[7,144,128]{2,1,0:T(8,128)(2,1)S(1)}, u32[]{:S(2)}, u32[]{:S(2)}) collective-permute-start(bf16[7,144,128]{2,1,0:T(8,128)(2,1)} %get-tuple-element.29), channel_id=1, source_target_pairs={{0,4},{2,6},{4,0},{6,2},{1,5},{3,7},{5,1},{7,3},{8,12},{10,14},{12... | collective-permute-start | bytes 774152 | tf_op jit(solution)/shard_map/ppermute | solution.py:440
  21.8 1.1 %collective-permute-start.2 = (bf16[7,144,128]{2,1,0:T(8,128)(2,1)}, bf16[7,144,128]{2,1,0:T(8,128)(2,1)}, u32[]{:S(2)}, u32[]{:S(2)}) collective-permute-start(bf16[7,144,128]{2,1,0:T(8,128)(2,1)} %get-tuple-element.30), channel_id=1, source_target_pairs={{0,6},{2,0},{4,2},{6,4},{1,7},{3,1},{5,3},{7,5},{8,14},{10,8},{12,... | collective-permute-start | bytes 774152 | tf_op jit(solution)/shard_map/ppermute | solution.py:440
  22.9 1.8 %collective-permute-start.4 = (bf16[2,256,128]{2,1,0:T(8,128)(2,1)}, bf16[2,256,128]{2,1,0:T(8,128)(2,1)S(1)}, u32[]{:S(2)}, u32[]{:S(2)}) collective-permute-start(bf16[2,256,128]{2,1,0:T(8,128)(2,1)} %get-tuple-element.35), channel_id=1, source_target_pairs={{0,1},{1,0},{2,3},{3,2},{4,5},{5,4},{6,7},{7,6},{8,9},{9,8},{10,11... | collective-permute-start | bytes 393224 | tf_op jit(solution)/shard_map/ppermute | solution.py:440
  24.7 1.2 %collective-permute-done.4 = bf16[2,256,128]{2,1,0:T(8,128)(2,1)S(1)} collective-permute-done((bf16[2,256,128]{2,1,0:T(8,128)(2,1)}, bf16[2,256,128]{2,1,0:T(8,128)(2,1)S(1)}, u32[]{:S(2)}, u32[]{:S(2)}) %collective-permute-start.4) | collective-permute-done | bytes 131104 | tf_op jit(solution)/shard_map/ppermute | solution.py:440
  25.9 0.9 pad_maximum_fusion.low0
  26.8 1.8 %collective-permute-start.5 = (bf16[2,2,256,128]{3,2,1,0:T(8,128)(2,1)S(1)}, bf16[2,2,256,128]{3,2,1,0:T(8,128)(2,1)S(1)}, u32[]{:S(2)}, u32[]{:S(2)}) collective-permute-start(bf16[2,2,256,128]{3,2,1,0:T(8,128)(2,1)S(1)} %pad_maximum_fusion.low0), channel_id=1, source_target_pairs={{0,64},{64,128},{128,192},{192,0},{1,65},{65,129},{129,193},{193,1... | collective-permute-start | bytes 786440 | tf_op jit(solution)/shard_map/ppermute | solution.py:440
  28.6 2.4 %collective-permute-start.6 = (bf16[2,2,256,128]{3,2,1,0:T(8,128)(2,1)S(1)}, bf16[2,2,256,128]{3,2,1,0:T(8,128)(2,1)S(1)}, u32[]{:S(2)}, u32[]{:S(2)}) collective-permute-start(bf16[2,2,256,128]{3,2,1,0:T(8,128)(2,1)S(1)} %pad_maximum_fusion.low0), channel_id=1, source_target_pairs={{0,128},{64,192},{128,0},{192,64},{1,129},{65,193},{129,1},{193,65... | collective-permute-start | bytes 786440 | tf_op jit(solution)/shard_map/ppermute | solution.py:440
  31.0 0.0 collective-permute-done.block1
  31.0 1.2 %collective-permute-start.7 = (bf16[2,2,256,128]{3,2,1,0:T(8,128)(2,1)S(1)}, bf16[2,2,256,128]{3,2,1,0:T(8,128)(2,1)S(1)}, u32[]{:S(2)}, u32[]{:S(2)}) collective-permute-start(bf16[2,2,256,128]{3,2,1,0:T(8,128)(2,1)S(1)} %pad_maximum_fusion.low0), channel_id=1, source_target_pairs={{0,192},{64,0},{128,64},{192,128},{1,193},{65,1},{129,65},{193,129... | collective-permute-start | bytes 786440 | tf_op jit(solution)/shard_map/ppermute | solution.py:440
  32.2 0.6 collective-permute-done.1.block2
  32.8 0.0 all-to-all-done.own
  32.8 1.9 %collective-permute-start.8 = (bf16[4,2,128,896]{3,2,1,0:T(8,128)(2,1)S(1)}, bf16[4,2,128,896]{3,2,1,0:T(8,128)(2,1)S(1)}, u32[]{:S(2)}, u32[]{:S(2)}) collective-permute-start(bf16[4,2,128,896]{3,2,1,0:T(8,128)(2,1)S(1)} %all-to-all-done.own), channel_id=1, source_target_pairs={{0,1},{1,0},{2,3},{3,2},{4,5},{5,4},{6,7},{7,6},{8,9},{9,8},{10,11... | collective-permute-start | bytes 5505032 | tf_op jit(solution)/shard_map/ppermute | solution.py:440
  34.7 0.0 collective-permute-done.2.block3
  34.7 0.0 copy-start.1
  34.7 0.9 copy-done.1
  35.6 7.1 %bag_sums.1 = (f32[7,256,128]{2,1,0:T(8,128)S(1)}, bf16[7,256,128]{2,1,0:T(8,128)(2,1)S(1)}) custom-call(bf16[7,144,128]{2,1,0:T(8,128)(2,1)S(1)} %copy-done.1, bf16[7,144,128]{2,1,0:T(8,128)(2,1)S(1)} %collective-permute-done.block1, bf16[7,144,128]{2,1,0:T(8,128)(2,1)S(1)} %collective-permute-done.1.block2, bf16[7,144,128]{2,1,0:T(8,128)(2,1)} %collective-permute-done.2.block3), custom_call_target="tpu_custom_call" | custom-call | flops 10000000000 | bytes 1000000 | tf_op jit(solution)/shard_map/bag_sums/pallas_call | solution.py:245
  42.7 0.3 collective-permute-start.3
  43.0 0.0 collective-permute-done.5.low1
  43.0 0.6 collective-permute-done.6.low2
  43.6 0.0 collective-permute-done.7.low3
  43.6 0.7 dense_own.1.first
  44.3 0.0 collective-permute-done.8.sib
  44.3 0.8 dense_both.1
  45.2 0.0 collective-permute-done.3.got
  45.2 2.5 %collective-permute-start.10 = (bf16[8,112,128]{2,1,0:T(8,128)(2,1)S(1)}, bf16[8,112,128]{2,1,0:T(8,128)(2,1)S(1)}, u32[]{:S(2)}, u32[]{:S(2)}) collective-permute-start(bf16[8,112,128]{2,1,0:T(8,128)(2,1)S(1)} %get-tuple-element.43), channel_id=1, source_target_pairs={{0,4},{2,6},{4,0},{6,2},{1,5},{3,7},{5,1},{7,3},{8,12},{10,14},{12... | collective-permute-start | bytes 688136 | tf_op jit(solution)/shard_map/ppermute | solution.py:440
  47.7 0.8 collective-permute-start.11
  48.6 0.6 collective-permute-start.9
  49.2 0.9 bag_add.1
  50.1 5.8 %all-to-all-start.1 = ((bf16[16,7,16,128]{3,2,1,0:T(8,128)(2,1)}), bf16[16,7,16,128]{3,2,1,0:T(8,128)(2,1)S(1)}, u32[]{:S(2)}, u32[]{:S(2)}) async-start(bf16[16,7,16,128]{3,2,1,0:T(8,128)(2,1)} %bag_add.1), calls=%async_computation.1 | async-start | bytes 917504 | tf_op jit(solution)/shard_map/all_to_all | solution.py:460
  55.8 0.0 copy-start
  55.8 0.0 collective-permute-done.10.part2
  55.9 2.0 %collective-permute-done.11.part3 = bf16[8,112,128]{2,1,0:T(8,128)(2,1)S(1)} collective-permute-done((bf16[8,112,128]{2,1,0:T(8,128)(2,1)S(1)}, bf16[8,112,128]{2,1,0:T(8,128)(2,1)S(1)}, u32[]{:S(2)}, u32[]{:S(2)}) %collective-permute-start.11) | collective-permute-done | bytes 229408 | tf_op jit(solution)/shard_map/ppermute | solution.py:440
  57.9 0.3 collective-permute-done.9.part1
  58.3 0.1 across.1.dense
  58.4 0.0 copy-start.3
  58.4 0.0 copy-start.4
  58.4 0.0 copy-start.2
  58.4 7.1 %all-to-all-done.1.got = bf16[16,7,16,128]{3,2,1,0:T(8,128)(2,1)S(1)} async-done(((bf16[16,7,16,128]{3,2,1,0:T(8,128)(2,1)}), bf16[16,7,16,128]{3,2,1,0:T(8,128)(2,1)S(1)}, u32[]{:S(2)}, u32[]{:S(2)}) %all-to-all-start.1) | async-done | bytes 458784 | tf_op jit(solution)/shard_map/all_to_all | solution.py:460
  65.5 0.0 copy-done
  65.5 0.9 merge.1
  66.4 19.5 %all_to_all.20.got = bf16[32,48,128]{2,1,0:T(8,128)(2,1)S(1)} all-to-all(bf16[32,48,128]{2,1,0:T(8,128)(2,1)S(1)} %merge.1), channel_id=1, replica_groups=mesh['y'=4,'z'=8,'x'=4,'c'=2] {'y','z'}, dimensions={0} | all-to-all | bytes 786432 | tf_op jit(solution)/shard_map/all_to_all | solution.py:462
  85.9 0.7 split.1
  86.6 15.8 %all_to_all.21 = f32[8,64,128]{2,1,0:T(8,128)S(1)} all-to-all(f32[8,64,128]{2,1,0:T(8,128)S(1)} %get-tuple-element.45), channel_id=1, replica_groups=mesh['y'=4,'z'=8,'x'=4,'c'=2] {'x','c'}, dimensions={0} | all-to-all | bytes 524288 | tf_op jit(solution)/shard_map/all_to_all | solution.py:464
  102.4 0.1 multiply_reduce_fusion
  102.6 0.1 div.18
  102.6 0.0 copy-done.3
  102.6 0.0 copy-done.4
  102.6 0.6 sqrt_add_fusion
  103.2 0.0 copy-done.2
  103.2 0.8 fusion
  (1 shorter events, 0.0 us)
Async XLA Ops:
  3.9 28.9 %all-to-all-start = ((bf16[4,2,128,896]{3,2,1,0:T(8,128)(2,1)}), bf16[4,2,128,896]{3,2,1,0:T(8,128)(2,1)S(1)}, u32[]{:S(2)}, u32[]{:S(2)}) async-start(bf16[4,2,128,896]{3,2,1,0:T(8,128)(2,1)} %get-tuple-element.33), calls=%async_computation | async-start | bytes 3670016 | tf_op jit(solution)/shard_map/all_to_all | solution.py:445
  18.0 13.0 %collective-permute-start = (bf16[7,144,128]{2,1,0:T(8,128)(2,1)}, bf16[7,144,128]{2,1,0:T(8,128)(2,1)S(1)}, u32[]{:S(2)}, u32[]{:S(2)}) collective-permute-start(bf16[7,144,128]{2,1,0:T(8,128)(2,1)} %get-tuple-element.28), channel_id=1, source_target_pairs={{0,2},{2,4},{4,6},{6,0},{1,3},{3,5},{5,7},{7,1},{8,10},{10,12},{12... | collective-permute-start | bytes 774152 | tf_op jit(solution)/shard_map/ppermute | solution.py:440
  19.3 13.5 %collective-permute-start.1 = (bf16[7,144,128]{2,1,0:T(8,128)(2,1)}, bf16[7,144,128]{2,1,0:T(8,128)(2,1)S(1)}, u32[]{:S(2)}, u32[]{:S(2)}) collective-permute-start(bf16[7,144,128]{2,1,0:T(8,128)(2,1)} %get-tuple-element.29), channel_id=1, source_target_pairs={{0,4},{2,6},{4,0},{6,2},{1,5},{3,7},{5,1},{7,3},{8,12},{10,14},{12... | collective-permute-start | bytes 774152 | tf_op jit(solution)/shard_map/ppermute | solution.py:440
  21.8 12.9 %collective-permute-start.2 = (bf16[7,144,128]{2,1,0:T(8,128)(2,1)}, bf16[7,144,128]{2,1,0:T(8,128)(2,1)}, u32[]{:S(2)}, u32[]{:S(2)}) collective-permute-start(bf16[7,144,128]{2,1,0:T(8,128)(2,1)} %get-tuple-element.30), channel_id=1, source_target_pairs={{0,6},{2,0},{4,2},{6,4},{1,7},{3,1},{5,3},{7,5},{8,14},{10,8},{12,... | collective-permute-start | bytes 774152 | tf_op jit(solution)/shard_map/ppermute | solution.py:440
  22.9 3.0 %collective-permute-start.4 = (bf16[2,256,128]{2,1,0:T(8,128)(2,1)}, bf16[2,256,128]{2,1,0:T(8,128)(2,1)S(1)}, u32[]{:S(2)}, u32[]{:S(2)}) collective-permute-start(bf16[2,256,128]{2,1,0:T(8,128)(2,1)} %get-tuple-element.35), channel_id=1, source_target_pairs={{0,1},{1,0},{2,3},{3,2},{4,5},{5,4},{6,7},{7,6},{8,9},{9,8},{10,11... | collective-permute-start | bytes 393224 | tf_op jit(solution)/shard_map/ppermute | solution.py:440
  26.8 16.1 %collective-permute-start.5 = (bf16[2,2,256,128]{3,2,1,0:T(8,128)(2,1)S(1)}, bf16[2,2,256,128]{3,2,1,0:T(8,128)(2,1)S(1)}, u32[]{:S(2)}, u32[]{:S(2)}) collective-permute-start(bf16[2,2,256,128]{3,2,1,0:T(8,128)(2,1)S(1)} %pad_maximum_fusion.low0), channel_id=1, source_target_pairs={{0,64},{64,128},{128,192},{192,0},{1,65},{65,129},{129,193},{193,1... | collective-permute-start | bytes 786440 | tf_op jit(solution)/shard_map/ppermute | solution.py:440
  28.6 14.9 %collective-permute-start.6 = (bf16[2,2,256,128]{3,2,1,0:T(8,128)(2,1)S(1)}, bf16[2,2,256,128]{3,2,1,0:T(8,128)(2,1)S(1)}, u32[]{:S(2)}, u32[]{:S(2)}) collective-permute-start(bf16[2,2,256,128]{3,2,1,0:T(8,128)(2,1)S(1)} %pad_maximum_fusion.low0), channel_id=1, source_target_pairs={{0,128},{64,192},{128,0},{192,64},{1,129},{65,193},{129,1},{193,65... | collective-permute-start | bytes 786440 | tf_op jit(solution)/shard_map/ppermute | solution.py:440
  31.0 12.5 %collective-permute-start.7 = (bf16[2,2,256,128]{3,2,1,0:T(8,128)(2,1)S(1)}, bf16[2,2,256,128]{3,2,1,0:T(8,128)(2,1)S(1)}, u32[]{:S(2)}, u32[]{:S(2)}) collective-permute-start(bf16[2,2,256,128]{3,2,1,0:T(8,128)(2,1)S(1)} %pad_maximum_fusion.low0), channel_id=1, source_target_pairs={{0,192},{64,0},{128,64},{192,128},{1,193},{65,1},{129,65},{193,129... | collective-permute-start | bytes 786440 | tf_op jit(solution)/shard_map/ppermute | solution.py:440
  32.8 11.5 %collective-permute-start.8 = (bf16[4,2,128,896]{3,2,1,0:T(8,128)(2,1)S(1)}, bf16[4,2,128,896]{3,2,1,0:T(8,128)(2,1)S(1)}, u32[]{:S(2)}, u32[]{:S(2)}) collective-permute-start(bf16[4,2,128,896]{3,2,1,0:T(8,128)(2,1)S(1)} %all-to-all-done.own), channel_id=1, source_target_pairs={{0,1},{1,0},{2,3},{3,2},{4,5},{5,4},{6,7},{7,6},{8,9},{9,8},{10,11... | collective-permute-start | bytes 5505032 | tf_op jit(solution)/shard_map/ppermute | solution.py:440
  34.7 0.9 copy-start.1
  42.7 2.5 %collective-permute-start.3 = (bf16[7,256,128]{2,1,0:T(8,128)(2,1)S(1)}, bf16[7,256,128]{2,1,0:T(8,128)(2,1)S(1)}, u32[]{:S(2)}, u32[]{:S(2)}) collective-permute-start(bf16[7,256,128]{2,1,0:T(8,128)(2,1)S(1)} %get-tuple-element.32), channel_id=1, source_target_pairs={{0,1},{1,0},{2,3},{3,2},{4,5},{5,4},{6,7},{7,6},{8,9},{9,8},{10,11... | collective-permute-start | bytes 1376264 | tf_op jit(solution)/shard_map/ppermute | solution.py:440
  45.2 10.6 %collective-permute-start.10 = (bf16[8,112,128]{2,1,0:T(8,128)(2,1)S(1)}, bf16[8,112,128]{2,1,0:T(8,128)(2,1)S(1)}, u32[]{:S(2)}, u32[]{:S(2)}) collective-permute-start(bf16[8,112,128]{2,1,0:T(8,128)(2,1)S(1)} %get-tuple-element.43), channel_id=1, source_target_pairs={{0,4},{2,6},{4,0},{6,2},{1,5},{3,7},{5,1},{7,3},{8,12},{10,14},{12... | collective-permute-start | bytes 688136 | tf_op jit(solution)/shard_map/ppermute | solution.py:440
  47.7 10.2 %collective-permute-start.11 = (bf16[8,112,128]{2,1,0:T(8,128)(2,1)S(1)}, bf16[8,112,128]{2,1,0:T(8,128)(2,1)S(1)}, u32[]{:S(2)}, u32[]{:S(2)}) collective-permute-start(bf16[8,112,128]{2,1,0:T(8,128)(2,1)S(1)} %get-tuple-element.44), channel_id=1, source_target_pairs={{0,6},{2,0},{4,2},{6,4},{1,7},{3,1},{5,3},{7,5},{8,14},{10,8},{12,... | collective-permute-start | bytes 688136 | tf_op jit(solution)/shard_map/ppermute | solution.py:440
  48.6 9.7 %collective-permute-start.9 = (bf16[8,112,128]{2,1,0:T(8,128)(2,1)S(1)}, bf16[8,112,128]{2,1,0:T(8,128)(2,1)S(1)}, u32[]{:S(2)}, u32[]{:S(2)}) collective-permute-start(bf16[8,112,128]{2,1,0:T(8,128)(2,1)S(1)} %get-tuple-element.42), channel_id=1, source_target_pairs={{0,2},{2,4},{4,6},{6,0},{1,3},{3,5},{5,7},{7,1},{8,10},{10,12},{12... | collective-permute-start | bytes 688136 | tf_op jit(solution)/shard_map/ppermute | solution.py:440
  50.1 15.4 %all-to-all-start.1 = ((bf16[16,7,16,128]{3,2,1,0:T(8,128)(2,1)}), bf16[16,7,16,128]{3,2,1,0:T(8,128)(2,1)S(1)}, u32[]{:S(2)}, u32[]{:S(2)}) async-start(bf16[16,7,16,128]{3,2,1,0:T(8,128)(2,1)} %bag_add.1), calls=%async_computation.1 | async-start | bytes 917504 | tf_op jit(solution)/shard_map/all_to_all | solution.py:460
  55.8 9.6 %copy-start = (s32[26]{0:T(128)S(1)}, s32[26]{0:T(128)}, u32[]{:S(2)}) copy-start(s32[26]{0:T(128)} %owner.1) | copy-start | bytes 316
  58.4 44.3 %copy-start.3 = (f32[512]{0:T(512)S(1)}, f32[512]{0:T(512)}, u32[]{:S(2)}) copy-start(f32[512]{0:T(512)} %param.21) | copy-start | bytes 6148
  58.4 44.3 %copy-start.4 = (s32[512]{0:T(512)S(1)}, s32[512]{0:T(512)}, u32[]{:S(2)}) copy-start(s32[512]{0:T(512)} %param.22) | copy-start | bytes 6148
  58.4 44.8 %copy-start.2 = (f32[512,128]{1,0:T(8,128)S(1)}, f32[512,128]{1,0:T(8,128)}, u32[]{:S(2)}) copy-start(f32[512,128]{1,0:T(8,128)} %param.20) | copy-start | bytes 786436
